TPU v7x, 32 devices: a whole 2x2x4 slice. The times are simulated.
32 devices in a mesh: ax: 16 (over z, y, x), rad: 2 (over core).
Axes of the slice: x: 2, y: 2, z: 4, core: 2. Of those that a mesh axis runs over, the one named last changes fastest.
Arguments:
- parcel_motion: float32 [6, 65536], P(None, ('ax', 'rad')), may hold values from -6 to 6
- parcel_size: float32 [65536], P(('ax', 'rad')), may hold values from 0.5 to 2
- parcel_block: int32 [1024], P(('ax', 'rad')), may hold values from 0 to 127, as said below
- parcel_offset: int32 [65536], P(('ax', 'rad')), may hold values from 0 to 127
- gas_velocity: float32 [3, 256, 1024], P(None, 'ax', 'rad'), may hold values from -6 to 6
- pressure: float32 [256, 1024], P('ax', 'rad'), may hold values from -6 to 6
- block_cols: int32 [16, 128, 4], P('ax', 'rad'), may hold values from 0 to 127
- block_kinds: int32 [16, 128, 4], P('ax', 'rad'), may hold values from 0 to 7
- block_table: float32 [8, 128, 128], replicated, may hold values from -0.5 to 0.5
- send_axial: int32 [16, 2, 2, 64], P('ax', 'rad'), may hold values from 0 to 2047, as said below
- send_radial: int32 [16, 2, 2, 32], P('ax', 'rad'), may hold values from 0 to 2047, as said below
- send_counts: int32 [16, 2, 4], P('ax', 'rad'), may hold values from 0 to 64, as said below
Outputs:
- motion_out: float32 [6, 65536], P(None, ('ax', 'rad'))
- arrivals_axial: float32 [16, 2, 2, 7, 64], P('ax', 'rad')
- arrivals_radial: float32 [16, 2, 2, 7, 32], P('ax', 'rad')
- gas_out: float32 [3, 256, 1024], P(None, 'ax', 'rad')
- liquid_load: float32 [256, 1024], P('ax', 'rad')
- pressure_image: float32 [256, 1024], P('ax', 'rad')
Inputs may be any that keep to these rules, and one draw needn't show every extreme that they name: `parcel_block`: most of a device's parcel blocks lie in cell blocks of its own radial group; the others lie in other radial groups of the slab. `send_axial`: each device's lists (both axial and both radial together) hold distinct indices of that device's parcels; entries past the counts are unused. `send_radial`: disjoint from the device's axial lists, see send_axial. `send_counts`: axial counts are at most 64, radial ones at most 32; devices of radial group 0 send full lists in all four directions.
All inputs are finite; a program needn't handle non-finite values.
Results may differ from a plain program's by a relative error of at most 0.000084.
Values sent between devices are 32-bit elements; how exact they have to be, the bound alone decides.
No kernel may reach another device: no remote copies, remote signals or barrier semaphores. Data moves between devices by JAX's collectives and lax.ppermute only.
A program may use at most 64 MiB of HBM per device.

v0:
```python
import jax
import jax.numpy as jnp
from jax import lax
from jax.sharding import PartitionSpec as P

BLOCK = 128
PARCEL_GROUP = 64
NT = 8


TOP_PRECISION = lax.Precision.HIGHEST
DRAG = 0.5
STEP = 0.5
DIAG = 6.0


def from_behind(value, axis, steps):
    count = lax.axis_size(axis)
    leading, last = (max(0, -steps), min(count, count - steps))
    return lax.ppermute(value, axis, [(source, source + steps) for source in range(leading, last)])


def with_halo(x, sides, width):
    for axis, dim in sides:
        count, length = (lax.axis_size(axis), x.shape[dim])
        up = [(i, (i + 1) % count) for i in range(count - 1)]
        down = [(j, i) for i, j in up]
        last = lax.slice_in_dim(x, length - width, length, axis=dim)
        leading = lax.slice_in_dim(x, 0, width, axis=dim)
        before = lax.ppermute(last, axis, up)
        after = lax.ppermute(leading, axis, down)
        x = jnp.concatenate([before, x, after], axis=dim)
    return x


def pass_axial(payload, offset):
    return from_behind(payload, "ax", offset)


def pass_radial(payload, offset):
    return from_behind(payload, "rad", offset)


def on_device(
    parcel_motion,
    parcel_size,
    parcel_block,
    parcel_offset,
    gas_velocity,
    pressure,
    block_cols,
    block_kinds,
    block_table,
    send_axial,
    send_radial,
    send_counts,
):
    blocks_here = pressure.shape[0] * pressure.shape[1] // BLOCK
    gas_local = gas_velocity.reshape(3, blocks_here, BLOCK)
    pres_local = pressure.reshape(blocks_here, BLOCK)
    parcel_groups = parcel_block.shape[0]
    gas_slab, pres_slab = (
        lax.all_gather(gas_local, "rad", axis=1, tiled=True),
        lax.all_gather(pres_local, "rad", axis=0, tiled=True),
    )
    gas_lookup = gas_slab[:, parcel_block, :]
    offsets = parcel_offset.reshape(parcel_groups, PARCEL_GROUP)
    block_selector = (offsets[:, :, None] == jnp.arange(BLOCK, dtype=jnp.int32)).astype(jnp.float32)
    visited_flags = jnp.einsum(
        "fpm,pkm->fpk", gas_lookup, block_selector, precision=TOP_PRECISION
    ).reshape(3, parcel_groups * PARCEL_GROUP)
    velocity = parcel_motion[3:6]
    factor = jnp.exp(-DRAG / (parcel_size * parcel_size))
    new_vel = visited_flags + (velocity - visited_flags) * factor
    new_pos = parcel_motion[0:3] + STEP * new_vel
    motion_out = jnp.concatenate([new_pos, new_vel], axis=0)
    mass = parcel_size * parcel_size * parcel_size
    deposit = jnp.concatenate([-mass * (new_vel - velocity), mass[None]], axis=0)
    deposit = deposit.reshape(4, parcel_groups, PARCEL_GROUP)
    dep_flat = jnp.einsum("cbj,bjn->bcn", deposit, block_selector, precision=TOP_PRECISION).reshape(
        parcel_groups, 4 * BLOCK
    )
    rows_here = jnp.arange(blocks_here * lax.axis_size("rad"), dtype=jnp.int32)
    hits = (parcel_block[None, :] == rows_here[:, None]).astype(jnp.float32)
    summed = lax.psum_scatter(
        jnp.dot(hits, dep_flat, precision=TOP_PRECISION), "rad", scatter_dimension=0, tiled=True
    )
    sources = summed.reshape(blocks_here, 4, BLOCK).transpose(1, 0, 2)
    gas_out = gas_velocity + sources[:3].reshape(gas_velocity.shape)
    liquid_load = sources[3].reshape(pressure.shape)
    state = jnp.concatenate([motion_out, parcel_size[None]], axis=0)
    counts = send_counts[0, 0]

    def pack(lists, live_counts):
        taken = jnp.moveaxis(jnp.take(state, lists, axis=1), 1, 0)
        live = jnp.arange(lists.shape[1], dtype=jnp.int32)[None, :] < live_counts[:, None]
        return jnp.where(live[:, None, :], taken, jnp.float32(0.0))

    out_ax = pack(send_axial[0, 0], counts[0:2])
    arrivals_axial = jnp.stack([pass_axial(out_ax[0], 1), pass_axial(out_ax[1], -1)], axis=0)[
        None, None
    ]
    out_rad = pack(send_radial[0, 0], counts[2:4])
    arrivals_radial = jnp.stack([pass_radial(out_rad[0], 1), pass_radial(out_rad[1], -1)], axis=0)[
        None, None
    ]
    padded = with_halo(pressure, (("ax", 0),), 1)
    image = DIAG * pressure - padded[2:] - padded[:-2]
    picked = pres_slab[block_cols[0]]
    kinds = (block_kinds[0][..., None] == jnp.arange(NT, dtype=jnp.int32)).astype(jnp.float32)
    grouped = jnp.einsum("bkt,bkn->btn", kinds, picked, precision=TOP_PRECISION)
    coupled = jnp.einsum("btn,tmn->bm", grouped, block_table, precision=TOP_PRECISION)
    pressure_image = image + coupled.reshape(pressure.shape)
    return (motion_out, arrivals_axial, arrivals_radial, gas_out, liquid_load, pressure_image)


def solution(mesh):
    return jax.shard_map(
        on_device,
        mesh=mesh,
        in_specs=(
            P(None, ("ax", "rad")),
            P(("ax", "rad")),
            P(("ax", "rad")),
            P(("ax", "rad")),
            P(None, "ax", "rad"),
            P("ax", "rad"),
            P("ax", "rad", None),
            P("ax", "rad", None),
            P(),
            P("ax", "rad", None, None),
            P("ax", "rad", None, None),
            P("ax", "rad", None),
        ),
        out_specs=(
            P(None, ("ax", "rad")),
            P("ax", "rad", None, None, None),
            P("ax", "rad", None, None, None),
            P(None, "ax", "rad"),
            P("ax", "rad"),
            P("ax", "rad"),
        ),
        check_vma=False,
    )
```

profile of v0, /device:TPU:0, one launch (start us, length us, event | category | flops | bytes accessed | tf_op | source)
XLA Modules:
  0.0 58.2 jit_solution(5946790278507918890)
XLA Ops:
  7.2 0.0 copy-start
  7.2 0.0 reduce-scatter.2.cloned.1.call-start
  7.2 0.8 %multiply_multiply_fusion = (f32[2048]{0:T(1024)S(1)}, f32[2048]{0:T(1024)S(1)}, f32[2048]{0:T(1024)S(1)}) fusion(f32[2048]{0:T(1024)} %param.13), kind=kLoop, calls=%fused_computation.34 | loop fusion | flops 8192 | bytes 32768 | tf_op jit(solution)/shard_map/mul | solution.py:77
  8.0 0.1 eq.43
  8.1 0.9 %reshape.182 = f32[3,64,128]{2,1,0:T(8,128)S(1)} reshape(f32[3,16,512]{2,1,0:T(8,128)} %param.16) | data formatting | bytes 196608 | tf_op jit(solution)/shard_map/reshape | solution.py:59
  9.0 2.0 %all_gather.6 = f32[3,128,128]{2,1,0:T(8,128)S(1)} all-gather(f32[3,64,128]{2,1,0:T(8,128)S(1)} %reshape.182), channel_id=1, replica_groups=mesh['ax'=16,'rad'=2] {'rad'}, dimensions={1}, use_global_device_ids=true | all-gather | bytes 294912 | tf_op jit(solution)/shard_map/all_gather | solution.py:63
  11.0 0.1 copy.64
  11.1 0.5 copy-done.11
  11.7 0.6 %gather_fusion = f32[32,3,128]{2,1,0:T(4,128)S(1)} fusion(f32[3,128,128]{2,0,1:T(4,128)S(1)} %copy.64, s32[1024]{0:T(1024)S(1)} %pad_clamp_fusion.3), kind=kCustom, calls=%fused_computation | custom fusion | bytes 98432 | tf_op jit(solution)/shard_map/gather | solution.py:66
  12.3 1.0 %convolution_bitcast_fusion = f32[3,32,64]{2,0,1:T(4,128)S(1)} fusion(s32[32,64]{1,0:T(8,128)S(1)} %eq.43, f32[32,3,128]{2,1,0:T(4,128)S(1)} %gather_fusion), kind=kOutput, calls=%fused_computation.4 | convolution fusion | flops 9699328 | bytes 81920 | tf_op jit(solution)/shard_map/fpm,pkm->fpk/dot_general | solution.py:69
  13.3 0.0 copy-start.3
  13.3 0.1 reshape.183
  13.4 0.7 %copy-done.3 = f32[6,2048]{1,0:T(8,128)S(1)} copy-done((f32[6,2048]{1,0:T(8,128)S(1)}, f32[6,2048]{1,0:T(8,128)}, u32[]{:S(2)}) %copy-start.3) | copy-done | bytes 49176
  14.2 0.0 copy-start.4
  14.2 0.7 %copy-done.4 = f32[2048]{0:T(1024)S(1)} copy-done((f32[2048]{0:T(1024)S(1)}, f32[2048]{0:T(1024)}, u32[]{:S(2)}) %copy-start.4) | copy-done | bytes 8216
  14.9 0.0 copy-start.6
  14.9 0.4 copy.66
  15.3 0.3 copy-done.6
  15.6 0.1 reshape.199
  15.7 0.6 %gather_fusion.1 = f32[128,7]{1,0:T(8,128)S(1)} fusion(f32[7,2048]{0,1:T(8,128)S(1)} %copy.66, s32[1024]{0:T(1024)S(1)} %pad_clamp_fusion.2), kind=kCustom, calls=%fused_computation.1 | custom fusion | bytes 7680 | tf_op jit(solution)/shard_map/jit(_take)/gather | solution.py:95
  16.3 0.1 copy.67
  16.4 0.6 copy-done.10
  17.0 0.1 slice_bitcast_fusion.4
  17.0 0.1 compare_and_fusion.1
  17.1 1.3 %collective-permute-start.1 = (f32[7,64]{1,0:T(8,128)S(1)}, f32[7,64]{1,0:T(8,128)S(1)}, u32[]{:S(2)}, u32[]{:S(2)}) collective-permute-start(f32[7,64]{1,0:T(8,128)S(1)} %get-tuple-element.34), channel_id=1, source_target_pairs={{2,0},{4,2},{6,4},{8,6},{10,8},{12,10},{14,12},{16,14},{18,16},{20... | collective-permute-start | bytes 5384 | tf_op jit(solution)/shard_map/ppermute | solution.py:20
  18.4 5.4 %collective-permute-start = (f32[7,64]{1,0:T(8,128)S(1)}, f32[7,64]{1,0:T(8,128)S(1)}, u32[]{:S(2)}, u32[]{:S(2)}) collective-permute-start(f32[7,64]{1,0:T(8,128)S(1)} %get-tuple-element.33), channel_id=1, source_target_pairs={{0,2},{2,4},{4,6},{6,8},{8,10},{10,12},{12,14},{14,16},{16,18},{18... | collective-permute-start | bytes 5384 | tf_op jit(solution)/shard_map/ppermute | solution.py:20
  23.8 0.1 reshape.207
  23.9 0.6 %gather_fusion.2 = f32[64,7]{1,0:T(8,128)S(1)} fusion(f32[7,2048]{0,1:T(8,128)S(1)} %copy.66, s32[1024]{0:T(1024)S(1)} %pad_clamp_fusion.1), kind=kCustom, calls=%fused_computation.2 | custom fusion | bytes 3840 | tf_op jit(solution)/shard_map/jit(_take)/gather | solution.py:95
  24.5 0.1 copy.70
  24.6 0.1 compare_and_fusion
  24.7 1.3 %collective-permute-start.3 = (f32[7,32]{1,0:T(8,128)S(1)}, f32[7,32]{1,0:T(8,128)S(1)}, u32[]{:S(2)}, u32[]{:S(2)}) collective-permute-start(f32[7,32]{1,0:T(8,128)S(1)} %get-tuple-element.32), channel_id=1, source_target_pairs={{1,0},{3,2},{5,4},{7,6},{9,8},{11,10},{13,12},{15,14},{17,16},{19,... | collective-permute-start | bytes 2696 | tf_op jit(solution)/shard_map/ppermute | solution.py:20
  26.0 3.0 %collective-permute-start.2 = (f32[7,32]{1,0:T(8,128)S(1)}, f32[7,32]{1,0:T(8,128)S(1)}, u32[]{:S(2)}, u32[]{:S(2)}) collective-permute-start(f32[7,32]{1,0:T(8,128)S(1)} %get-tuple-element.31), channel_id=1, source_target_pairs={{0,1},{2,3},{4,5},{6,7},{8,9},{10,11},{12,13},{14,15},{16,17},{18,... | collective-permute-start | bytes 2696 | tf_op jit(solution)/shard_map/ppermute | solution.py:20
  29.0 0.1 concatenate.25
  29.1 0.1 concatenate.24
  29.3 0.7 %fusion = f32[32,4,128]{2,1,0:T(4,128)S(1)} fusion(s32[32,64]{1,0:T(8,128)S(1)} %eq.43, f32[1,32,64]{2,0,1:T(1,128)S(1)} %concatenate.25, f32[3,32,64]{2,0,1:T(4,128)S(1)} %copy.72), kind=kOutput, calls=%fused_computation.7 | convolution fusion | flops 12853248 | bytes 106496 | tf_op jit(solution)/shard_map/cbj,bjn->bcn/dot_general | solution.py:80
  30.0 1.0 %fusion.5 = f32[128,512]{1,0:T(8,128)} fusion(f32[4,8,4,128]{3,2,1,0:T(4,128)S(1)} %bitcast.62, s32[32]{0:T(128)S(1)} %copy-done.11), kind=kOutput, calls=%fused_computation.13 | convolution fusion | flops 25169920 | bytes 327808 | tf_op jit(solution)/shard_map/dot_general | solution.py:86
  30.9 0.0 reduce-scatter.2.cloned.1.call-update
  31.0 0.7 %copy-done.2 = f32[16,512]{1,0:T(8,128)S(1)} copy-done((f32[16,512]{1,0:T(8,128)S(1)}, f32[16,512]{1,0:T(8,128)}, u32[]{:S(2)}) %copy-start.2) | copy-done | bytes 32792
  31.7 4.8 %collective-permute-start.5 = (f32[1,512]{1,0:T(1,128)S(1)}, f32[1,512]{1,0:T(1,128)S(1)}, u32[]{:S(2)}, u32[]{:S(2)}) collective-permute-start(f32[1,512]{1,0:T(1,128)S(1)} %get-tuple-element.27), channel_id=1, source_target_pairs={{0,2},{2,4},{4,6},{6,8},{8,10},{10,12},{12,14},{14,16},{16,18},{18... | collective-permute-start | bytes 6152 | tf_op jit(solution)/shard_map/ppermute | solution.py:30
  36.5 0.6 %pad_maximum_fusion = f32[6,2048]{1,0:T(8,128)} fusion(f32[3,2048]{1,0:T(4,128)S(1)} %get-tuple-element.25, f32[3,2048]{1,0:T(4,128)S(1)} %multiply_add_fusion), kind=kLoop, calls=%fused_computation.16 | loop fusion | flops 12288 | bytes 98304 | tf_op jit(solution)/shard_map/concatenate | solution.py:76
  37.2 2.0 %all_gather.7 = f32[128,128]{1,0:T(8,128)S(1)} all-gather(f32[64,128]{1,0:T(8,128)S(1)} %reshape.187), channel_id=1, replica_groups=mesh['ax'=16,'rad'=2] {'rad'}, dimensions={0}, use_global_device_ids=true | all-gather | bytes 98304 | tf_op jit(solution)/shard_map/all_gather | solution.py:64
  39.2 0.1 copy.75
  39.3 0.1 reshape.215
  39.4 0.5 copy-done.8
  39.8 0.1 copy.74
  39.9 0.7 %gather_fusion.3 = f32[256,128]{1,0:T(8,128)S(1)} fusion(f32[128,128]{1,0:T(8,128)S(1)} %all_gather.7, s32[1024]{0:T(1024)S(1)} %pad_clamp_fusion), kind=kCustom, calls=%fused_computation.3 | custom fusion | bytes 263168 | tf_op jit(solution)/shard_map/gather | solution.py:109
  40.7 0.6 %fusion.4 = f32[64,8,128]{2,1,0:T(8,128)S(1)} fusion(f32[64,4,128]{2,1,0:T(4,128)S(1)} %bitcast.60, s32[64,4]{1,0:T(8,128)S(1)} %copy.74), kind=kOutput, calls=%fused_computation.12 | convolution fusion | flops 3147776 | bytes 394240 | tf_op jit(solution)/shard_map/bkt,bkn->btn/dot_general | solution.py:111
  41.3 0.7 %convolution_bitcast_fusion.1 = f32[64,128]{1,0:T(8,128)S(1)} fusion(f32[8,128,128]{2,1,0:T(8,128)S(1)} %copy-done, f32[64,8,128]{2,1,0:T(8,128)S(1)} %fusion.4), kind=kOutput, calls=%fused_computation.5 | convolution fusion | flops 100663296 | bytes 819200 | tf_op jit(solution)/shard_map/btn,tmn->bm/dot_general | solution.py:112
  42.0 0.0 collective-permute-done.2
  42.0 1.3 %collective-permute-start.4 = (f32[1,512]{1,0:T(1,128)S(1)}, f32[1,512]{1,0:T(1,128)S(1)}, u32[]{:S(2)}, u32[]{:S(2)}) collective-permute-start(f32[1,512]{1,0:T(1,128)S(1)} %get-tuple-element.26), channel_id=1, source_target_pairs={{2,0},{4,2},{6,4},{8,6},{10,8},{12,10},{14,12},{16,14},{18,16},{20... | collective-permute-start | bytes 6152 | tf_op jit(solution)/shard_map/ppermute | solution.py:31
  43.3 0.0 collective-permute-done.3
  43.3 0.6 %maximum_bitcast_fusion.1 = f32[1,1,2,7,32]{4,2,3,1,0:T(2,128)} fusion(f32[1,7,32]{2,0,1:T(1,128)S(1)} %stack.22, f32[1,7,32]{2,0,1:T(1,128)S(1)} %copy.71), kind=kLoop, calls=%fused_computation.40 | loop fusion | flops 448 | bytes 3584 | tf_op jit(solution)/shard_map/broadcast_in_dim | solution.py:104
  43.9 0.0 collective-permute-done
  43.9 0.0 collective-permute-done.1
  44.0 0.6 %maximum_bitcast_fusion = f32[1,1,2,7,64]{4,2,3,1,0:T(2,128)} fusion(f32[1,7,64]{2,0,1:T(1,128)S(1)} %stack.19, f32[1,7,64]{2,0,1:T(1,128)S(1)} %copy.68), kind=kLoop, calls=%fused_computation.39 | loop fusion | flops 896 | bytes 7168 | tf_op jit(solution)/shard_map/broadcast_in_dim | solution.py:100
  44.6 0.0 collective-permute-done.5
  44.6 2.9 %collective-permute-done.4 = f32[1,512]{1,0:T(1,128)S(1)} collective-permute-done((f32[1,512]{1,0:T(1,128)S(1)}, f32[1,512]{1,0:T(1,128)S(1)}, u32[]{:S(2)}, u32[]{:S(2)}) %collective-permute-start.4) | collective-permute-done | bytes 2080 | tf_op jit(solution)/shard_map/ppermute | solution.py:31
  47.5 0.6 %fusion.14 = f32[16,512]{1,0:T(8,128)} fusion(f32[16,512]{1,0:T(8,128)S(1)} %reshape.188, f32[16,512]{1,0:T(8,128)S(1)} %copy-done.2, f32[1,512]{1,0:T(1,128)S(1)} %collective-permute-done.5, f32[1,512]{1,0:T(1,128)S(1)} %collective-permute-done.4), kind=kLoop, calls=%fused_computation.26 | loop fusion | flops 49152 | bytes 102400 | tf_op jit(solution)/shard_map/add | solution.py:113
  48.1 0.9 %reshape.185 = f32[64,4,128]{2,1,0:T(4,128)S(1)} reshape(f32[64,512]{1,0:T(8,128)} %reduce-scatter.2.cloned.1.call-done) | data formatting | bytes 262144 | tf_op jit(solution)/shard_map/reshape | solution.py:88
  49.1 0.1 slice_reduce_fusion
  49.2 0.0 copy-start.1
  49.2 0.9 %copy-done.1 = f32[3,16,512]{2,1,0:T(8,128)S(1)} copy-done((f32[3,16,512]{2,1,0:T(8,128)S(1)}, f32[3,16,512]{2,1,0:T(8,128)}, u32[]{:S(2)}) %copy-start.1) | copy-done | bytes 98328
  50.1 0.7 %add.87 = f32[3,16,512]{2,1,0:T(8,128)} add(f32[3,16,512]{2,1,0:T(8,128)S(1)} %copy-done.1, f32[3,16,512]{2,1,0:T(8,128)S(1)} %reshape.186) | non-fusion elementwise | flops 24576 | bytes 294912 | tf_op jit(solution)/shard_map/add | solution.py:89
  50.7 0.6 %reshape_squeeze.3 = f32[16,512]{1,0:T(8,128)} reshape(f32[64,128]{1,0:T(8,128)S(1)} %slice_reduce_fusion) | data formatting | bytes 65536 | tf_op jit(solution)/shard_map/reshape;squeeze | solution.py:90
  (38 shorter events, 0.3 us)
Async XLA Ops:
  7.2 34.1 %copy-start = (f32[8,128,128]{2,1,0:T(8,128)S(1)}, f32[8,128,128]{2,1,0:T(8,128)}, u32[]{:S(2)}) copy-start(f32[8,128,128]{2,1,0:T(8,128)} %param.20) | copy-start | bytes 1572868
  7.2 0.8 %copy-start.5 = (s32[2048]{0:T(1024)S(1)}, s32[2048]{0:T(1024)}, u32[]{:S(2)}) copy-start(s32[2048]{0:T(1024)} %param.15) | copy-start | bytes 24580
  7.2 40.9 %reduce-scatter.2.cloned.1.call-start = ((), (), s32[]{:S(2)}) async-start(), calls=%async_computation.1 | async-start | bytes 393216 | tf_op jit(solution)/shard_map/reduce_scatter | solution.py:85
  11.0 0.7 %copy-start.11 = (s32[32]{0:T(128)S(1)}, s32[32]{0:T(128)}, u32[]{:S(2)}) copy-start(s32[32]{0:T(128)} %param.14) | copy-start | bytes 388
  13.3 0.9 %copy-start.3 = (f32[6,2048]{1,0:T(8,128)S(1)}, f32[6,2048]{1,0:T(8,128)}, u32[]{:S(2)}) copy-start(f32[6,2048]{1,0:T(8,128)} %param.12) | copy-start | bytes 147460
  14.2 0.7 %copy-start.4 = (f32[2048]{0:T(1024)S(1)}, f32[2048]{0:T(1024)}, u32[]{:S(2)}) copy-start(f32[2048]{0:T(1024)} %param.13) | copy-start | bytes 24580
  14.9 0.7 %copy-start.6 = (s32[1,1,2,64]{3,2,1,0:T(2,128)S(1)}, s32[1,1,2,64]{3,2,1,0:T(2,128)}, u32[]{:S(2)}) copy-start(s32[1,1,2,64]{3,2,1,0:T(2,128)} %param.21) | copy-start | bytes 1540
  16.3 0.7 %copy-start.10 = (s32[1,1,4]{2,1,0:T(1,128)S(1)}, s32[1,1,4]{2,1,0:T(1,128)}, u32[]{:S(2)}) copy-start(s32[1,1,4]{2,1,0:T(1,128)} %param.23) | copy-start | bytes 52
  17.1 6.7 %copy-start.7 = (s32[1,1,2,32]{3,2,1,0:T(2,128)S(1)}, s32[1,1,2,32]{3,2,1,0:T(2,128)}, u32[]{:S(2)}) copy-start(s32[1,1,2,32]{3,2,1,0:T(2,128)} %param.22) | copy-start | bytes 772
  17.1 26.8 %collective-permute-start.1 = (f32[7,64]{1,0:T(8,128)S(1)}, f32[7,64]{1,0:T(8,128)S(1)}, u32[]{:S(2)}, u32[]{:S(2)}) collective-permute-start(f32[7,64]{1,0:T(8,128)S(1)} %get-tuple-element.34), channel_id=1, source_target_pairs={{2,0},{4,2},{6,4},{8,6},{10,8},{12,10},{14,12},{16,14},{18,16},{20... | collective-permute-start | bytes 5384 | tf_op jit(solution)/shard_map/ppermute | solution.py:20
  18.4 25.5 %collective-permute-start = (f32[7,64]{1,0:T(8,128)S(1)}, f32[7,64]{1,0:T(8,128)S(1)}, u32[]{:S(2)}, u32[]{:S(2)}) collective-permute-start(f32[7,64]{1,0:T(8,128)S(1)} %get-tuple-element.33), channel_id=1, source_target_pairs={{0,2},{2,4},{4,6},{6,8},{8,10},{10,12},{12,14},{14,16},{16,18},{18... | collective-permute-start | bytes 5384 | tf_op jit(solution)/shard_map/ppermute | solution.py:20
  24.7 18.6 %collective-permute-start.3 = (f32[7,32]{1,0:T(8,128)S(1)}, f32[7,32]{1,0:T(8,128)S(1)}, u32[]{:S(2)}, u32[]{:S(2)}) collective-permute-start(f32[7,32]{1,0:T(8,128)S(1)} %get-tuple-element.32), channel_id=1, source_target_pairs={{1,0},{3,2},{5,4},{7,6},{9,8},{11,10},{13,12},{15,14},{17,16},{19,... | collective-permute-start | bytes 2696 | tf_op jit(solution)/shard_map/ppermute | solution.py:20
  26.0 16.0 %collective-permute-start.2 = (f32[7,32]{1,0:T(8,128)S(1)}, f32[7,32]{1,0:T(8,128)S(1)}, u32[]{:S(2)}, u32[]{:S(2)}) collective-permute-start(f32[7,32]{1,0:T(8,128)S(1)} %get-tuple-element.31), channel_id=1, source_target_pairs={{0,1},{2,3},{4,5},{6,7},{8,9},{10,11},{12,13},{14,15},{16,17},{18,... | collective-permute-start | bytes 2696 | tf_op jit(solution)/shard_map/ppermute | solution.py:20
  30.9 0.8 %copy-start.2 = (f32[16,512]{1,0:T(8,128)S(1)}, f32[16,512]{1,0:T(8,128)}, u32[]{:S(2)}) copy-start(f32[16,512]{1,0:T(8,128)} %param.17) | copy-start | bytes 98308
  31.7 12.9 %collective-permute-start.5 = (f32[1,512]{1,0:T(1,128)S(1)}, f32[1,512]{1,0:T(1,128)S(1)}, u32[]{:S(2)}, u32[]{:S(2)}) collective-permute-start(f32[1,512]{1,0:T(1,128)S(1)} %get-tuple-element.27), channel_id=1, source_target_pairs={{0,2},{2,4},{4,6},{6,8},{8,10},{10,12},{12,14},{14,16},{16,18},{18... | collective-permute-start | bytes 6152 | tf_op jit(solution)/shard_map/ppermute | solution.py:30
  37.2 2.0 %copy-start.9 = (s32[1,64,4]{1,2,0:T(4,128)S(1)}, s32[1,64,4]{1,2,0:T(4,128)}, u32[]{:S(2)}) copy-start(s32[1,64,4]{1,2,0:T(4,128)} %param.18) | copy-start | bytes 3076
  39.2 0.7 %copy-start.8 = (s32[1,64,4]{1,2,0:T(4,128)S(1)}, s32[1,64,4]{1,2,0:T(4,128)}, u32[]{:S(2)}) copy-start(s32[1,64,4]{1,2,0:T(4,128)} %param.19) | copy-start | bytes 3076
  42.0 5.5 %collective-permute-start.4 = (f32[1,512]{1,0:T(1,128)S(1)}, f32[1,512]{1,0:T(1,128)S(1)}, u32[]{:S(2)}, u32[]{:S(2)}) collective-permute-start(f32[1,512]{1,0:T(1,128)S(1)} %get-tuple-element.26), channel_id=1, source_target_pairs={{2,0},{4,2},{6,4},{8,6},{10,8},{12,10},{14,12},{16,14},{18,16},{20... | collective-permute-start | bytes 6152 | tf_op jit(solution)/shard_map/ppermute | solution.py:31
  49.2 0.9 %copy-start.1 = (f32[3,16,512]{2,1,0:T(8,128)S(1)}, f32[3,16,512]{2,1,0:T(8,128)}, u32[]{:S(2)}) copy-start(f32[3,16,512]{2,1,0:T(8,128)} %param.16) | copy-start | bytes 294916
Sparse Core Ops, SparseCore 0:
  31.1 10.2 reduce-scatter.1
where the time goes:
time: 58.8 us; the launch traced here: 58.2 us
  starting transfers between devices  17.1 us (29%)
  between operations  14.3 us (24%)
  local copies, waits for them, and re-layouts  11.7 us (20%)
  other arithmetic  4.18 us (7%)
  blocking collectives  4 us (7%)
  matrix products  3.95 us (7%)
  waiting for transfers between devices  2.93 us (5%)
    ppermute x4, starting transfers between devices, from_behind(): lax.ppermute(value, axis, [(source, source + steps) for source in range(l...  11 us
    unnamed x24, local copies, waits for them, and re-layouts  4.89 us
    ppermute x1, starting transfers between devices, with_halo(): before = lax.ppermute(last, axis, up)  4.81 us
    ppermute x1, waiting for transfers between devices, with_halo(): after = lax.ppermute(leading, axis, down)  2.9 us
    all_gather x1, blocking collectives, on_device(): lax.all_gather(gas_local, 'rad', axis=1, tiled=True)  2.03 us
    all_gather x1, blocking collectives, on_device(): lax.all_gather(pres_local, 'rad', axis=0, tiled=True)  1.97 us
    gather x4, local copies, waits for them, and re-layouts, pack(): taken = jnp.moveaxis(jnp.take(state, lists, axis=1), 1, 0)  1.41 us
    ppermute x1, starting transfers between devices, with_halo(): after = lax.ppermute(leading, axis, down)  1.29 us
  transfers between devices with their start and end apart: 7, of which 1 were waited for; matrix products, arithmetic and copies ran while one was open for 13% of the time, Pallas kernels for 0%

commit v1 on v0

v1 whole, which is shorter than its diff:
```python
import functools

import jax
import jax.numpy as jnp
from jax import lax
from jax.experimental import pallas as pl
from jax.experimental.pallas import tpu as pltpu
from jax.sharding import PartitionSpec as P

BLOCK = 128
GROUP = 64
NT = 8
DRAG = 0.5
STEP = 0.5
DIAG = 6.0
VMEM_LIMIT = 24 * 1024 * 1024

F32 = jnp.float32
BF16 = jnp.bfloat16
I32 = jnp.int32

vmem = pl.BlockSpec(memory_space=pltpu.VMEM)
smem = pl.BlockSpec(memory_space=pltpu.SMEM)


class Sizes:
    def __init__(self, layers, radial, parcels):
        self.layers = layers
        self.quarters = radial // BLOCK
        self.blocks = layers * self.quarters
        self.tiles = parcels // BLOCK
        self.groups = parcels // GROUP
        self.gas = 0
        self.pres = 3 * self.blocks
        self.motion = self.pres + self.blocks
        self.size = self.motion + 6 * self.tiles
        self.offset = self.size + self.tiles
        self.meta = self.offset + self.tiles
        self.rows = self.meta + 8


def split2(x):
    high = x.astype(BF16)
    return high, (x - high.astype(F32)).astype(BF16)


def dot(a, b):
    return jnp.dot(a, b, preferred_element_type=F32)


def dot_nt(a, b):
    return lax.dot_general(a, b, (((1,), (1,)), ((), ())), preferred_element_type=F32)


def iota(shape, dim):
    return lax.broadcasted_iota(I32, shape, dim)


def block_row(sz, b):
    local = b % sz.blocks
    return b - local + (local % sz.quarters) * sz.layers + local // sz.quarters


def pack_kernel(sz, motion, size, block, offset, gas, pres, lists, counts, out):
    layers = sz.layers
    for c in range(3):
        for q in range(sz.quarters):
            out[pl.ds(sz.gas + c * sz.blocks + q * layers, layers), :] = gas[c, :, q * BLOCK : (q + 1) * BLOCK]
    for q in range(sz.quarters):
        out[pl.ds(sz.pres + q * layers, layers), :] = pres[:, q * BLOCK : (q + 1) * BLOCK]
    for i in range(sz.tiles):
        out[pl.ds(sz.motion + i, 6, stride=sz.tiles), :] = motion[:, i * BLOCK : (i + 1) * BLOCK]
    out[pl.ds(sz.size, sz.tiles), :] = size[...]
    out[pl.ds(sz.offset, sz.tiles), :] = offset[...].astype(F32)
    out[pl.ds(sz.meta, 8), :] = jnp.full((8, BLOCK), -1.0, F32)
    out[pl.ds(sz.meta, 1), pl.ds(0, sz.groups)] = block_row(sz, block[...]).astype(F32)
    width = lists.shape[1]
    lane = iota((1, width), 1)
    for slot in range(2):
        kept = jnp.where(lane < counts[0, 2 + slot], lists[slot : slot + 1, :], -1)
        out[pl.ds(sz.meta + 1 + slot, 1), pl.ds(0, width)] = kept.astype(F32)


def take_lanes(x, idx):
    return jnp.take_along_axis(x, idx, axis=1, mode="promise_in_bounds")


def pick(sz, state, idx):
    shape = (sz.tiles, BLOCK)
    idx = jnp.broadcast_to(idx, shape)
    lane = idx & (BLOCK - 1)
    here = (idx >> 7) == iota(shape, 0)
    return [jnp.sum(jnp.where(here, take_lanes(s, lane), 0.0), axis=0, keepdims=True) for s in state]


def main_kernel(
    sz, n_rad, G, cols, kinds, table, axial, counts, me,
    motion_out, arr_rad, gas_out, liquid, image, up, down,
    near, state, deps, spread, coup,
):
    r = me[0]
    layers, tiles, blocks, groups = sz.layers, sz.tiles, sz.blocks, sz.groups
    slab_blocks = n_rad * blocks
    T = n_rad * tiles
    lane_row = iota((1, BLOCK), 1)

    block_rows = [G[d, pl.ds(sz.meta, 1), :] for d in range(n_rad)]
    column = jnp.concatenate(
        [jnp.transpose(jnp.broadcast_to(b, (BLOCK, BLOCK)))[:groups] for b in block_rows], axis=0
    ).astype(I32)
    lanes = iota((n_rad * groups, BLOCK), 1)
    chooser = jnp.concatenate(
        [(column == lanes + first).astype(F32).astype(BF16) for first in range(0, slab_blocks, BLOCK)], axis=1
    )
    gas_slab = jnp.concatenate(
        [
            jnp.concatenate([G[d, pl.ds(sz.gas + c * blocks, blocks), :] for d in range(n_rad)], axis=0)
            for c in range(3)
        ],
        axis=1,
    )
    high, low = split2(gas_slab)
    found = dot(chooser, high) + dot(chooser, low)
    for c in range(3):
        near[c] = found[:, c * BLOCK : (c + 1) * BLOCK]

    def rows(first):
        return jnp.concatenate([G[d, pl.ds(first, tiles), :] for d in range(n_rad)], axis=0)

    size = rows(sz.size)
    offset = rows(sz.offset).astype(I32)
    factor = jnp.exp(-DRAG / (size * size))
    mass = size * size * size
    even = iota((T, BLOCK), 1) < GROUP
    dep = []
    for c in range(3):
        u_even = take_lanes(near[c, pl.ds(0, T, stride=2), :], offset)
        u_odd = take_lanes(near[c, pl.ds(1, T, stride=2), :], offset)
        u = jnp.where(even, u_even, u_odd)
        v = rows(sz.motion + (3 + c) * tiles)
        new = u + (v - u) * factor
        state[pl.ds(c * T, T), :] = rows(sz.motion + c * tiles) + STEP * new
        state[pl.ds((3 + c) * T, T), :] = new
        dep.append(-mass * (new - v))
    state[pl.ds(6 * T, T), :] = size
    dep.append(mass)

    mine = pl.multiple_of(r * tiles, tiles)
    for i in range(tiles):
        motion_out[:, i * BLOCK : (i + 1) * BLOCK] = state[pl.ds(mine + i, 6, stride=T), :]

    def state_of(d):
        first = pl.multiple_of(d * tiles, tiles)
        return [state[pl.ds(c * T + first, tiles), :] for c in range(7)]

    wide = jnp.concatenate([axial[0:1, :], axial[1:2, :]], axis=1)
    half = axial.shape[1]
    limit = jnp.where(lane_row < half, counts[0, 0], counts[0, 1])
    place = jnp.where(lane_row < half, lane_row, lane_row - half)
    payload = pick(sz, state_of(r), jnp.where(place < limit, wide, -1))
    pres_first = [G[r, pl.ds(sz.pres + q * layers, 1), :] for q in range(sz.quarters)]
    pres_last = [G[r, pl.ds(sz.pres + q * layers + layers - 1, 1), :] for q in range(sz.quarters)]
    for c in range(7):
        up[c : c + 1, :] = payload[c]
        down[c : c + 1, :] = payload[c]
    for q in range(sz.quarters):
        up[8 + q : 9 + q, :] = pres_last[q]
        down[8 + q : 9 + q, :] = pres_first[q]
    zero_row = jnp.zeros((1, BLOCK), F32)
    for row in (7, *range(8 + sz.quarters, 16)):
        up[row : row + 1, :] = zero_row
        down[row : row + 1, :] = zero_row

    width = arr_rad.shape[2]
    for slot, exists, other in ((0, r > 0, jnp.maximum(r - 1, 0)), (1, r < n_rad - 1, jnp.minimum(r + 1, n_rad - 1))):
        idx = G[other, pl.ds(sz.meta + 1 + slot, 1), :].astype(I32)
        idx = jnp.where(exists, idx, -1)
        got = pick(sz, state_of(other), idx)
        for c in range(7):
            arr_rad[c, slot : slot + 1, :] = got[c][:, :width]

    for c in range(4):
        high = dep[c].astype(BF16).astype(F32)
        low = dep[c] - high
        for piece, part in enumerate((high, low)):
            deps[pl.ds((piece * 8 + c) * T, T), :] = jnp.where(even, part, 0.0)
            deps[pl.ds((piece * 8 + 4 + c) * T, T), :] = jnp.where(even, 0.0, part)
    cell = iota((BLOCK, BLOCK), 0)
    for d in range(n_rad):
        for i in range(tiles):
            t = d * tiles + i
            off = G[d, pl.ds(sz.offset + i, 1), :].astype(I32)
            onehot = (cell == off).astype(F32).astype(BF16)
            lhs = deps[pl.ds(t, 16, stride=T), :].astype(BF16)
            res = dot_nt(lhs, onehot)
            res = res[:8] + res[8:]
            spread[pl.ds(2 * t, 4, stride=2 * T), :] = res[:4]
            spread[pl.ds(2 * t + 1, 4, stride=2 * T), :] = res[4:]
    own = iota((blocks, groups), 0) + r * blocks
    adder = jnp.concatenate(
        [(own == b[:, :groups].astype(I32)).astype(F32) for b in block_rows], axis=1
    ).astype(BF16)
    for c in range(4):
        high, low = split2(spread[pl.ds(c * 2 * T, 2 * T), :])
        total = dot(adder, high) + dot(adder, low)
        for q in range(sz.quarters):
            part = total[q * layers : (q + 1) * layers]
            at = slice(q * BLOCK, (q + 1) * BLOCK)
            if c < 3:
                gas_out[c, :, at] = G[r, pl.ds(sz.gas + c * blocks + q * layers, layers), :] + part
            else:
                liquid[:, at] = part

    pres = jnp.concatenate([G[d, pl.ds(sz.pres, blocks), :] for d in range(n_rad)], axis=0)
    index = kinds[...] * slab_blocks + block_row(sz, cols[...])
    index = jnp.concatenate([index, index], axis=1)
    grouped = [None] * (NT // 2)
    for first in range(0, slab_blocks, BLOCK):
        p_high, p_low = split2(jnp.transpose(pres[first : first + BLOCK]))
        here = iota((BLOCK, BLOCK), 0) + first + jnp.where(iota((BLOCK, BLOCK), 1) < blocks, 0, slab_blocks)
        for j in range(NT // 2):
            aim = here + 2 * j * slab_blocks
            count = (aim == index[0:1]).astype(F32)
            for k in range(1, index.shape[0]):
                count = count + (aim == index[k : k + 1]).astype(F32)
            count = count.astype(BF16)
            part = dot(p_high, count) + dot(p_low, count)
            grouped[j] = part if grouped[j] is None else grouped[j] + part
    sums = [None, None]
    for j in range(NT // 2):
        g_high, g_low = split2(grouped[j])
        for s in range(2):
            t_high, t_low = split2(table[2 * j + s])
            part = dot(t_high, g_high) + dot(t_low, g_high) + dot(t_high, g_low)
            sums[s] = part if sums[s] is None else sums[s] + part
    both = jnp.where(iota((BLOCK, BLOCK), 1) < blocks, sums[0], sums[1])
    both = both + pltpu.roll(jnp.where(iota((BLOCK, BLOCK), 1) < blocks, 0.0, sums[1]), blocks, 1)
    coup[...] = jnp.transpose(both)
    layer = iota((layers, BLOCK), 0)
    for q in range(sz.quarters):
        p = G[r, pl.ds(sz.pres + q * layers, layers), :]
        below = jnp.where(layer == 0, 0.0, pltpu.roll(p, 1, 0))
        above = jnp.where(layer == layers - 1, 0.0, pltpu.roll(p, layers - 1, 0))
        image[:, q * BLOCK : (q + 1) * BLOCK] = (
            DIAG * p - above - below + coup[pl.ds(q, layers, stride=sz.quarters), :]
        )


def finish_kernel(sz, from_lower, from_upper, image, arr_ax, pressure_image):
    half = arr_ax.shape[2]
    arr_ax[:, 0, :] = from_lower[0:7, 0:half]
    arr_ax[:, 1, :] = from_upper[0:7, half : 2 * half]
    pressure_image[...] = image[...]
    last = sz.layers - 1
    for q in range(sz.quarters):
        at = slice(q * BLOCK, (q + 1) * BLOCK)
        pressure_image[0:1, at] = image[0:1, at] - from_lower[8 + q : 9 + q, :]
        pressure_image[last : last + 1, at] = image[last : last + 1, at] - from_upper[8 + q : 9 + q, :]


def on_device(
    parcel_motion,
    parcel_size,
    parcel_block,
    parcel_offset,
    gas_velocity,
    pressure,
    block_cols,
    block_kinds,
    block_table,
    send_axial,
    send_radial,
    send_counts,
):
    n_ax, n_rad = lax.axis_size("ax"), lax.axis_size("rad")
    layers, radial = pressure.shape
    parcels = parcel_size.shape[0]
    sz = Sizes(layers, radial, parcels)
    T = n_rad * sz.tiles
    cap_ax, cap_rad = send_axial.shape[-1], send_radial.shape[-1]
    params = pltpu.CompilerParams(vmem_limit_bytes=VMEM_LIMIT)
    counts = send_counts.reshape(1, 4)
    size2 = parcel_size.reshape(sz.tiles, BLOCK)
    offset2 = parcel_offset.reshape(sz.tiles, BLOCK)

    packed = pl.pallas_call(
        functools.partial(pack_kernel, sz),
        out_shape=jax.ShapeDtypeStruct((sz.rows, BLOCK), F32),
        in_specs=[vmem] * 7 + [smem],
        out_specs=vmem,
        compiler_params=params,
        name="pack",
    )(
        parcel_motion, size2, parcel_block.reshape(1, sz.groups), offset2, gas_velocity, pressure,
        send_radial.reshape(2, cap_rad), counts,
    )
    gathered = lax.all_gather(packed, "rad", axis=0)

    me = lax.axis_index("rad").astype(I32).reshape(1)
    motion_out, arr_rad, gas_out, liquid, image, up, down = pl.pallas_call(
        functools.partial(main_kernel, sz, n_rad),
        out_shape=[
            jax.ShapeDtypeStruct((6, parcels), F32),
            jax.ShapeDtypeStruct((7, 2, cap_rad), F32),
            jax.ShapeDtypeStruct(gas_velocity.shape, F32),
            jax.ShapeDtypeStruct(pressure.shape, F32),
            jax.ShapeDtypeStruct(pressure.shape, F32),
            jax.ShapeDtypeStruct((16, BLOCK), F32),
            jax.ShapeDtypeStruct((16, BLOCK), F32),
        ],
        in_specs=[vmem] * 5 + [smem] * 2,
        out_specs=[vmem] * 7,
        scratch_shapes=[
            pltpu.VMEM((3, n_rad * sz.groups, BLOCK), F32),
            pltpu.VMEM((7 * T, BLOCK), F32),
            pltpu.VMEM((16 * T, BLOCK), F32),
            pltpu.VMEM((4 * 2 * T, BLOCK), F32),
            pltpu.VMEM((BLOCK, BLOCK), F32),
        ],
        compiler_params=params,
        name="slab",
    )(
        gathered,
        block_cols[0].T,
        block_kinds[0].T,
        block_table,
        send_axial.reshape(2, cap_ax),
        counts,
        me,
    )

    from_lower = lax.ppermute(up, "ax", [(i, i + 1) for i in range(n_ax - 1)])
    from_upper = lax.ppermute(down, "ax", [(i + 1, i) for i in range(n_ax - 1)])

    arr_ax, pressure_image = pl.pallas_call(
        functools.partial(finish_kernel, sz),
        out_shape=[
            jax.ShapeDtypeStruct((7, 2, cap_ax), F32),
            jax.ShapeDtypeStruct(pressure.shape, F32),
        ],
        in_specs=[vmem] * 3,
        out_specs=[vmem] * 2,
        compiler_params=params,
        name="finish",
    )(from_lower, from_upper, image)

    arrivals_axial = arr_ax.transpose(1, 0, 2)[None, None]
    arrivals_radial = arr_rad.transpose(1, 0, 2)[None, None]
    return (motion_out, arrivals_axial, arrivals_radial, gas_out, liquid, pressure_image)


def solution(mesh):
    return jax.shard_map(
        on_device,
        mesh=mesh,
        in_specs=(
            P(None, ("ax", "rad")),
            P(("ax", "rad")),
            P(("ax", "rad")),
            P(("ax", "rad")),
            P(None, "ax", "rad"),
            P("ax", "rad"),
            P("ax", "rad", None),
            P("ax", "rad", None),
            P(),
            P("ax", "rad", None, None),
            P("ax", "rad", None, None),
            P("ax", "rad", None),
        ),
        out_specs=(
            P(None, ("ax", "rad")),
            P("ax", "rad", None, None, None),
            P("ax", "rad", None, None, None),
            P(None, "ax", "rad"),
            P("ax", "rad"),
            P("ax", "rad"),
        ),
        check_vma=False,
    )
```

time: 58.8 us -> 24.7 us (0.42)
  the two profiles are of different devices: /device:TPU:0 before, /device:TPU:6 now
where the time goes in v1:
time: 24.7 us; the launch traced here: 24.3 us
  local copies, waits for them, and re-layouts  6.63 us (27%)
  starting transfers between devices  5.83 us (24%)
  waiting for transfers between devices  4.88 us (20%)
  Pallas kernels  4.12 us (17%)
  blocking collectives  2.09 us (8%)
  between operations  0.7 us (3%)
    unnamed x26, local copies, waits for them, and re-layouts  6.63 us
    ppermute x1, waiting for transfers between devices, on_device(): from_upper = lax.ppermute(down, 'ax', [(i + 1, i) for i in range(n_ax - 1)])  4.88 us
    ppermute x1, starting transfers between devices, on_device(): from_lower = lax.ppermute(up, 'ax', [(i, i + 1) for i in range(n_ax - 1)])  3.39 us
    pallas_call x1, Pallas kernels, on_device(): pl.pallas_call(functools.partial(main_kernel, sz, n_rad), out_shape=[jax....  2.86 us
    ppermute x1, starting transfers between devices, on_device(): from_upper = lax.ppermute(down, 'ax', [(i + 1, i) for i in range(n_ax - 1)])  2.44 us
    all_gather x1, blocking collectives, on_device(): gathered = lax.all_gather(packed, 'rad', axis=0)  2.09 us
    pallas_call x1, Pallas kernels, on_device(): pl.pallas_call(functools.partial(finish_kernel, sz), out_shape=[jax.Shape...  0.68 us
    pallas_call x1, Pallas kernels, on_device(): pl.pallas_call(functools.partial(pack_kernel, sz), out_shape=jax.ShapeDty...  0.58 us
  transfers between devices with their start and end apart: 2, of which 1 were waited for; matrix products, arithmetic and copies ran while one was open for 0% of the time, Pallas kernels for 0%

profile of v1, /device:TPU:6, one launch (start us, length us, event | category | flops | bytes accessed | tf_op | source)
XLA Modules:
  0.0 24.3 jit_solution(8013322926734838004)
XLA Ops:
  0.6 0.0 copy-start
  0.6 0.0 copy-start.1
  0.7 0.9 %copy-done.1 = f32[3,16,512]{2,1,0:T(8,128)S(1)} copy-done((f32[3,16,512]{2,1,0:T(8,128)S(1)}, f32[3,16,512]{2,1,0:T(8,128)}, u32[]{:S(2)}) %copy-start.1) | copy-done | bytes 98328
  1.6 0.0 copy-start.2
  1.6 0.8 %copy-done.2 = f32[6,2048]{1,0:T(8,128)S(1)} copy-done((f32[6,2048]{1,0:T(8,128)S(1)}, f32[6,2048]{1,0:T(8,128)}, u32[]{:S(2)}) %copy-start.2) | copy-done | bytes 49176
  2.4 0.0 copy-start.3
  2.4 0.8 %copy-done.3 = f32[16,512]{1,0:T(8,128)S(1)} copy-done((f32[16,512]{1,0:T(8,128)S(1)}, f32[16,512]{1,0:T(8,128)}, u32[]{:S(2)}) %copy-start.3) | copy-done | bytes 32792
  3.2 0.0 copy-start.4
  3.2 0.7 %copy-done.4 = f32[2048]{0:T(1024)S(1)} copy-done((f32[2048]{0:T(1024)S(1)}, f32[2048]{0:T(1024)}, u32[]{:S(2)}) %copy-start.4) | copy-done | bytes 8216
  3.9 0.0 copy-start.5
  3.9 0.7 %copy-done.5 = s32[2048]{0:T(1024)S(1)} copy-done((s32[2048]{0:T(1024)S(1)}, s32[2048]{0:T(1024)}, u32[]{:S(2)}) %copy-start.5) | copy-done | bytes 8216
  4.6 0.0 copy-start.6
  4.6 0.7 %copy-done.6 = s32[1,1,4]{2,1,0:T(1,128)S(1)} copy-done((s32[1,1,4]{2,1,0:T(1,128)S(1)}, s32[1,1,4]{2,1,0:T(1,128)}, u32[]{:S(2)}) %copy-start.6) | copy-done | bytes 40
  5.2 0.0 copy-start.10
  5.2 0.7 %copy-done.10 = s32[1,1,2,32]{3,2,1,0:T(2,128)S(1)} copy-done((s32[1,1,2,32]{3,2,1,0:T(2,128)S(1)}, s32[1,1,2,32]{3,2,1,0:T(2,128)}, u32[]{:S(2)}) %copy-start.10) | copy-done | bytes 280
  5.9 0.0 copy-start.12
  5.9 0.7 %copy-done.12 = s32[32]{0:T(128)S(1)} copy-done((s32[32]{0:T(128)S(1)}, s32[32]{0:T(128)}, u32[]{:S(2)}) %copy-start.12) | copy-done | bytes 152
  6.6 0.6 %pack.1 = f32[392,128]{1,0:T(8,128)S(1)} custom-call(f32[6,2048]{1,0:T(8,128)S(1)} %copy-done.2, f32[16,128]{1,0:T(8,128)S(1)} %bitcast.21, s32[1,32]{1,0:T(1,128)S(1)} %bitcast.29, s32[16,128]{1,0:T(8,128)S(1)} %bitcast.22, f32[3,16,512]{2,1,0:T(8,128)S(1)} %copy-done.1, f32[16,512]{1,0:T(8,128)S(1)} %copy-done.3, s32[2,32]{1,0:T(2,128)S(1)} %bitcast.27, ...), custom_call_target="tpu_custom_call" | custom-call | tf_op jit(solution)/shard_map/pack/pallas_call | solution.py:286
  7.2 2.1 %all-gather = f32[784,128]{1,0:T(8,128)S(1)} all-gather(f32[392,128]{1,0:T(8,128)S(1)} %pack.1), channel_id=2, replica_groups=mesh['ax'=16,'rad'=2] {'rad'}, dimensions={0}, use_global_device_ids=true | all-gather | bytes 602112 | tf_op jit(solution)/shard_map/all_gather | solution.py:297
  9.3 0.0 copy-start.9
  9.3 0.0 copy-start.8
  9.3 0.0 copy-start.7
  9.3 0.0 copy-start.11
  9.3 0.0 copy-done
  9.3 0.7 %copy-done.9 = s32[1,64,4]{1,2,0:T(4,128)S(1)} copy-done((s32[1,64,4]{1,2,0:T(4,128)S(1)}, s32[1,64,4]{1,2,0:T(4,128)}, u32[]{:S(2)}) %copy-start.9) | copy-done | bytes 1048
  9.9 0.0 copy-done.8
  10.0 0.0 copy-done.7
  10.0 0.0 copy-done.11
  10.0 2.9 %slab.1 = (f32[6,2048]{1,0:T(8,128)}, f32[7,2,32]{2,1,0:T(2,128)}, f32[3,16,512]{2,1,0:T(8,128)}, f32[16,512]{1,0:T(8,128)}, f32[16,512]{1,0:T(8,128)S(1)}, /*in...) custom-call(f32[2,392,128]{2,1,0:T(8,128)S(1)} %bitcast.20, s32[4,64]{1,0:T(4,128)S(1)} %bitcast.25, s32[4,64]{1,0:T(4,128)S(1)} %bitcast.26, ...), custom_call_target="tpu_custom_call" | custom-call | tf_op jit(solution)/shard_map/slab/pallas_call | solution.py:300
  12.8 3.4 %collective-permute-start = (f32[16,128]{1,0:T(8,128)S(1)}, f32[16,128]{1,0:T(8,128)S(1)}, u32[]{:S(2)}, u32[]{:S(2)}) collective-permute-start(f32[16,128]{1,0:T(8,128)S(1)} %get-tuple-element.16), channel_id=1, source_target_pairs={{0,2},{2,4},{4,6},{6,8},{8,10},{10,12},{12,14},{14,16},{16,18},{18... | collective-permute-start | bytes 24584 | tf_op jit(solution)/shard_map/ppermute | solution.py:332
  16.2 2.4 %collective-permute-start.1 = (f32[16,128]{1,0:T(8,128)S(1)}, f32[16,128]{1,0:T(8,128)S(1)}, u32[]{:S(2)}, u32[]{:S(2)}) collective-permute-start(f32[16,128]{1,0:T(8,128)S(1)} %get-tuple-element.17), channel_id=1, source_target_pairs={{2,0},{4,2},{6,4},{8,6},{10,8},{12,10},{14,12},{16,14},{18,16},{20... | collective-permute-start | bytes 24584 | tf_op jit(solution)/shard_map/ppermute | solution.py:333
  18.7 0.0 collective-permute-done.from_lower
  18.7 4.9 %collective-permute-done.1.from_upper = f32[16,128]{1,0:T(8,128)S(1)} collective-permute-done((f32[16,128]{1,0:T(8,128)S(1)}, f32[16,128]{1,0:T(8,128)S(1)}, u32[]{:S(2)}, u32[]{:S(2)}) %collective-permute-start.1) | collective-permute-done | bytes 8224 | tf_op jit(solution)/shard_map/ppermute | solution.py:333
  23.6 0.7 %finish.1 = (f32[7,2,64]{2,1,0:T(2,128)}, f32[16,512]{1,0:T(8,128)}) custom-call(f32[16,128]{1,0:T(8,128)S(1)} %collective-permute-done.from_lower, f32[16,128]{1,0:T(8,128)S(1)} %collective-permute-done.1.from_upper, f32[16,512]{1,0:T(8,128)S(1)} %get-tuple-element.18.image), custom_call_target="tpu_custom_call" | custom-call | tf_op jit(solution)/shard_map/finish/pallas_call | solution.py:335
Async XLA Ops:
  0.6 8.6 %copy-start = (f32[8,128,128]{2,1,0:T(8,128)S(1)}, f32[8,128,128]{2,1,0:T(8,128)}, u32[]{:S(2)}) copy-start(f32[8,128,128]{2,1,0:T(8,128)} %table.1) | copy-start | bytes 1572868
  0.6 0.9 %copy-start.1 = (f32[3,16,512]{2,1,0:T(8,128)S(1)}, f32[3,16,512]{2,1,0:T(8,128)}, u32[]{:S(2)}) copy-start(f32[3,16,512]{2,1,0:T(8,128)} %gas.1) | copy-start | bytes 294916
  1.6 0.8 %copy-start.2 = (f32[6,2048]{1,0:T(8,128)S(1)}, f32[6,2048]{1,0:T(8,128)}, u32[]{:S(2)}) copy-start(f32[6,2048]{1,0:T(8,128)} %motion.1) | copy-start | bytes 147460
  2.4 0.8 %copy-start.3 = (f32[16,512]{1,0:T(8,128)S(1)}, f32[16,512]{1,0:T(8,128)}, u32[]{:S(2)}) copy-start(f32[16,512]{1,0:T(8,128)} %pres.1) | copy-start | bytes 98308
  3.2 0.7 %copy-start.4 = (f32[2048]{0:T(1024)S(1)}, f32[2048]{0:T(1024)}, u32[]{:S(2)}) copy-start(f32[2048]{0:T(1024)} %param.13) | copy-start | bytes 24580
  3.9 0.7 %copy-start.5 = (s32[2048]{0:T(1024)S(1)}, s32[2048]{0:T(1024)}, u32[]{:S(2)}) copy-start(s32[2048]{0:T(1024)} %param.15) | copy-start | bytes 24580
  4.6 0.7 %copy-start.6 = (s32[1,1,4]{2,1,0:T(1,128)S(1)}, s32[1,1,4]{2,1,0:T(1,128)}, u32[]{:S(2)}) copy-start(s32[1,1,4]{2,1,0:T(1,128)} %param.23) | copy-start | bytes 52
  5.2 0.7 %copy-start.10 = (s32[1,1,2,32]{3,2,1,0:T(2,128)S(1)}, s32[1,1,2,32]{3,2,1,0:T(2,128)}, u32[]{:S(2)}) copy-start(s32[1,1,2,32]{3,2,1,0:T(2,128)} %param.22) | copy-start | bytes 772
  5.9 0.7 %copy-start.12 = (s32[32]{0:T(128)S(1)}, s32[32]{0:T(128)}, u32[]{:S(2)}) copy-start(s32[32]{0:T(128)} %param.14) | copy-start | bytes 388
  9.3 0.7 %copy-start.9 = (s32[1,64,4]{1,2,0:T(4,128)S(1)}, s32[1,64,4]{1,2,0:T(4,128)}, u32[]{:S(2)}) copy-start(s32[1,64,4]{1,2,0:T(4,128)} %param.19) | copy-start | bytes 3076
  9.3 0.7 %copy-start.8 = (s32[1,64,4]{1,2,0:T(4,128)S(1)}, s32[1,64,4]{1,2,0:T(4,128)}, u32[]{:S(2)}) copy-start(s32[1,64,4]{1,2,0:T(4,128)} %param.18) | copy-start | bytes 3076
  9.3 0.7 %copy-start.7 = (s32[1,1,4]{2,1,0:T(1,128)S(1)}, s32[1,1,4]{2,1,0:T(1,128)}, u32[]{:S(2)}) copy-start(s32[1,1,4]{2,1,0:T(1,128)} %param.23) | copy-start | bytes 52
  9.3 0.7 %copy-start.11 = (s32[1,1,2,64]{3,2,1,0:T(2,128)S(1)}, s32[1,1,2,64]{3,2,1,0:T(2,128)}, u32[]{:S(2)}) copy-start(s32[1,1,2,64]{3,2,1,0:T(2,128)} %param.21) | copy-start | bytes 1540
  12.8 5.8 %collective-permute-start = (f32[16,128]{1,0:T(8,128)S(1)}, f32[16,128]{1,0:T(8,128)S(1)}, u32[]{:S(2)}, u32[]{:S(2)}) collective-permute-start(f32[16,128]{1,0:T(8,128)S(1)} %get-tuple-element.16), channel_id=1, source_target_pairs={{0,2},{2,4},{4,6},{6,8},{8,10},{10,12},{12,14},{14,16},{16,18},{18... | collective-permute-start | bytes 24584 | tf_op jit(solution)/shard_map/ppermute | solution.py:332
  16.2 7.3 %collective-permute-start.1 = (f32[16,128]{1,0:T(8,128)S(1)}, f32[16,128]{1,0:T(8,128)S(1)}, u32[]{:S(2)}, u32[]{:S(2)}) collective-permute-start(f32[16,128]{1,0:T(8,128)S(1)} %get-tuple-element.17), channel_id=1, source_target_pairs={{2,0},{4,2},{6,4},{8,6},{10,8},{12,10},{14,12},{16,14},{18,16},{20... | collective-permute-start | bytes 24584 | tf_op jit(solution)/shard_map/ppermute | solution.py:333

commit v2 on v1

--- a/solution.py
+++ b/solution.py
@@ -20,7 +20,7 @@
 I32 = jnp.int32
 
 vmem = pl.BlockSpec(memory_space=pltpu.VMEM)
-smem = pl.BlockSpec(memory_space=pltpu.SMEM)
+hbm = pl.BlockSpec(memory_space=pltpu.HBM)
 
 
 class Sizes:
@@ -61,7 +61,23 @@
     return b - local + (local % sz.quarters) * sz.layers + local // sz.quarters
 
 
-def pack_kernel(sz, motion, size, block, offset, gas, pres, lists, counts, out):
+def pack_kernel(
+    sz, n_rad, motion_hbm, size_hbm, block_hbm, offset_hbm, gas_hbm, pres_hbm, radial_hbm, counts_hbm, cols_hbm,
+    kinds_hbm, axial_hbm,
+    out, aux,
+    motion, size, block, offset, gas, pres, radial, counts, cols, kinds, axial, sem,
+):
+    pairs = (
+        (counts_hbm, counts), (gas_hbm, gas), (motion_hbm, motion), (pres_hbm, pres), (size_hbm, size),
+        (offset_hbm, offset), (block_hbm, block), (radial_hbm, radial), (cols_hbm, cols), (kinds_hbm, kinds),
+        (axial_hbm, axial),
+    )
+    copies = [pltpu.make_async_copy(src, dst, sem.at[i]) for i, (src, dst) in enumerate(pairs)]
+    for copy in copies:
+        copy.start()
+    out[pl.ds(sz.meta, 8), :] = jnp.full((8, BLOCK), -1.0, F32)
+    for copy in copies:
+        copy.wait()
     layers = sz.layers
     for c in range(3):
         for q in range(sz.quarters):
@@ -72,13 +88,18 @@
         out[pl.ds(sz.motion + i, 6, stride=sz.tiles), :] = motion[:, i * BLOCK : (i + 1) * BLOCK]
     out[pl.ds(sz.size, sz.tiles), :] = size[...]
     out[pl.ds(sz.offset, sz.tiles), :] = offset[...].astype(F32)
-    out[pl.ds(sz.meta, 8), :] = jnp.full((8, BLOCK), -1.0, F32)
     out[pl.ds(sz.meta, 1), pl.ds(0, sz.groups)] = block_row(sz, block[...]).astype(F32)
-    width = lists.shape[1]
+    width = radial.shape[1]
     lane = iota((1, width), 1)
     for slot in range(2):
-        kept = jnp.where(lane < counts[0, 2 + slot], lists[slot : slot + 1, :], -1)
+        kept = jnp.where(lane < counts[0, 2 + slot], radial[slot : slot + 1, :], -1)
         out[pl.ds(sz.meta + 1 + slot, 1), pl.ds(0, width)] = kept.astype(F32)
+
+    index = kinds[...] * (n_rad * sz.blocks) + block_row(sz, cols[...])
+    aux[pl.ds(0, index.shape[0]), :] = jnp.concatenate([index, index], axis=1)
+    lane = iota((1, axial.shape[1]), 1)
+    kept = [jnp.where(lane < counts[0, slot], axial[slot : slot + 1, :], -1) for slot in range(2)]
+    aux[pl.ds(8, 1), :] = jnp.concatenate(kept, axis=1)
 
 
 def take_lanes(x, idx):
@@ -94,15 +115,20 @@
 
 
 def main_kernel(
-    sz, n_rad, G, cols, kinds, table, axial, counts, me,
-    motion_out, arr_rad, gas_out, liquid, image, up, down,
-    near, state, deps, spread, coup,
+    sz, n_rad, G, aux, table,
+    motion_hbm, arr_hbm, gas_hbm, liquid_hbm, image, message,
+    near, state, deps, spread, coup, motion_out, arr_rad, gas_out, liquid, sem,
 ):
-    r = me[0]
+    r = lax.axis_index("rad")
+    sends = [
+        pltpu.make_async_copy(src, dst, sem.at[i])
+        for i, (src, dst) in enumerate(
+            ((motion_out, motion_hbm), (arr_rad, arr_hbm), (gas_out, gas_hbm), (liquid, liquid_hbm))
+        )
+    ]
     layers, tiles, blocks, groups = sz.layers, sz.tiles, sz.blocks, sz.groups
     slab_blocks = n_rad * blocks
     T = n_rad * tiles
-    lane_row = iota((1, BLOCK), 1)
 
     block_rows = [G[d, pl.ds(sz.meta, 1), :] for d in range(n_rad)]
     column = jnp.concatenate(
@@ -148,28 +174,20 @@
     mine = pl.multiple_of(r * tiles, tiles)
     for i in range(tiles):
         motion_out[:, i * BLOCK : (i + 1) * BLOCK] = state[pl.ds(mine + i, 6, stride=T), :]
+    sends[0].start()
 
     def state_of(d):
         first = pl.multiple_of(d * tiles, tiles)
         return [state[pl.ds(c * T + first, tiles), :] for c in range(7)]
 
-    wide = jnp.concatenate([axial[0:1, :], axial[1:2, :]], axis=1)
-    half = axial.shape[1]
-    limit = jnp.where(lane_row < half, counts[0, 0], counts[0, 1])
-    place = jnp.where(lane_row < half, lane_row, lane_row - half)
-    payload = pick(sz, state_of(r), jnp.where(place < limit, wide, -1))
-    pres_first = [G[r, pl.ds(sz.pres + q * layers, 1), :] for q in range(sz.quarters)]
-    pres_last = [G[r, pl.ds(sz.pres + q * layers + layers - 1, 1), :] for q in range(sz.quarters)]
+    payload = pick(sz, state_of(r), aux[pl.ds(8, 1), :])
     for c in range(7):
-        up[c : c + 1, :] = payload[c]
-        down[c : c + 1, :] = payload[c]
+        message[c : c + 1, :] = payload[c]
+    message[7:8, :] = jnp.zeros((1, BLOCK), F32)
     for q in range(sz.quarters):
-        up[8 + q : 9 + q, :] = pres_last[q]
-        down[8 + q : 9 + q, :] = pres_first[q]
-    zero_row = jnp.zeros((1, BLOCK), F32)
-    for row in (7, *range(8 + sz.quarters, 16)):
-        up[row : row + 1, :] = zero_row
-        down[row : row + 1, :] = zero_row
+        first = sz.pres + q * layers
+        message[8 + q : 9 + q, :] = G[r, pl.ds(first + layers - 1, 1), :]
+        message[12 + q : 13 + q, :] = G[r, pl.ds(first, 1), :]
 
     width = arr_rad.shape[2]
     for slot, exists, other in ((0, r > 0, jnp.maximum(r - 1, 0)), (1, r < n_rad - 1, jnp.minimum(r + 1, n_rad - 1))):
@@ -178,6 +196,7 @@
         got = pick(sz, state_of(other), idx)
         for c in range(7):
             arr_rad[c, slot : slot + 1, :] = got[c][:, :width]
+    sends[1].start()
 
     for c in range(4):
         high = dep[c].astype(BF16).astype(F32)
@@ -210,10 +229,11 @@
                 gas_out[c, :, at] = G[r, pl.ds(sz.gas + c * blocks + q * layers, layers), :] + part
             else:
                 liquid[:, at] = part
+    sends[2].start()
+    sends[3].start()
 
     pres = jnp.concatenate([G[d, pl.ds(sz.pres, blocks), :] for d in range(n_rad)], axis=0)
-    index = kinds[...] * slab_blocks + block_row(sz, cols[...])
-    index = jnp.concatenate([index, index], axis=1)
+    index = aux[pl.ds(0, 4), :]
     grouped = [None] * (NT // 2)
     for first in range(0, slab_blocks, BLOCK):
         p_high, p_low = split2(jnp.transpose(pres[first : first + BLOCK]))
@@ -244,18 +264,23 @@
         image[:, q * BLOCK : (q + 1) * BLOCK] = (
             DIAG * p - above - below + coup[pl.ds(q, layers, stride=sz.quarters), :]
         )
-
-
-def finish_kernel(sz, from_lower, from_upper, image, arr_ax, pressure_image):
+    for send in sends:
+        send.wait()
+
+
+def finish_kernel(sz, got_a, got_b, image, arr_ax, pressure_image):
+    even = lax.axis_index("ax") % 2 == 0
+    low = jnp.where(even, got_b[...], got_a[...])
+    up = jnp.where(even, got_a[...], got_b[...])
     half = arr_ax.shape[2]
-    arr_ax[:, 0, :] = from_lower[0:7, 0:half]
-    arr_ax[:, 1, :] = from_upper[0:7, half : 2 * half]
+    arr_ax[:, 0, :] = low[0:7, 0:half]
+    arr_ax[:, 1, :] = up[0:7, half : 2 * half]
     pressure_image[...] = image[...]
     last = sz.layers - 1
     for q in range(sz.quarters):
         at = slice(q * BLOCK, (q + 1) * BLOCK)
-        pressure_image[0:1, at] = image[0:1, at] - from_lower[8 + q : 9 + q, :]
-        pressure_image[last : last + 1, at] = image[last : last + 1, at] - from_upper[8 + q : 9 + q, :]
+        pressure_image[0:1, at] = image[0:1, at] - low[8 + q : 9 + q, :]
+        pressure_image[last : last + 1, at] = image[last : last + 1, at] - up[12 + q : 13 + q, :]
 
 
 def on_device(
@@ -283,21 +308,43 @@
     size2 = parcel_size.reshape(sz.tiles, BLOCK)
     offset2 = parcel_offset.reshape(sz.tiles, BLOCK)
 
-    packed = pl.pallas_call(
-        functools.partial(pack_kernel, sz),
-        out_shape=jax.ShapeDtypeStruct((sz.rows, BLOCK), F32),
-        in_specs=[vmem] * 7 + [smem],
-        out_specs=vmem,
+    packed, aux = pl.pallas_call(
+        functools.partial(pack_kernel, sz, n_rad),
+        out_shape=[
+            jax.ShapeDtypeStruct((sz.rows, BLOCK), F32),
+            jax.ShapeDtypeStruct((16, BLOCK), I32),
+        ],
+        in_specs=[hbm] * 11,
+        out_specs=[vmem] * 2,
+        scratch_shapes=[
+            pltpu.VMEM(parcel_motion.shape, F32),
+            pltpu.VMEM(size2.shape, F32),
+            pltpu.VMEM((1, sz.groups), I32),
+            pltpu.VMEM(offset2.shape, I32),
+            pltpu.VMEM(gas_velocity.shape, F32),
+            pltpu.VMEM(pressure.shape, F32),
+            pltpu.VMEM((2, cap_rad), I32),
+            pltpu.SMEM((1, 4), I32),
+            pltpu.VMEM((4, sz.blocks), I32),
+            pltpu.VMEM((4, sz.blocks), I32),
+            pltpu.VMEM((2, cap_ax), I32),
+            pltpu.SemaphoreType.DMA((11,)),
+        ],
         compiler_params=params,
         name="pack",
     )(
-        parcel_motion, size2, parcel_block.reshape(1, sz.groups), offset2, gas_velocity, pressure,
-        send_radial.reshape(2, cap_rad), counts,
+        *(
+            pltpu.with_memory_space_constraint(x, pltpu.HBM)
+            for x in (
+                parcel_motion, size2, parcel_block.reshape(1, sz.groups), offset2, gas_velocity, pressure,
+                send_radial.reshape(2, cap_rad), counts, block_cols[0].T, block_kinds[0].T,
+                send_axial.reshape(2, cap_ax),
+            )
+        )
     )
     gathered = lax.all_gather(packed, "rad", axis=0)
 
-    me = lax.axis_index("rad").astype(I32).reshape(1)
-    motion_out, arr_rad, gas_out, liquid, image, up, down = pl.pallas_call(
+    motion_out, arr_rad, gas_out, liquid, image, message = pl.pallas_call(
         functools.partial(main_kernel, sz, n_rad),
         out_shape=[
             jax.ShapeDtypeStruct((6, parcels), F32),
@@ -306,31 +353,31 @@
             jax.ShapeDtypeStruct(pressure.shape, F32),
             jax.ShapeDtypeStruct(pressure.shape, F32),
             jax.ShapeDtypeStruct((16, BLOCK), F32),
-            jax.ShapeDtypeStruct((16, BLOCK), F32),
-        ],
-        in_specs=[vmem] * 5 + [smem] * 2,
-        out_specs=[vmem] * 7,
+        ],
+        in_specs=[vmem] * 3,
+        out_specs=[hbm] * 4 + [vmem] * 2,
         scratch_shapes=[
             pltpu.VMEM((3, n_rad * sz.groups, BLOCK), F32),
             pltpu.VMEM((7 * T, BLOCK), F32),
             pltpu.VMEM((16 * T, BLOCK), F32),
             pltpu.VMEM((4 * 2 * T, BLOCK), F32),
             pltpu.VMEM((BLOCK, BLOCK), F32),
+            pltpu.VMEM((6, parcels), F32),
+            pltpu.VMEM((7, 2, cap_rad), F32),
+            pltpu.VMEM(gas_velocity.shape, F32),
+            pltpu.VMEM(pressure.shape, F32),
+            pltpu.SemaphoreType.DMA((4,)),
         ],
         compiler_params=params,
         name="slab",
-    )(
-        gathered,
-        block_cols[0].T,
-        block_kinds[0].T,
-        block_table,
-        send_axial.reshape(2, cap_ax),
-        counts,
-        me,
-    )
-
-    from_lower = lax.ppermute(up, "ax", [(i, i + 1) for i in range(n_ax - 1)])
-    from_upper = lax.ppermute(down, "ax", [(i + 1, i) for i in range(n_ax - 1)])
+    )(gathered, aux, block_table)
+
+    def exchange(first):
+        pairs = [(i, i + 1) for i in range(first, n_ax - 1, 2)]
+        return lax.ppermute(message, "ax", pairs + [(j, i) for i, j in pairs])
+
+    got_b = exchange(1)
+    got_a = exchange(0)
 
     arr_ax, pressure_image = pl.pallas_call(
         functools.partial(finish_kernel, sz),
@@ -342,7 +389,7 @@
         out_specs=[vmem] * 2,
         compiler_params=params,
         name="finish",
-    )(from_lower, from_upper, image)
+    )(got_a, got_b, image)
 
     arrivals_axial = arr_ax.transpose(1, 0, 2)[None, None]
     arrivals_radial = arr_rad.transpose(1, 0, 2)[None, None]

time: 24.7 us -> 15.2 us (0.62)
  the two profiles are of different devices: /device:TPU:6 before, /device:TPU:0 now
where the time goes in v2:
time: 15.2 us; the launch traced here: 15 us
  starting transfers between devices  6.32 us (42%)
  Pallas kernels  4.22 us (28%)
  blocking collectives  2.17 us (14%)
  waiting for transfers between devices  1.63 us (11%)
  between operations  0.67 us (4%)
    ppermute x2, starting transfers between devices, exchange(): return lax.ppermute(message, 'ax', pairs + [(j, i) for i, j in pairs])  6.32 us
    pallas_call x1, Pallas kernels, on_device(): pl.pallas_call(functools.partial(main_kernel, sz, n_rad), out_shape=[jax....  2.37 us
    all_gather x1, blocking collectives, on_device(): gathered = lax.all_gather(packed, 'rad', axis=0)  2.17 us
    ppermute x2, waiting for transfers between devices, exchange(): return lax.ppermute(message, 'ax', pairs + [(j, i) for i, j in pairs])  1.63 us
    pallas_call x1, Pallas kernels, on_device(): pl.pallas_call(functools.partial(pack_kernel, sz, n_rad), out_shape=[jax....  1.18 us
    pallas_call x1, Pallas kernels, on_device(): pl.pallas_call(functools.partial(finish_kernel, sz), out_shape=[jax.Shape...  0.68 us
  transfers between devices with their start and end apart: 2, of which 1 were waited for; matrix products, arithmetic and copies ran while one was open for 0% of the time, Pallas kernels for 0%

profile of v2, /device:TPU:0, one launch (start us, length us, event | category | flops | bytes accessed | tf_op | source)
XLA Modules:
  0.0 15.0 jit_solution(9461999989493073404)
XLA Ops:
  0.6 0.0 copy-start
  0.6 1.2 %pack.1 = (f32[392,128]{1,0:T(8,128)S(1)}, s32[16,128]{1,0:T(8,128)S(1)}) custom-call(f32[6,2048]{1,0:T(8,128)} %motion_hbm.1, f32[16,128]{1,0:T(8,128)} %bitcast.20, s32[1,32]{1,0:T(1,128)} %bitcast.26, s32[16,128]{1,0:T(8,128)} %bitcast.21, f32[3,16,512]{2,1,0:T(8,128)} %gas_hbm.1, f32[16,512]{1,0:T(8,128)} %pres_hbm.1, s32[2,32]{1,0:T(2,128)} %bitcast.24, ...), custom_call_target="tpu_custom_call" | custom-call | tf_op jit(solution)/shard_map/pack/pallas_call | solution.py:311
  1.8 2.2 %all-gather = f32[784,128]{1,0:T(8,128)S(1)} all-gather(f32[392,128]{1,0:T(8,128)S(1)} %get-tuple-element.16), channel_id=2, replica_groups=mesh['ax'=16,'rad'=2] {'rad'}, dimensions={0}, use_global_device_ids=true | all-gather | bytes 602112 | tf_op jit(solution)/shard_map/all_gather | solution.py:345
  4.0 0.0 copy-done
  4.0 2.4 %slab.1 = (f32[6,2048]{1,0:T(8,128)}, f32[7,2,32]{2,1,0:T(2,128)}, f32[3,16,512]{2,1,0:T(8,128)}, f32[16,512]{1,0:T(8,128)}, f32[16,512]{1,0:T(8,128)S(1)}, /*index=5*/f32[16,128]{1,0:T(8,128)S(1)}) custom-call(f32[2,392,128]{2,1,0:T(8,128)S(1)} %bitcast.19, s32[16,128]{1,0:T(8,128)S(1)} %get-tuple-element.17.aux, f32[8,128,128]{2,1,0:T(8,128)S(1)} %copy-done), custom_call_target="tpu_custom_call" | custom-call | tf_op jit(solution)/shard_map/slab/pallas_call | solution.py:347
  6.4 0.7 %collective-permute-start.1 = (f32[16,128]{1,0:T(8,128)S(1)}, f32[16,128]{1,0:T(8,128)S(1)}, u32[]{:S(2)}, u32[]{:S(2)}) collective-permute-start(f32[16,128]{1,0:T(8,128)S(1)} %get-tuple-element.19), channel_id=1, source_target_pairs={{2,4},{6,8},{10,12},{14,16},{18,20},{22,24},{26,28},{4,2},{8,6},{1... | collective-permute-start | bytes 24584 | tf_op jit(solution)/shard_map/ppermute | solution.py:377
  7.1 5.7 %collective-permute-start = (f32[16,128]{1,0:T(8,128)S(1)}, f32[16,128]{1,0:T(8,128)S(1)}, u32[]{:S(2)}, u32[]{:S(2)}) collective-permute-start(f32[16,128]{1,0:T(8,128)S(1)} %get-tuple-element.19), channel_id=1, source_target_pairs={{0,2},{4,6},{8,10},{12,14},{16,18},{20,22},{24,26},{28,30},{2,0},{... | collective-permute-start | bytes 24584 | tf_op jit(solution)/shard_map/ppermute | solution.py:377
  12.7 0.0 collective-permute-done.1.got_b
  12.7 1.6 %collective-permute-done.got_a = f32[16,128]{1,0:T(8,128)S(1)} collective-permute-done((f32[16,128]{1,0:T(8,128)S(1)}, f32[16,128]{1,0:T(8,128)S(1)}, u32[]{:S(2)}, u32[]{:S(2)}) %collective-permute-start) | collective-permute-done | bytes 8224 | tf_op jit(solution)/shard_map/ppermute | solution.py:377
  14.3 0.7 %finish.1 = (f32[7,2,64]{2,1,0:T(2,128)}, f32[16,512]{1,0:T(8,128)}) custom-call(f32[16,128]{1,0:T(8,128)S(1)} %collective-permute-done.got_a, f32[16,128]{1,0:T(8,128)S(1)} %collective-permute-done.1.got_b, f32[16,512]{1,0:T(8,128)S(1)} %get-tuple-element.20.image), custom_call_target="tpu_custom_call" | custom-call | tf_op jit(solution)/shard_map/finish/pallas_call | solution.py:382
Async XLA Ops:
  0.6 3.4 %copy-start = (f32[8,128,128]{2,1,0:T(8,128)S(1)}, f32[8,128,128]{2,1,0:T(8,128)}, u32[]{:S(2)}) copy-start(f32[8,128,128]{2,1,0:T(8,128)} %table.1) | copy-start | bytes 1572868
  6.4 6.3 %collective-permute-start.1 = (f32[16,128]{1,0:T(8,128)S(1)}, f32[16,128]{1,0:T(8,128)S(1)}, u32[]{:S(2)}, u32[]{:S(2)}) collective-permute-start(f32[16,128]{1,0:T(8,128)S(1)} %get-tuple-element.19), channel_id=1, source_target_pairs={{2,4},{6,8},{10,12},{14,16},{18,20},{22,24},{26,28},{4,2},{8,6},{1... | collective-permute-start | bytes 24584 | tf_op jit(solution)/shard_map/ppermute | solution.py:377
  7.1 7.3 %collective-permute-start = (f32[16,128]{1,0:T(8,128)S(1)}, f32[16,128]{1,0:T(8,128)S(1)}, u32[]{:S(2)}, u32[]{:S(2)}) collective-permute-start(f32[16,128]{1,0:T(8,128)S(1)} %get-tuple-element.19), channel_id=1, source_target_pairs={{0,2},{4,6},{8,10},{12,14},{16,18},{20,22},{24,26},{28,30},{2,0},{... | collective-permute-start | bytes 24584 | tf_op jit(solution)/shard_map/ppermute | solution.py:377

commit v3 on v2

--- a/solution.py
+++ b/solution.py
@@ -114,18 +114,17 @@
     return [jnp.sum(jnp.where(here, take_lanes(s, lane), 0.0), axis=0, keepdims=True) for s in state]
 
 
-def main_kernel(
-    sz, n_rad, G, aux, table,
-    motion_hbm, arr_hbm, gas_hbm, liquid_hbm, image, message,
-    near, state, deps, spread, coup, motion_out, arr_rad, gas_out, liquid, sem,
-):
+def slab_rows(sz, n_rad, G, first):
+    return jnp.concatenate([G[d, pl.ds(first, sz.tiles), :] for d in range(n_rad)], axis=0)
+
+
+def state_of(sz, T, state, d):
+    first = pl.multiple_of(d * sz.tiles, sz.tiles)
+    return [state[pl.ds(c * T + first, sz.tiles), :] for c in range(7)]
+
+
+def move_kernel(sz, n_rad, G, aux, state, message, near):
     r = lax.axis_index("rad")
-    sends = [
-        pltpu.make_async_copy(src, dst, sem.at[i])
-        for i, (src, dst) in enumerate(
-            ((motion_out, motion_hbm), (arr_rad, arr_hbm), (gas_out, gas_hbm), (liquid, liquid_hbm))
-        )
-    ]
     layers, tiles, blocks, groups = sz.layers, sz.tiles, sz.blocks, sz.groups
     slab_blocks = n_rad * blocks
     T = n_rad * tiles
@@ -150,15 +149,11 @@
     for c in range(3):
         near[c] = found[:, c * BLOCK : (c + 1) * BLOCK]
 
-    def rows(first):
-        return jnp.concatenate([G[d, pl.ds(first, tiles), :] for d in range(n_rad)], axis=0)
-
+    rows = functools.partial(slab_rows, sz, n_rad, G)
     size = rows(sz.size)
     offset = rows(sz.offset).astype(I32)
     factor = jnp.exp(-DRAG / (size * size))
-    mass = size * size * size
     even = iota((T, BLOCK), 1) < GROUP
-    dep = []
     for c in range(3):
         u_even = take_lanes(near[c, pl.ds(0, T, stride=2), :], offset)
         u_odd = take_lanes(near[c, pl.ds(1, T, stride=2), :], offset)
@@ -167,20 +162,9 @@
         new = u + (v - u) * factor
         state[pl.ds(c * T, T), :] = rows(sz.motion + c * tiles) + STEP * new
         state[pl.ds((3 + c) * T, T), :] = new
-        dep.append(-mass * (new - v))
     state[pl.ds(6 * T, T), :] = size
-    dep.append(mass)
-
-    mine = pl.multiple_of(r * tiles, tiles)
-    for i in range(tiles):
-        motion_out[:, i * BLOCK : (i + 1) * BLOCK] = state[pl.ds(mine + i, 6, stride=T), :]
-    sends[0].start()
-
-    def state_of(d):
-        first = pl.multiple_of(d * tiles, tiles)
-        return [state[pl.ds(c * T + first, tiles), :] for c in range(7)]
-
-    payload = pick(sz, state_of(r), aux[pl.ds(8, 1), :])
+
+    payload = pick(sz, state_of(sz, T, state, r), aux[pl.ds(8, 1), :])
     for c in range(7):
         message[c : c + 1, :] = payload[c]
     message[7:8, :] = jnp.zeros((1, BLOCK), F32)
@@ -189,14 +173,43 @@
         message[8 + q : 9 + q, :] = G[r, pl.ds(first + layers - 1, 1), :]
         message[12 + q : 13 + q, :] = G[r, pl.ds(first, 1), :]
 
+
+def rest_kernel(
+    sz, n_rad, G, aux, table, state,
+    motion_hbm, arr_hbm, gas_hbm, liquid_hbm, image,
+    deps, spread, coup, motion_out, arr_rad, gas_out, liquid, sem,
+):
+    r = lax.axis_index("rad")
+    sends = [
+        pltpu.make_async_copy(src, dst, sem.at[i])
+        for i, (src, dst) in enumerate(
+            ((motion_out, motion_hbm), (arr_rad, arr_hbm), (gas_out, gas_hbm), (liquid, liquid_hbm))
+        )
+    ]
+    layers, tiles, blocks, groups = sz.layers, sz.tiles, sz.blocks, sz.groups
+    slab_blocks = n_rad * blocks
+    T = n_rad * tiles
+    block_rows = [G[d, pl.ds(sz.meta, 1), :] for d in range(n_rad)]
+
+    mine = pl.multiple_of(r * tiles, tiles)
+    for i in range(tiles):
+        motion_out[:, i * BLOCK : (i + 1) * BLOCK] = state[pl.ds(mine + i, 6, stride=T), :]
+    sends[0].start()
+
     width = arr_rad.shape[2]
     for slot, exists, other in ((0, r > 0, jnp.maximum(r - 1, 0)), (1, r < n_rad - 1, jnp.minimum(r + 1, n_rad - 1))):
         idx = G[other, pl.ds(sz.meta + 1 + slot, 1), :].astype(I32)
         idx = jnp.where(exists, idx, -1)
-        got = pick(sz, state_of(other), idx)
+        got = pick(sz, state_of(sz, T, state, other), idx)
         for c in range(7):
             arr_rad[c, slot : slot + 1, :] = got[c][:, :width]
     sends[1].start()
+
+    rows = functools.partial(slab_rows, sz, n_rad, G)
+    size = rows(sz.size)
+    mass = size * size * size
+    dep = [-mass * (state[pl.ds((3 + c) * T, T), :] - rows(sz.motion + (3 + c) * tiles)) for c in range(3)] + [mass]
+    even = iota((T, BLOCK), 1) < GROUP
 
     for c in range(4):
         high = dep[c].astype(BF16).astype(F32)
@@ -344,21 +357,38 @@
     )
     gathered = lax.all_gather(packed, "rad", axis=0)
 
-    motion_out, arr_rad, gas_out, liquid, image, message = pl.pallas_call(
-        functools.partial(main_kernel, sz, n_rad),
+    state, message = pl.pallas_call(
+        functools.partial(move_kernel, sz, n_rad),
+        out_shape=[
+            jax.ShapeDtypeStruct((7 * T, BLOCK), F32),
+            jax.ShapeDtypeStruct((16, BLOCK), F32),
+        ],
+        in_specs=[vmem] * 2,
+        out_specs=[vmem] * 2,
+        scratch_shapes=[pltpu.VMEM((3, n_rad * sz.groups, BLOCK), F32)],
+        compiler_params=params,
+        name="move",
+    )(gathered, aux)
+
+    def exchange(first):
+        pairs = [(i, i + 1) for i in range(first, n_ax - 1, 2)]
+        return lax.ppermute(message, "ax", pairs + [(j, i) for i, j in pairs])
+
+    got_b = exchange(1)
+    got_a = exchange(0)
+
+    motion_out, arr_rad, gas_out, liquid, image = pl.pallas_call(
+        functools.partial(rest_kernel, sz, n_rad),
         out_shape=[
             jax.ShapeDtypeStruct((6, parcels), F32),
             jax.ShapeDtypeStruct((7, 2, cap_rad), F32),
             jax.ShapeDtypeStruct(gas_velocity.shape, F32),
             jax.ShapeDtypeStruct(pressure.shape, F32),
             jax.ShapeDtypeStruct(pressure.shape, F32),
-            jax.ShapeDtypeStruct((16, BLOCK), F32),
-        ],
-        in_specs=[vmem] * 3,
-        out_specs=[hbm] * 4 + [vmem] * 2,
+        ],
+        in_specs=[vmem] * 4,
+        out_specs=[hbm] * 4 + [vmem],
         scratch_shapes=[
-            pltpu.VMEM((3, n_rad * sz.groups, BLOCK), F32),
-            pltpu.VMEM((7 * T, BLOCK), F32),
             pltpu.VMEM((16 * T, BLOCK), F32),
             pltpu.VMEM((4 * 2 * T, BLOCK), F32),
             pltpu.VMEM((BLOCK, BLOCK), F32),
@@ -369,15 +399,9 @@
             pltpu.SemaphoreType.DMA((4,)),
         ],
         compiler_params=params,
-        name="slab",
-    )(gathered, aux, block_table)
-
-    def exchange(first):
-        pairs = [(i, i + 1) for i in range(first, n_ax - 1, 2)]
-        return lax.ppermute(message, "ax", pairs + [(j, i) for i, j in pairs])
-
-    got_b = exchange(1)
-    got_a = exchange(0)
+        cost_estimate=pl.CostEstimate(flops=2_000_000_000, bytes_accessed=2_000_000, transcendentals=0),
+        name="rest",
+    )(gathered, aux, block_table, state)
 
     arr_ax, pressure_image = pl.pallas_call(
         functools.partial(finish_kernel, sz),

time: 15.2 us -> 13.8 us (0.908)
  waiting for transfers between devices: 1.63 us -> 0.01 us
    ppermute x2, waiting for transfers between devices: 1.63 us -> 0.01 us  [exchange(): return lax.ppermute(message, 'ax', pairs + [(j, i) for i, j in pairs])]
    pallas_call x1 -> x2, Pallas kernels: 2.37 us -> 2.51 us  [the longest x1 2.07 us: on_device(): pl.pallas_call(functools.partial(rest_kernel, sz, n_rad), out_shape=[jax....]
  transfers between devices with their start and end apart: 2 -> 2, of which waited for: 1 -> 0; matrix products, arithmetic and copies ran while one was open for 0% -> 0% of each run, Pallas kernels for 0% -> 15%
where the time goes in v3:
time: 13.8 us; the launch traced here: 13.6 us
  starting transfers between devices  6.32 us (46%)
  Pallas kernels  4.32 us (31%)
  blocking collectives  2.31 us (17%)
  between operations  0.69 us (5%)
    ppermute x2, starting transfers between devices, exchange(): return lax.ppermute(message, 'ax', pairs + [(j, i) for i, j in pairs])  6.32 us
    all_gather x1, blocking collectives, on_device(): gathered = lax.all_gather(packed, 'rad', axis=0)  2.31 us
    pallas_call x1, Pallas kernels, on_device(): pl.pallas_call(functools.partial(rest_kernel, sz, n_rad), out_shape=[jax....  2.07 us
    pallas_call x1, Pallas kernels, on_device(): pl.pallas_call(functools.partial(pack_kernel, sz, n_rad), out_shape=[jax....  1.12 us
    pallas_call x1, Pallas kernels, on_device(): pl.pallas_call(functools.partial(finish_kernel, sz), out_shape=[jax.Shape...  0.69 us
    pallas_call x1, Pallas kernels, on_device(): pl.pallas_call(functools.partial(move_kernel, sz, n_rad), out_shape=[jax....  0.44 us
  transfers between devices with their start and end apart: 2, of which 0 were waited for; matrix products, arithmetic and copies ran while one was open for 0% of the time, Pallas kernels for 15%

profile of v3, /device:TPU:0, one launch (start us, length us, event | category | flops | bytes accessed | tf_op | source)
XLA Modules:
  0.0 13.6 jit_solution(4246984475540104274)
XLA Ops:
  0.6 1.1 %pack.1 = (f32[392,128]{1,0:T(8,128)S(1)}, s32[16,128]{1,0:T(8,128)S(1)}) custom-call(f32[6,2048]{1,0:T(8,128)} %motion_hbm.1, f32[16,128]{1,0:T(8,128)} %bitcast.21, s32[1,32]{1,0:T(1,128)} %bitcast.27, s32[16,128]{1,0:T(8,128)} %bitcast.22, f32[3,16,512]{2,1,0:T(8,128)} %gas_hbm.1, f32[16,512]{1,0:T(8,128)} %pres_hbm.1, s32[2,32]{1,0:T(2,128)} %bitcast.25, ...), custom_call_target="tpu_custom_call" | custom-call | tf_op jit(solution)/shard_map/pack/pallas_call | solution.py:324
  1.8 0.0 copy-start
  1.8 2.3 %all-gather = f32[784,128]{1,0:T(8,128)S(1)} all-gather(f32[392,128]{1,0:T(8,128)S(1)} %get-tuple-element.17), channel_id=2, replica_groups=mesh['ax'=16,'rad'=2] {'rad'}, dimensions={0}, use_global_device_ids=true | all-gather | bytes 602112 | tf_op jit(solution)/shard_map/all_gather | solution.py:358
  4.1 0.4 %move.1 = (f32[224,128]{1,0:T(8,128)S(1)}, f32[16,128]{1,0:T(8,128)S(1)}) custom-call(f32[2,392,128]{2,1,0:T(8,128)S(1)} %bitcast.19, s32[16,128]{1,0:T(8,128)S(1)} %get-tuple-element.18.aux), custom_call_target="tpu_custom_call" | custom-call | tf_op jit(solution)/shard_map/move/pallas_call | solution.py:360
  4.5 0.7 %collective-permute-start.1 = (f32[16,128]{1,0:T(8,128)S(1)}, f32[16,128]{1,0:T(8,128)S(1)}, u32[]{:S(2)}, u32[]{:S(2)}) collective-permute-start(f32[16,128]{1,0:T(8,128)S(1)} %get-tuple-element.21), channel_id=1, source_target_pairs={{2,4},{6,8},{10,12},{14,16},{18,20},{22,24},{26,28},{4,2},{8,6},{1... | collective-permute-start | bytes 24584 | tf_op jit(solution)/shard_map/ppermute | solution.py:375
  5.2 5.7 %collective-permute-start = (f32[16,128]{1,0:T(8,128)S(1)}, f32[16,128]{1,0:T(8,128)S(1)}, u32[]{:S(2)}, u32[]{:S(2)}) collective-permute-start(f32[16,128]{1,0:T(8,128)S(1)} %get-tuple-element.21), channel_id=1, source_target_pairs={{0,2},{4,6},{8,10},{12,14},{16,18},{20,22},{24,26},{28,30},{2,0},{... | collective-permute-start | bytes 24584 | tf_op jit(solution)/shard_map/ppermute | solution.py:375
  10.9 0.0 copy-done
  10.9 2.1 %rest.1 = (f32[6,2048]{1,0:T(8,128)}, f32[7,2,32]{2,1,0:T(2,128)}, f32[3,16,512]{2,1,0:T(8,128)}, f32[16,512]{1,0:T(8,128)}, f32[16,512]{1,0:T(8,128)S(1)}) custom-call(f32[2,392,128]{2,1,0:T(8,128)S(1)} %bitcast.20, s32[16,128]{1,0:T(8,128)S(1)} %get-tuple-element.18.aux, f32[8,128,128]{2,1,0:T(8,128)S(1)} %copy-done, f32[224,128]{1,0:T(8,128)S(1)} %get-tuple-element.19.state), custom_call_target="tpu_custom_call" | custom-call | flops 2000000000 | bytes 2000000 | tf_op jit(solution)/shard_map/rest/pallas_call | solution.py:380
  12.9 0.0 collective-permute-done.1.got_b
  12.9 0.0 collective-permute-done.got_a
  13.0 0.7 %finish.1 = (f32[7,2,64]{2,1,0:T(2,128)}, f32[16,512]{1,0:T(8,128)}) custom-call(f32[16,128]{1,0:T(8,128)S(1)} %collective-permute-done.got_a, f32[16,128]{1,0:T(8,128)S(1)} %collective-permute-done.1.got_b, f32[16,512]{1,0:T(8,128)S(1)} %get-tuple-element.22.image), custom_call_target="tpu_custom_call" | custom-call | tf_op jit(solution)/shard_map/finish/pallas_call | solution.py:406
Async XLA Ops:
  1.8 9.1 %copy-start = (f32[8,128,128]{2,1,0:T(8,128)S(1)}, f32[8,128,128]{2,1,0:T(8,128)}, u32[]{:S(2)}) copy-start(f32[8,128,128]{2,1,0:T(8,128)} %table.1) | copy-start | bytes 1572868
  4.5 8.4 %collective-permute-start.1 = (f32[16,128]{1,0:T(8,128)S(1)}, f32[16,128]{1,0:T(8,128)S(1)}, u32[]{:S(2)}, u32[]{:S(2)}) collective-permute-start(f32[16,128]{1,0:T(8,128)S(1)} %get-tuple-element.21), channel_id=1, source_target_pairs={{2,4},{6,8},{10,12},{14,16},{18,20},{22,24},{26,28},{4,2},{8,6},{1... | collective-permute-start | bytes 24584 | tf_op jit(solution)/shard_map/ppermute | solution.py:375
  5.2 7.8 %collective-permute-start = (f32[16,128]{1,0:T(8,128)S(1)}, f32[16,128]{1,0:T(8,128)S(1)}, u32[]{:S(2)}, u32[]{:S(2)}) collective-permute-start(f32[16,128]{1,0:T(8,128)S(1)} %get-tuple-element.21), channel_id=1, source_target_pairs={{0,2},{4,6},{8,10},{12,14},{16,18},{20,22},{24,26},{28,30},{2,0},{... | collective-permute-start | bytes 24584 | tf_op jit(solution)/shard_map/ppermute | solution.py:375

commit v4 on v3

--- a/solution.py
+++ b/solution.py
@@ -68,24 +68,27 @@
     motion, size, block, offset, gas, pres, radial, counts, cols, kinds, axial, sem,
 ):
     pairs = (
-        (counts_hbm, counts), (gas_hbm, gas), (motion_hbm, motion), (pres_hbm, pres), (size_hbm, size),
-        (offset_hbm, offset), (block_hbm, block), (radial_hbm, radial), (cols_hbm, cols), (kinds_hbm, kinds),
-        (axial_hbm, axial),
+        (motion_hbm, motion), (gas_hbm, gas), (pres_hbm, pres), (size_hbm, size), (offset_hbm, offset),
+        (block_hbm, block), (counts_hbm, counts), (radial_hbm, radial), (axial_hbm, axial), (cols_hbm, cols),
+        (kinds_hbm, kinds),
     )
     copies = [pltpu.make_async_copy(src, dst, sem.at[i]) for i, (src, dst) in enumerate(pairs)]
     for copy in copies:
         copy.start()
     out[pl.ds(sz.meta, 8), :] = jnp.full((8, BLOCK), -1.0, F32)
-    for copy in copies:
-        copy.wait()
     layers = sz.layers
+    copies[0].wait()
+    for i in range(sz.tiles):
+        out[pl.ds(sz.motion + i, 6, stride=sz.tiles), :] = motion[:, i * BLOCK : (i + 1) * BLOCK]
+    copies[1].wait()
     for c in range(3):
         for q in range(sz.quarters):
             out[pl.ds(sz.gas + c * sz.blocks + q * layers, layers), :] = gas[c, :, q * BLOCK : (q + 1) * BLOCK]
+    copies[2].wait()
     for q in range(sz.quarters):
         out[pl.ds(sz.pres + q * layers, layers), :] = pres[:, q * BLOCK : (q + 1) * BLOCK]
-    for i in range(sz.tiles):
-        out[pl.ds(sz.motion + i, 6, stride=sz.tiles), :] = motion[:, i * BLOCK : (i + 1) * BLOCK]
+    for copy in copies[3:]:
+        copy.wait()
     out[pl.ds(sz.size, sz.tiles), :] = size[...]
     out[pl.ds(sz.offset, sz.tiles), :] = offset[...].astype(F32)
     out[pl.ds(sz.meta, 1), pl.ds(0, sz.groups)] = block_row(sz, block[...]).astype(F32)
@@ -175,11 +178,13 @@
 
 
 def rest_kernel(
-    sz, n_rad, G, aux, table, state,
+    sz, n_rad, G, aux, table_hbm, state,
     motion_hbm, arr_hbm, gas_hbm, liquid_hbm, image,
-    deps, spread, coup, motion_out, arr_rad, gas_out, liquid, sem,
+    table, deps, spread, coup, motion_out, arr_rad, gas_out, liquid, sem,
 ):
     r = lax.axis_index("rad")
+    load = pltpu.make_async_copy(table_hbm, table, sem.at[4])
+    load.start()
     sends = [
         pltpu.make_async_copy(src, dst, sem.at[i])
         for i, (src, dst) in enumerate(
@@ -259,6 +264,7 @@
             count = count.astype(BF16)
             part = dot(p_high, count) + dot(p_low, count)
             grouped[j] = part if grouped[j] is None else grouped[j] + part
+    load.wait()
     sums = [None, None]
     for j in range(NT // 2):
         g_high, g_low = split2(grouped[j])
@@ -281,7 +287,7 @@
         send.wait()
 
 
-def finish_kernel(sz, got_a, got_b, image, arr_ax, pressure_image):
+def finish_kernel(sz, got_b, got_a, image, arr_ax, pressure_image):
     even = lax.axis_index("ax") % 2 == 0
     low = jnp.where(even, got_b[...], got_a[...])
     up = jnp.where(even, got_a[...], got_b[...])
@@ -374,8 +380,8 @@
         pairs = [(i, i + 1) for i in range(first, n_ax - 1, 2)]
         return lax.ppermute(message, "ax", pairs + [(j, i) for i, j in pairs])
 
+    got_a = exchange(0)
     got_b = exchange(1)
-    got_a = exchange(0)
 
     motion_out, arr_rad, gas_out, liquid, image = pl.pallas_call(
         functools.partial(rest_kernel, sz, n_rad),
@@ -386,9 +392,10 @@
             jax.ShapeDtypeStruct(pressure.shape, F32),
             jax.ShapeDtypeStruct(pressure.shape, F32),
         ],
-        in_specs=[vmem] * 4,
+        in_specs=[vmem, vmem, hbm, vmem],
         out_specs=[hbm] * 4 + [vmem],
         scratch_shapes=[
+            pltpu.VMEM(block_table.shape, F32),
             pltpu.VMEM((16 * T, BLOCK), F32),
             pltpu.VMEM((4 * 2 * T, BLOCK), F32),
             pltpu.VMEM((BLOCK, BLOCK), F32),
@@ -396,12 +403,12 @@
             pltpu.VMEM((7, 2, cap_rad), F32),
             pltpu.VMEM(gas_velocity.shape, F32),
             pltpu.VMEM(pressure.shape, F32),
-            pltpu.SemaphoreType.DMA((4,)),
+            pltpu.SemaphoreType.DMA((5,)),
         ],
         compiler_params=params,
         cost_estimate=pl.CostEstimate(flops=2_000_000_000, bytes_accessed=2_000_000, transcendentals=0),
         name="rest",
-    )(gathered, aux, block_table, state)
+    )(gathered, aux, pltpu.with_memory_space_constraint(block_table, pltpu.HBM), state)
 
     arr_ax, pressure_image = pl.pallas_call(
         functools.partial(finish_kernel, sz),
@@ -413,7 +420,7 @@
         out_specs=[vmem] * 2,
         compiler_params=params,
         name="finish",
-    )(got_a, got_b, image)
+    )(got_b, got_a, image)
 
     arrivals_axial = arr_ax.transpose(1, 0, 2)[None, None]
     arrivals_radial = arr_rad.transpose(1, 0, 2)[None, None]

time: 13.8 us -> 14.1 us (1.022)
  the two profiles are of different devices: /device:TPU:0 before, /device:TPU:8 now
where the time goes in v4:
time: 14.1 us; the launch traced here: 13.9 us
  starting transfers between devices  4.83 us (34%)
  Pallas kernels  4.7 us (33%)
  blocking collectives  2.09 us (15%)
  waiting for transfers between devices  1.61 us (11%)
  between operations  0.68 us (5%)
    ppermute x2, starting transfers between devices, exchange(): return lax.ppermute(message, 'ax', pairs + [(j, i) for i, j in pairs])  4.83 us
    pallas_call x1, Pallas kernels, on_device(): pl.pallas_call(functools.partial(rest_kernel, sz, n_rad), out_shape=[jax....  2.43 us
    all_gather x1, blocking collectives, on_device(): gathered = lax.all_gather(packed, 'rad', axis=0)  2.09 us
    ppermute x2, waiting for transfers between devices, exchange(): return lax.ppermute(message, 'ax', pairs + [(j, i) for i, j in pairs])  1.61 us
    pallas_call x1, Pallas kernels, on_device(): pl.pallas_call(functools.partial(pack_kernel, sz, n_rad), out_shape=[jax....  1.15 us
    pallas_call x1, Pallas kernels, on_device(): pl.pallas_call(functools.partial(finish_kernel, sz), out_shape=[jax.Shape...  0.68 us
    pallas_call x1, Pallas kernels, on_device(): pl.pallas_call(functools.partial(move_kernel, sz, n_rad), out_shape=[jax....  0.44 us
  transfers between devices with their start and end apart: 2, of which 1 were waited for; matrix products, arithmetic and copies ran while one was open for 0% of the time, Pallas kernels for 17%

profile of v4, /device:TPU:8, one launch (start us, length us, event | category | flops | bytes accessed | tf_op | source)
XLA Modules:
  0.0 13.9 jit_solution(5107515617753573839)
XLA Ops:
  0.6 1.1 %pack.1 = (f32[392,128]{1,0:T(8,128)S(1)}, s32[16,128]{1,0:T(8,128)S(1)}) custom-call(f32[6,2048]{1,0:T(8,128)} %motion_hbm.1, f32[16,128]{1,0:T(8,128)} %bitcast.21, s32[1,32]{1,0:T(1,128)} %bitcast.27, s32[16,128]{1,0:T(8,128)} %bitcast.22, f32[3,16,512]{2,1,0:T(8,128)} %gas_hbm.1, f32[16,512]{1,0:T(8,128)} %pres_hbm.1, s32[2,32]{1,0:T(2,128)} %bitcast.25, ...), custom_call_target="tpu_custom_call" | custom-call | tf_op jit(solution)/shard_map/pack/pallas_call | solution.py:330
  1.8 2.1 %all-gather = f32[784,128]{1,0:T(8,128)S(1)} all-gather(f32[392,128]{1,0:T(8,128)S(1)} %get-tuple-element.17), channel_id=2, replica_groups=mesh['ax'=16,'rad'=2] {'rad'}, dimensions={0}, use_global_device_ids=true | all-gather | bytes 602112 | tf_op jit(solution)/shard_map/all_gather | solution.py:364
  3.9 0.4 %move.1 = (f32[224,128]{1,0:T(8,128)S(1)}, f32[16,128]{1,0:T(8,128)S(1)}) custom-call(f32[2,392,128]{2,1,0:T(8,128)S(1)} %bitcast.19, s32[16,128]{1,0:T(8,128)S(1)} %get-tuple-element.18.aux), custom_call_target="tpu_custom_call" | custom-call | tf_op jit(solution)/shard_map/move/pallas_call | solution.py:366
  4.3 1.6 %collective-permute-start.1 = (f32[16,128]{1,0:T(8,128)S(1)}, f32[16,128]{1,0:T(8,128)S(1)}, u32[]{:S(2)}, u32[]{:S(2)}) collective-permute-start(f32[16,128]{1,0:T(8,128)S(1)} %get-tuple-element.21), channel_id=1, source_target_pairs={{0,2},{4,6},{8,10},{12,14},{16,18},{20,22},{24,26},{28,30},{2,0},{... | collective-permute-start | bytes 24584 | tf_op jit(solution)/shard_map/ppermute | solution.py:381
  5.9 3.3 %collective-permute-start = (f32[16,128]{1,0:T(8,128)S(1)}, f32[16,128]{1,0:T(8,128)S(1)}, u32[]{:S(2)}, u32[]{:S(2)}) collective-permute-start(f32[16,128]{1,0:T(8,128)S(1)} %get-tuple-element.21), channel_id=1, source_target_pairs={{2,4},{6,8},{10,12},{14,16},{18,20},{22,24},{26,28},{4,2},{8,6},{1... | collective-permute-start | bytes 24584 | tf_op jit(solution)/shard_map/ppermute | solution.py:381
  9.2 2.4 %rest.1 = (f32[6,2048]{1,0:T(8,128)}, f32[7,2,32]{2,1,0:T(2,128)}, f32[3,16,512]{2,1,0:T(8,128)}, f32[16,512]{1,0:T(8,128)}, f32[16,512]{1,0:T(8,128)S(1)}) custom-call(f32[2,392,128]{2,1,0:T(8,128)S(1)} %bitcast.20, s32[16,128]{1,0:T(8,128)S(1)} %get-tuple-element.18.aux, f32[8,128,128]{2,1,0:T(8,128)} %table_hbm.1, f32[224,128]{1,0:T(8,128)S(1)} %get-tuple-element.19.state), custom_call_target="tpu_custom_call" | custom-call | flops 2000000000 | bytes 2000000 | tf_op jit(solution)/shard_map/rest/pallas_call | solution.py:386
  11.6 0.0 collective-permute-done.1.got_a
  11.6 1.6 %collective-permute-done.got_b = f32[16,128]{1,0:T(8,128)S(1)} collective-permute-done((f32[16,128]{1,0:T(8,128)S(1)}, f32[16,128]{1,0:T(8,128)S(1)}, u32[]{:S(2)}, u32[]{:S(2)}) %collective-permute-start) | collective-permute-done | bytes 8224 | tf_op jit(solution)/shard_map/ppermute | solution.py:381
  13.2 0.7 %finish.1 = (f32[7,2,64]{2,1,0:T(2,128)}, f32[16,512]{1,0:T(8,128)}) custom-call(f32[16,128]{1,0:T(8,128)S(1)} %collective-permute-done.got_b, f32[16,128]{1,0:T(8,128)S(1)} %collective-permute-done.1.got_a, f32[16,512]{1,0:T(8,128)S(1)} %get-tuple-element.22.image), custom_call_target="tpu_custom_call" | custom-call | tf_op jit(solution)/shard_map/finish/pallas_call | solution.py:413
Async XLA Ops:
  4.3 7.3 %collective-permute-start.1 = (f32[16,128]{1,0:T(8,128)S(1)}, f32[16,128]{1,0:T(8,128)S(1)}, u32[]{:S(2)}, u32[]{:S(2)}) collective-permute-start(f32[16,128]{1,0:T(8,128)S(1)} %get-tuple-element.21), channel_id=1, source_target_pairs={{0,2},{4,6},{8,10},{12,14},{16,18},{20,22},{24,26},{28,30},{2,0},{... | collective-permute-start | bytes 24584 | tf_op jit(solution)/shard_map/ppermute | solution.py:381
  5.9 7.3 %collective-permute-start = (f32[16,128]{1,0:T(8,128)S(1)}, f32[16,128]{1,0:T(8,128)S(1)}, u32[]{:S(2)}, u32[]{:S(2)}) collective-permute-start(f32[16,128]{1,0:T(8,128)S(1)} %get-tuple-element.21), channel_id=1, source_target_pairs={{2,4},{6,8},{10,12},{14,16},{18,20},{22,24},{26,28},{4,2},{8,6},{1... | collective-permute-start | bytes 24584 | tf_op jit(solution)/shard_map/ppermute | solution.py:381

commit v5 on v3

--- a/solution.py
+++ b/solution.py
@@ -63,29 +63,32 @@
 
 def pack_kernel(
     sz, n_rad, motion_hbm, size_hbm, block_hbm, offset_hbm, gas_hbm, pres_hbm, radial_hbm, counts_hbm, cols_hbm,
-    kinds_hbm, axial_hbm,
-    out, aux,
+    kinds_hbm, axial_hbm, table_hbm,
+    out, aux, table,
     motion, size, block, offset, gas, pres, radial, counts, cols, kinds, axial, sem,
 ):
     pairs = (
-        (counts_hbm, counts), (gas_hbm, gas), (motion_hbm, motion), (pres_hbm, pres), (size_hbm, size),
-        (offset_hbm, offset), (block_hbm, block), (radial_hbm, radial), (cols_hbm, cols), (kinds_hbm, kinds),
-        (axial_hbm, axial),
+        (motion_hbm, motion), (gas_hbm, gas), (pres_hbm, pres), (size_hbm, size), (offset_hbm, offset),
+        (block_hbm, block), (counts_hbm, counts), (radial_hbm, radial), (axial_hbm, axial), (cols_hbm, cols),
+        (kinds_hbm, kinds), (table_hbm, table),
     )
     copies = [pltpu.make_async_copy(src, dst, sem.at[i]) for i, (src, dst) in enumerate(pairs)]
     for copy in copies:
         copy.start()
     out[pl.ds(sz.meta, 8), :] = jnp.full((8, BLOCK), -1.0, F32)
-    for copy in copies:
-        copy.wait()
     layers = sz.layers
+    copies[0].wait()
+    for i in range(sz.tiles):
+        out[pl.ds(sz.motion + i, 6, stride=sz.tiles), :] = motion[:, i * BLOCK : (i + 1) * BLOCK]
+    copies[1].wait()
     for c in range(3):
         for q in range(sz.quarters):
             out[pl.ds(sz.gas + c * sz.blocks + q * layers, layers), :] = gas[c, :, q * BLOCK : (q + 1) * BLOCK]
+    copies[2].wait()
     for q in range(sz.quarters):
         out[pl.ds(sz.pres + q * layers, layers), :] = pres[:, q * BLOCK : (q + 1) * BLOCK]
-    for i in range(sz.tiles):
-        out[pl.ds(sz.motion + i, 6, stride=sz.tiles), :] = motion[:, i * BLOCK : (i + 1) * BLOCK]
+    for copy in copies[3:11]:
+        copy.wait()
     out[pl.ds(sz.size, sz.tiles), :] = size[...]
     out[pl.ds(sz.offset, sz.tiles), :] = offset[...].astype(F32)
     out[pl.ds(sz.meta, 1), pl.ds(0, sz.groups)] = block_row(sz, block[...]).astype(F32)
@@ -100,6 +103,7 @@
     lane = iota((1, axial.shape[1]), 1)
     kept = [jnp.where(lane < counts[0, slot], axial[slot : slot + 1, :], -1) for slot in range(2)]
     aux[pl.ds(8, 1), :] = jnp.concatenate(kept, axis=1)
+    copies[11].wait()
 
 
 def take_lanes(x, idx):
@@ -281,10 +285,11 @@
         send.wait()
 
 
-def finish_kernel(sz, got_a, got_b, image, arr_ax, pressure_image):
-    even = lax.axis_index("ax") % 2 == 0
-    low = jnp.where(even, got_b[...], got_a[...])
-    up = jnp.where(even, got_a[...], got_b[...])
+def finish_kernel(sz, n_ax, got_a, got_b, image, arr_ax, pressure_image):
+    a = lax.axis_index("ax")
+    even = a % 2 == 0
+    low = jnp.where(a > 0, jnp.where(even, got_b[...], got_a[...]), 0.0)
+    up = jnp.where(a < n_ax - 1, jnp.where(even, got_a[...], got_b[...]), 0.0)
     half = arr_ax.shape[2]
     arr_ax[:, 0, :] = low[0:7, 0:half]
     arr_ax[:, 1, :] = up[0:7, half : 2 * half]
@@ -321,14 +326,15 @@
     size2 = parcel_size.reshape(sz.tiles, BLOCK)
     offset2 = parcel_offset.reshape(sz.tiles, BLOCK)
 
-    packed, aux = pl.pallas_call(
+    packed, aux, table = pl.pallas_call(
         functools.partial(pack_kernel, sz, n_rad),
         out_shape=[
             jax.ShapeDtypeStruct((sz.rows, BLOCK), F32),
             jax.ShapeDtypeStruct((16, BLOCK), I32),
-        ],
-        in_specs=[hbm] * 11,
-        out_specs=[vmem] * 2,
+            jax.ShapeDtypeStruct(block_table.shape, F32),
+        ],
+        in_specs=[hbm] * 12,
+        out_specs=[vmem] * 3,
         scratch_shapes=[
             pltpu.VMEM(parcel_motion.shape, F32),
             pltpu.VMEM(size2.shape, F32),
@@ -341,7 +347,7 @@
             pltpu.VMEM((4, sz.blocks), I32),
             pltpu.VMEM((4, sz.blocks), I32),
             pltpu.VMEM((2, cap_ax), I32),
-            pltpu.SemaphoreType.DMA((11,)),
+            pltpu.SemaphoreType.DMA((12,)),
         ],
         compiler_params=params,
         name="pack",
@@ -351,7 +357,7 @@
             for x in (
                 parcel_motion, size2, parcel_block.reshape(1, sz.groups), offset2, gas_velocity, pressure,
                 send_radial.reshape(2, cap_rad), counts, block_cols[0].T, block_kinds[0].T,
-                send_axial.reshape(2, cap_ax),
+                send_axial.reshape(2, cap_ax), block_table,
             )
         )
     )
@@ -371,8 +377,15 @@
     )(gathered, aux)
 
     def exchange(first):
-        pairs = [(i, i + 1) for i in range(first, n_ax - 1, 2)]
-        return lax.ppermute(message, "ax", pairs + [(j, i) for i, j in pairs])
+        to = list(range(n_ax * n_rad))
+        for low in range(first, n_ax - 1, 2):
+            for r in range(n_rad):
+                i, j = low * n_rad + r, (low + 1) * n_rad + r
+                to[i], to[j] = j, i
+        alone = [i for i in range(n_ax * n_rad) if to[i] == i]
+        for i, j in zip(alone[0::2], alone[1::2]):
+            to[i], to[j] = j, i
+        return lax.ppermute(message, ("ax", "rad"), list(enumerate(to)))
 
     got_b = exchange(1)
     got_a = exchange(0)
@@ -401,10 +414,10 @@
         compiler_params=params,
         cost_estimate=pl.CostEstimate(flops=2_000_000_000, bytes_accessed=2_000_000, transcendentals=0),
         name="rest",
-    )(gathered, aux, block_table, state)
+    )(gathered, aux, table, state)
 
     arr_ax, pressure_image = pl.pallas_call(
-        functools.partial(finish_kernel, sz),
+        functools.partial(finish_kernel, sz, n_ax),
         out_shape=[
             jax.ShapeDtypeStruct((7, 2, cap_ax), F32),
             jax.ShapeDtypeStruct(pressure.shape, F32),

time: 13.8 us -> 12 us (0.87)
  starting transfers between devices: 6.32 us -> 4.41 us
  Pallas kernels: 4.32 us -> 4.55 us
  blocking collectives: 2.31 us -> 2.17 us
    ppermute x2, starting transfers between devices: 6.32 us -> 4.41 us  [exchange(): return lax.ppermute(message, ('ax', 'rad'), list(enumerate(to)))]
    pallas_call x1, Pallas kernels: 1.12 us -> 1.35 us  [on_device(): pl.pallas_call(functools.partial(pack_kernel, sz, n_rad), out_shape=[jax....]
  transfers between devices with their start and end apart: 2 -> 2, of which waited for: 0 -> 0; matrix products, arithmetic and copies ran while one was open for 0% -> 0% of each run, Pallas kernels for 15% -> 18%
where the time goes in v5:
time: 12 us; the launch traced here: 11.8 us
  Pallas kernels  4.55 us (38%)
  starting transfers between devices  4.41 us (37%)
  blocking collectives  2.17 us (18%)
  between operations  0.68 us (6%)
    ppermute x2, starting transfers between devices, exchange(): return lax.ppermute(message, ('ax', 'rad'), list(enumerate(to)))  4.41 us
    all_gather x1, blocking collectives, on_device(): gathered = lax.all_gather(packed, 'rad', axis=0)  2.17 us
    pallas_call x1, Pallas kernels, on_device(): pl.pallas_call(functools.partial(rest_kernel, sz, n_rad), out_shape=[jax....  2.08 us
    pallas_call x1, Pallas kernels, on_device(): pl.pallas_call(functools.partial(pack_kernel, sz, n_rad), out_shape=[jax....  1.35 us
    pallas_call x1, Pallas kernels, on_device(): pl.pallas_call(functools.partial(finish_kernel, sz, n_ax), out_shape=[jax...  0.69 us
    pallas_call x1, Pallas kernels, on_device(): pl.pallas_call(functools.partial(move_kernel, sz, n_rad), out_shape=[jax....  0.44 us
  transfers between devices with their start and end apart: 2, of which 0 were waited for; matrix products, arithmetic and copies ran while one was open for 0% of the time, Pallas kernels for 18%

profile of v5, /device:TPU:0, one launch (start us, length us, event | category | flops | bytes accessed | tf_op | source)
XLA Modules:
  0.0 11.8 jit_solution(13231261563260977008)
XLA Ops:
  0.6 1.3 %pack.1 = (f32[392,128]{1,0:T(8,128)S(1)}, s32[16,128]{1,0:T(8,128)S(1)}, f32[8,128,128]{2,1,0:T(8,128)S(1)}) custom-call(f32[6,2048]{1,0:T(8,128)} %motion_hbm.1, f32[16,128]{1,0:T(8,128)} %bitcast.21, s32[1,32]{1,0:T(1,128)} %bitcast.27, s32[16,128]{1,0:T(8,128)} %bitcast.22, f32[3,16,512]{2,1,0:T(8,128)} %gas_hbm.1, f32[16,512]{1,0:T(8,128)} %pres_hbm.1, ...), custom_call_target="tpu_custom_call" | custom-call | tf_op jit(solution)/shard_map/pack/pallas_call | solution.py:329
  2.0 2.2 %all-gather = f32[784,128]{1,0:T(8,128)S(1)} all-gather(f32[392,128]{1,0:T(8,128)S(1)} %get-tuple-element.18), channel_id=2, replica_groups=mesh['ax'=16,'rad'=2] {'rad'}, dimensions={0}, use_global_device_ids=true | all-gather | bytes 602112 | tf_op jit(solution)/shard_map/all_gather | solution.py:364
  4.2 0.4 %move.1 = (f32[224,128]{1,0:T(8,128)S(1)}, f32[16,128]{1,0:T(8,128)S(1)}) custom-call(f32[2,392,128]{2,1,0:T(8,128)S(1)} %bitcast.19, s32[16,128]{1,0:T(8,128)S(1)} %get-tuple-element.19.aux), custom_call_target="tpu_custom_call" | custom-call | tf_op jit(solution)/shard_map/move/pallas_call | solution.py:366
  4.6 0.4 %collective-permute-start.1 = (f32[16,128]{1,0:T(8,128)S(1)}, f32[16,128]{1,0:T(8,128)S(1)}, u32[]{:S(2)}, u32[]{:S(2)}) collective-permute-start(f32[16,128]{1,0:T(8,128)S(1)} %get-tuple-element.23), channel_id=1, source_target_pairs={{0,1},{1,0},{2,4},{3,5},{4,2},{5,3},{6,8},{7,9},{8,6},{9,7},{10,12... | collective-permute-start | bytes 24584 | tf_op jit(solution)/shard_map/ppermute | solution.py:388
  5.0 4.0 %collective-permute-start = (f32[16,128]{1,0:T(8,128)S(1)}, f32[16,128]{1,0:T(8,128)S(1)}, u32[]{:S(2)}, u32[]{:S(2)}) collective-permute-start(f32[16,128]{1,0:T(8,128)S(1)} %get-tuple-element.23), channel_id=1, source_target_pairs={{0,2},{1,3},{2,0},{3,1},{4,6},{5,7},{6,4},{7,5},{8,10},{9,11},{10,... | collective-permute-start | bytes 24584 | tf_op jit(solution)/shard_map/ppermute | solution.py:388
  9.0 2.1 %rest.1 = (f32[6,2048]{1,0:T(8,128)}, f32[7,2,32]{2,1,0:T(2,128)}, f32[3,16,512]{2,1,0:T(8,128)}, f32[16,512]{1,0:T(8,128)}, f32[16,512]{1,0:T(8,128)S(1)}) custom-call(f32[2,392,128]{2,1,0:T(8,128)S(1)} %bitcast.20, s32[16,128]{1,0:T(8,128)S(1)} %get-tuple-element.19.aux, f32[8,128,128]{2,1,0:T(8,128)S(1)} %get-tuple-element.20.table, ...), custom_call_target="tpu_custom_call" | custom-call | flops 2000000000 | bytes 2000000 | tf_op jit(solution)/shard_map/rest/pallas_call | solution.py:393
  11.1 0.0 collective-permute-done.1.got_b
  11.1 0.0 collective-permute-done.got_a
  11.1 0.7 %finish.1 = (f32[7,2,64]{2,1,0:T(2,128)}, f32[16,512]{1,0:T(8,128)}) custom-call(f32[16,128]{1,0:T(8,128)S(1)} %collective-permute-done.got_a, f32[16,128]{1,0:T(8,128)S(1)} %collective-permute-done.1.got_b, f32[16,512]{1,0:T(8,128)S(1)} %get-tuple-element.24.image), custom_call_target="tpu_custom_call" | custom-call | tf_op jit(solution)/shard_map/finish/pallas_call | solution.py:419
Async XLA Ops:
  4.6 6.5 %collective-permute-start.1 = (f32[16,128]{1,0:T(8,128)S(1)}, f32[16,128]{1,0:T(8,128)S(1)}, u32[]{:S(2)}, u32[]{:S(2)}) collective-permute-start(f32[16,128]{1,0:T(8,128)S(1)} %get-tuple-element.23), channel_id=1, source_target_pairs={{0,1},{1,0},{2,4},{3,5},{4,2},{5,3},{6,8},{7,9},{8,6},{9,7},{10,12... | collective-permute-start | bytes 24584 | tf_op jit(solution)/shard_map/ppermute | solution.py:388
  5.0 6.1 %collective-permute-start = (f32[16,128]{1,0:T(8,128)S(1)}, f32[16,128]{1,0:T(8,128)S(1)}, u32[]{:S(2)}, u32[]{:S(2)}) collective-permute-start(f32[16,128]{1,0:T(8,128)S(1)} %get-tuple-element.23), channel_id=1, source_target_pairs={{0,2},{1,3},{2,0},{3,1},{4,6},{5,7},{6,4},{7,5},{8,10},{9,11},{10,... | collective-permute-start | bytes 24584 | tf_op jit(solution)/shard_map/ppermute | solution.py:388

commit v6 on v5

--- a/solution.py
+++ b/solution.py
@@ -67,27 +67,32 @@
     out, aux, table,
     motion, size, block, offset, gas, pres, radial, counts, cols, kinds, axial, sem,
 ):
-    pairs = (
-        (motion_hbm, motion), (gas_hbm, gas), (pres_hbm, pres), (size_hbm, size), (offset_hbm, offset),
-        (block_hbm, block), (counts_hbm, counts), (radial_hbm, radial), (axial_hbm, axial), (cols_hbm, cols),
-        (kinds_hbm, kinds), (table_hbm, table),
-    )
-    copies = [pltpu.make_async_copy(src, dst, sem.at[i]) for i, (src, dst) in enumerate(pairs)]
+    half = motion.shape[1] // 2
+    big = [(motion_hbm.at[:, pl.ds(i * half, half)], motion.at[:, pl.ds(i * half, half)]) for i in range(2)]
+    big += [(gas_hbm.at[c], gas.at[c]) for c in range(3)]
+    rest = [
+        (pres_hbm, pres), (size_hbm, size), (offset_hbm, offset), (block_hbm, block), (counts_hbm, counts),
+        (radial_hbm, radial), (axial_hbm, axial), (cols_hbm, cols), (kinds_hbm, kinds),
+    ]
+    late = [(table_hbm.at[t], table.at[t]) for t in range(table.shape[0])]
+    copies = [pltpu.make_async_copy(src, dst, sem.at[i]) for i, (src, dst) in enumerate(big + rest + late)]
     for copy in copies:
         copy.start()
     out[pl.ds(sz.meta, 8), :] = jnp.full((8, BLOCK), -1.0, F32)
     layers = sz.layers
     copies[0].wait()
+    copies[1].wait()
     for i in range(sz.tiles):
         out[pl.ds(sz.motion + i, 6, stride=sz.tiles), :] = motion[:, i * BLOCK : (i + 1) * BLOCK]
-    copies[1].wait()
+    for copy in copies[2:5]:
+        copy.wait()
     for c in range(3):
         for q in range(sz.quarters):
             out[pl.ds(sz.gas + c * sz.blocks + q * layers, layers), :] = gas[c, :, q * BLOCK : (q + 1) * BLOCK]
-    copies[2].wait()
+    copies[5].wait()
     for q in range(sz.quarters):
         out[pl.ds(sz.pres + q * layers, layers), :] = pres[:, q * BLOCK : (q + 1) * BLOCK]
-    for copy in copies[3:11]:
+    for copy in copies[6 : len(big + rest)]:
         copy.wait()
     out[pl.ds(sz.size, sz.tiles), :] = size[...]
     out[pl.ds(sz.offset, sz.tiles), :] = offset[...].astype(F32)
@@ -103,7 +108,8 @@
     lane = iota((1, axial.shape[1]), 1)
     kept = [jnp.where(lane < counts[0, slot], axial[slot : slot + 1, :], -1) for slot in range(2)]
     aux[pl.ds(8, 1), :] = jnp.concatenate(kept, axis=1)
-    copies[11].wait()
+    for copy in copies[len(big + rest) :]:
+        copy.wait()
 
 
 def take_lanes(x, idx):
@@ -221,12 +227,13 @@
         for piece, part in enumerate((high, low)):
             deps[pl.ds((piece * 8 + c) * T, T), :] = jnp.where(even, part, 0.0)
             deps[pl.ds((piece * 8 + 4 + c) * T, T), :] = jnp.where(even, 0.0, part)
-    cell = iota((BLOCK, BLOCK), 0)
+    cell = iota((BLOCK, BLOCK), 0).astype(F32).astype(BF16)
+    one, none = jnp.ones((BLOCK, BLOCK), BF16), jnp.zeros((BLOCK, BLOCK), BF16)
     for d in range(n_rad):
         for i in range(tiles):
             t = d * tiles + i
-            off = G[d, pl.ds(sz.offset + i, 1), :].astype(I32)
-            onehot = (cell == off).astype(F32).astype(BF16)
+            off = jnp.broadcast_to(G[d, pl.ds(sz.offset + i, 1), :], (16, BLOCK)).astype(BF16)
+            onehot = jnp.where(cell == jnp.concatenate([off] * (BLOCK // 16), axis=0), one, none)
             lhs = deps[pl.ds(t, 16, stride=T), :].astype(BF16)
             res = dot_nt(lhs, onehot)
             res = res[:8] + res[8:]
@@ -250,17 +257,16 @@
     sends[3].start()
 
     pres = jnp.concatenate([G[d, pl.ds(sz.pres, blocks), :] for d in range(n_rad)], axis=0)
-    index = aux[pl.ds(0, 4), :]
+    index = [jnp.broadcast_to(aux[pl.ds(k, 1), :], (BLOCK, BLOCK)).astype(jnp.int16) for k in range(4)]
     grouped = [None] * (NT // 2)
     for first in range(0, slab_blocks, BLOCK):
         p_high, p_low = split2(jnp.transpose(pres[first : first + BLOCK]))
         here = iota((BLOCK, BLOCK), 0) + first + jnp.where(iota((BLOCK, BLOCK), 1) < blocks, 0, slab_blocks)
         for j in range(NT // 2):
-            aim = here + 2 * j * slab_blocks
-            count = (aim == index[0:1]).astype(F32)
-            for k in range(1, index.shape[0]):
-                count = count + (aim == index[k : k + 1]).astype(F32)
-            count = count.astype(BF16)
+            aim = (here + 2 * j * slab_blocks).astype(jnp.int16)
+            count = none
+            for k in range(4):
+                count = count + jnp.where(aim == index[k], one, none)
             part = dot(p_high, count) + dot(p_low, count)
             grouped[j] = part if grouped[j] is None else grouped[j] + part
     sums = [None, None]
@@ -347,7 +353,7 @@
             pltpu.VMEM((4, sz.blocks), I32),
             pltpu.VMEM((4, sz.blocks), I32),
             pltpu.VMEM((2, cap_ax), I32),
-            pltpu.SemaphoreType.DMA((12,)),
+            pltpu.SemaphoreType.DMA((14 + NT,)),
         ],
         compiler_params=params,
         name="pack",

time: 12 us -> 12.1 us (level)
  transfers between devices with their start and end apart: 2 -> 2, of which waited for: 0 -> 0; matrix products, arithmetic and copies ran while one was open for 0% -> 0% of each run, Pallas kernels for 18% -> 17%
where the time goes in v6:
time: 12.1 us; the launch traced here: 11.9 us
  Pallas kernels  4.61 us (38%)
  starting transfers between devices  4.41 us (36%)
  blocking collectives  2.17 us (18%)
  between operations  0.68 us (6%)
    ppermute x2, starting transfers between devices, exchange(): return lax.ppermute(message, ('ax', 'rad'), list(enumerate(to)))  4.41 us
    all_gather x1, blocking collectives, on_device(): gathered = lax.all_gather(packed, 'rad', axis=0)  2.17 us
    pallas_call x1, Pallas kernels, on_device(): pl.pallas_call(functools.partial(rest_kernel, sz, n_rad), out_shape=[jax....  2.08 us
    pallas_call x1, Pallas kernels, on_device(): pl.pallas_call(functools.partial(pack_kernel, sz, n_rad), out_shape=[jax....  1.4 us
    pallas_call x1, Pallas kernels, on_device(): pl.pallas_call(functools.partial(finish_kernel, sz, n_ax), out_shape=[jax...  0.69 us
    pallas_call x1, Pallas kernels, on_device(): pl.pallas_call(functools.partial(move_kernel, sz, n_rad), out_shape=[jax....  0.44 us
  transfers between devices with their start and end apart: 2, of which 0 were waited for; matrix products, arithmetic and copies ran while one was open for 0% of the time, Pallas kernels for 17%

profile of v6, /device:TPU:0, one launch (start us, length us, event | category | flops | bytes accessed | tf_op | source)
XLA Modules:
  0.0 11.9 jit_solution(375588031684825341)
XLA Ops:
  0.6 1.4 %pack.1 = (f32[392,128]{1,0:T(8,128)S(1)}, s32[16,128]{1,0:T(8,128)S(1)}, f32[8,128,128]{2,1,0:T(8,128)S(1)}) custom-call(f32[6,2048]{1,0:T(8,128)} %motion_hbm.1, f32[16,128]{1,0:T(8,128)} %bitcast.21, s32[1,32]{1,0:T(1,128)} %bitcast.27, s32[16,128]{1,0:T(8,128)} %bitcast.22, f32[3,16,512]{2,1,0:T(8,128)} %gas_hbm.1, f32[16,512]{1,0:T(8,128)} %pres_hbm.1, ...), custom_call_target="tpu_custom_call" | custom-call | tf_op jit(solution)/shard_map/pack/pallas_call | solution.py:335
  2.0 2.2 %all-gather = f32[784,128]{1,0:T(8,128)S(1)} all-gather(f32[392,128]{1,0:T(8,128)S(1)} %get-tuple-element.18), channel_id=2, replica_groups=mesh['ax'=16,'rad'=2] {'rad'}, dimensions={0}, use_global_device_ids=true | all-gather | bytes 602112 | tf_op jit(solution)/shard_map/all_gather | solution.py:370
  4.2 0.4 %move.1 = (f32[224,128]{1,0:T(8,128)S(1)}, f32[16,128]{1,0:T(8,128)S(1)}) custom-call(f32[2,392,128]{2,1,0:T(8,128)S(1)} %bitcast.19, s32[16,128]{1,0:T(8,128)S(1)} %get-tuple-element.19.aux), custom_call_target="tpu_custom_call" | custom-call | tf_op jit(solution)/shard_map/move/pallas_call | solution.py:372
  4.7 0.4 %collective-permute-start.1 = (f32[16,128]{1,0:T(8,128)S(1)}, f32[16,128]{1,0:T(8,128)S(1)}, u32[]{:S(2)}, u32[]{:S(2)}) collective-permute-start(f32[16,128]{1,0:T(8,128)S(1)} %get-tuple-element.23), channel_id=1, source_target_pairs={{0,1},{1,0},{2,4},{3,5},{4,2},{5,3},{6,8},{7,9},{8,6},{9,7},{10,12... | collective-permute-start | bytes 24584 | tf_op jit(solution)/shard_map/ppermute | solution.py:394
  5.1 4.0 %collective-permute-start = (f32[16,128]{1,0:T(8,128)S(1)}, f32[16,128]{1,0:T(8,128)S(1)}, u32[]{:S(2)}, u32[]{:S(2)}) collective-permute-start(f32[16,128]{1,0:T(8,128)S(1)} %get-tuple-element.23), channel_id=1, source_target_pairs={{0,2},{1,3},{2,0},{3,1},{4,6},{5,7},{6,4},{7,5},{8,10},{9,11},{10,... | collective-permute-start | bytes 24584 | tf_op jit(solution)/shard_map/ppermute | solution.py:394
  9.1 2.1 %rest.1 = (f32[6,2048]{1,0:T(8,128)}, f32[7,2,32]{2,1,0:T(2,128)}, f32[3,16,512]{2,1,0:T(8,128)}, f32[16,512]{1,0:T(8,128)}, f32[16,512]{1,0:T(8,128)S(1)}) custom-call(f32[2,392,128]{2,1,0:T(8,128)S(1)} %bitcast.20, s32[16,128]{1,0:T(8,128)S(1)} %get-tuple-element.19.aux, f32[8,128,128]{2,1,0:T(8,128)S(1)} %get-tuple-element.20.table, ...), custom_call_target="tpu_custom_call" | custom-call | flops 2000000000 | bytes 2000000 | tf_op jit(solution)/shard_map/rest/pallas_call | solution.py:399
  11.2 0.0 collective-permute-done.1.got_b
  11.2 0.0 collective-permute-done.got_a
  11.2 0.7 %finish.1 = (f32[7,2,64]{2,1,0:T(2,128)}, f32[16,512]{1,0:T(8,128)}) custom-call(f32[16,128]{1,0:T(8,128)S(1)} %collective-permute-done.got_a, f32[16,128]{1,0:T(8,128)S(1)} %collective-permute-done.1.got_b, f32[16,512]{1,0:T(8,128)S(1)} %get-tuple-element.24.image), custom_call_target="tpu_custom_call" | custom-call | tf_op jit(solution)/shard_map/finish/pallas_call | solution.py:425
Async XLA Ops:
  4.7 6.5 %collective-permute-start.1 = (f32[16,128]{1,0:T(8,128)S(1)}, f32[16,128]{1,0:T(8,128)S(1)}, u32[]{:S(2)}, u32[]{:S(2)}) collective-permute-start(f32[16,128]{1,0:T(8,128)S(1)} %get-tuple-element.23), channel_id=1, source_target_pairs={{0,1},{1,0},{2,4},{3,5},{4,2},{5,3},{6,8},{7,9},{8,6},{9,7},{10,12... | collective-permute-start | bytes 24584 | tf_op jit(solution)/shard_map/ppermute | solution.py:394
  5.1 6.1 %collective-permute-start = (f32[16,128]{1,0:T(8,128)S(1)}, f32[16,128]{1,0:T(8,128)S(1)}, u32[]{:S(2)}, u32[]{:S(2)}) collective-permute-start(f32[16,128]{1,0:T(8,128)S(1)} %get-tuple-element.23), channel_id=1, source_target_pairs={{0,2},{1,3},{2,0},{3,1},{4,6},{5,7},{6,4},{7,5},{8,10},{9,11},{10,... | collective-permute-start | bytes 24584 | tf_op jit(solution)/shard_map/ppermute | solution.py:394

commit v7 on v5

--- a/solution.py
+++ b/solution.py
@@ -63,14 +63,14 @@
 
 def pack_kernel(
     sz, n_rad, motion_hbm, size_hbm, block_hbm, offset_hbm, gas_hbm, pres_hbm, radial_hbm, counts_hbm, cols_hbm,
-    kinds_hbm, axial_hbm, table_hbm,
-    out, aux, table,
+    kinds_hbm, axial_hbm,
+    out, aux,
     motion, size, block, offset, gas, pres, radial, counts, cols, kinds, axial, sem,
 ):
     pairs = (
         (motion_hbm, motion), (gas_hbm, gas), (pres_hbm, pres), (size_hbm, size), (offset_hbm, offset),
         (block_hbm, block), (counts_hbm, counts), (radial_hbm, radial), (axial_hbm, axial), (cols_hbm, cols),
-        (kinds_hbm, kinds), (table_hbm, table),
+        (kinds_hbm, kinds),
     )
     copies = [pltpu.make_async_copy(src, dst, sem.at[i]) for i, (src, dst) in enumerate(pairs)]
     for copy in copies:
@@ -87,7 +87,7 @@
     copies[2].wait()
     for q in range(sz.quarters):
         out[pl.ds(sz.pres + q * layers, layers), :] = pres[:, q * BLOCK : (q + 1) * BLOCK]
-    for copy in copies[3:11]:
+    for copy in copies[3:]:
         copy.wait()
     out[pl.ds(sz.size, sz.tiles), :] = size[...]
     out[pl.ds(sz.offset, sz.tiles), :] = offset[...].astype(F32)
@@ -103,7 +103,6 @@
     lane = iota((1, axial.shape[1]), 1)
     kept = [jnp.where(lane < counts[0, slot], axial[slot : slot + 1, :], -1) for slot in range(2)]
     aux[pl.ds(8, 1), :] = jnp.concatenate(kept, axis=1)
-    copies[11].wait()
 
 
 def take_lanes(x, idx):
@@ -198,7 +197,6 @@
     mine = pl.multiple_of(r * tiles, tiles)
     for i in range(tiles):
         motion_out[:, i * BLOCK : (i + 1) * BLOCK] = state[pl.ds(mine + i, 6, stride=T), :]
-    sends[0].start()
 
     width = arr_rad.shape[2]
     for slot, exists, other in ((0, r > 0, jnp.maximum(r - 1, 0)), (1, r < n_rad - 1, jnp.minimum(r + 1, n_rad - 1))):
@@ -207,7 +205,6 @@
         got = pick(sz, state_of(sz, T, state, other), idx)
         for c in range(7):
             arr_rad[c, slot : slot + 1, :] = got[c][:, :width]
-    sends[1].start()
 
     rows = functools.partial(slab_rows, sz, n_rad, G)
     size = rows(sz.size)
@@ -221,12 +218,13 @@
         for piece, part in enumerate((high, low)):
             deps[pl.ds((piece * 8 + c) * T, T), :] = jnp.where(even, part, 0.0)
             deps[pl.ds((piece * 8 + 4 + c) * T, T), :] = jnp.where(even, 0.0, part)
-    cell = iota((BLOCK, BLOCK), 0)
+    cell = iota((BLOCK, BLOCK), 0).astype(F32).astype(BF16)
+    one, none = jnp.ones((BLOCK, BLOCK), BF16), jnp.zeros((BLOCK, BLOCK), BF16)
     for d in range(n_rad):
         for i in range(tiles):
             t = d * tiles + i
-            off = G[d, pl.ds(sz.offset + i, 1), :].astype(I32)
-            onehot = (cell == off).astype(F32).astype(BF16)
+            off = jnp.broadcast_to(G[d, pl.ds(sz.offset + i, 1), :], (16, BLOCK)).astype(BF16)
+            onehot = jnp.where(cell == jnp.concatenate([off] * (BLOCK // 16), axis=0), one, none)
             lhs = deps[pl.ds(t, 16, stride=T), :].astype(BF16)
             res = dot_nt(lhs, onehot)
             res = res[:8] + res[8:]
@@ -246,23 +244,22 @@
                 gas_out[c, :, at] = G[r, pl.ds(sz.gas + c * blocks + q * layers, layers), :] + part
             else:
                 liquid[:, at] = part
-    sends[2].start()
-    sends[3].start()
 
     pres = jnp.concatenate([G[d, pl.ds(sz.pres, blocks), :] for d in range(n_rad)], axis=0)
-    index = aux[pl.ds(0, 4), :]
+    index = [jnp.broadcast_to(aux[pl.ds(k, 1), :], (BLOCK, BLOCK)).astype(jnp.int16) for k in range(4)]
     grouped = [None] * (NT // 2)
     for first in range(0, slab_blocks, BLOCK):
         p_high, p_low = split2(jnp.transpose(pres[first : first + BLOCK]))
         here = iota((BLOCK, BLOCK), 0) + first + jnp.where(iota((BLOCK, BLOCK), 1) < blocks, 0, slab_blocks)
         for j in range(NT // 2):
-            aim = here + 2 * j * slab_blocks
-            count = (aim == index[0:1]).astype(F32)
-            for k in range(1, index.shape[0]):
-                count = count + (aim == index[k : k + 1]).astype(F32)
-            count = count.astype(BF16)
+            aim = (here + 2 * j * slab_blocks).astype(jnp.int16)
+            count = none
+            for k in range(4):
+                count = count + jnp.where(aim == index[k], one, none)
             part = dot(p_high, count) + dot(p_low, count)
             grouped[j] = part if grouped[j] is None else grouped[j] + part
+    for send in sends:
+        send.start()
     sums = [None, None]
     for j in range(NT // 2):
         g_high, g_low = split2(grouped[j])
@@ -326,15 +323,14 @@
     size2 = parcel_size.reshape(sz.tiles, BLOCK)
     offset2 = parcel_offset.reshape(sz.tiles, BLOCK)
 
-    packed, aux, table = pl.pallas_call(
+    packed, aux = pl.pallas_call(
         functools.partial(pack_kernel, sz, n_rad),
         out_shape=[
             jax.ShapeDtypeStruct((sz.rows, BLOCK), F32),
             jax.ShapeDtypeStruct((16, BLOCK), I32),
-            jax.ShapeDtypeStruct(block_table.shape, F32),
-        ],
-        in_specs=[hbm] * 12,
-        out_specs=[vmem] * 3,
+        ],
+        in_specs=[hbm] * 11,
+        out_specs=[vmem] * 2,
         scratch_shapes=[
             pltpu.VMEM(parcel_motion.shape, F32),
             pltpu.VMEM(size2.shape, F32),
@@ -347,7 +343,7 @@
             pltpu.VMEM((4, sz.blocks), I32),
             pltpu.VMEM((4, sz.blocks), I32),
             pltpu.VMEM((2, cap_ax), I32),
-            pltpu.SemaphoreType.DMA((12,)),
+            pltpu.SemaphoreType.DMA((11,)),
         ],
         compiler_params=params,
         name="pack",
@@ -357,7 +353,7 @@
             for x in (
                 parcel_motion, size2, parcel_block.reshape(1, sz.groups), offset2, gas_velocity, pressure,
                 send_radial.reshape(2, cap_rad), counts, block_cols[0].T, block_kinds[0].T,
-                send_axial.reshape(2, cap_ax), block_table,
+                send_axial.reshape(2, cap_ax),
             )
         )
     )
@@ -373,6 +369,7 @@
         out_specs=[vmem] * 2,
         scratch_shapes=[pltpu.VMEM((3, n_rad * sz.groups, BLOCK), F32)],
         compiler_params=params,
+        cost_estimate=pl.CostEstimate(flops=4_000_000_000, bytes_accessed=1_000_000, transcendentals=0),
         name="move",
     )(gathered, aux)
 
@@ -414,7 +411,7 @@
         compiler_params=params,
         cost_estimate=pl.CostEstimate(flops=2_000_000_000, bytes_accessed=2_000_000, transcendentals=0),
         name="rest",
-    )(gathered, aux, table, state)
+    )(gathered, aux, block_table, state)
 
     arr_ax, pressure_image = pl.pallas_call(
         functools.partial(finish_kernel, sz, n_ax),

time: 12 us -> 11.8 us (0.983)
  Pallas kernels: 4.55 us -> 4.35 us
    pallas_call x1, Pallas kernels: 1.35 us -> 1.15 us  [on_device(): pl.pallas_call(functools.partial(pack_kernel, sz, n_rad), out_shape=[jax....]
where the time goes in v7:
time: 11.8 us; the launch traced here: 11.6 us
  starting transfers between devices  4.41 us (37%)
  Pallas kernels  4.35 us (37%)
  blocking collectives  2.17 us (18%)
  between operations  0.68 us (6%)
    ppermute x2, starting transfers between devices, exchange(): return lax.ppermute(message, ('ax', 'rad'), list(enumerate(to)))  4.41 us
    all_gather x1, blocking collectives, on_device(): gathered = lax.all_gather(packed, 'rad', axis=0)  2.17 us
    pallas_call x1, Pallas kernels, on_device(): pl.pallas_call(functools.partial(rest_kernel, sz, n_rad), out_shape=[jax....  2.08 us
    pallas_call x1, Pallas kernels, on_device(): pl.pallas_call(functools.partial(pack_kernel, sz, n_rad), out_shape=[jax....  1.15 us
    pallas_call x1, Pallas kernels, on_device(): pl.pallas_call(functools.partial(finish_kernel, sz, n_ax), out_shape=[jax...  0.69 us
    pallas_call x1, Pallas kernels, on_device(): pl.pallas_call(functools.partial(move_kernel, sz, n_rad), out_shape=[jax....  0.44 us
  transfers between devices with their start and end apart: 2, of which 0 were waited for; matrix products, arithmetic and copies ran while one was open for 0% of the time, Pallas kernels for 18%

profile of v7, /device:TPU:0, one launch (start us, length us, event | category | flops | bytes accessed | tf_op | source)
XLA Modules:
  0.0 11.6 jit_solution(12726429631311283012)
XLA Ops:
  0.6 1.1 %pack.1 = (f32[392,128]{1,0:T(8,128)S(1)}, s32[16,128]{1,0:T(8,128)S(1)}) custom-call(f32[6,2048]{1,0:T(8,128)} %motion_hbm.1, f32[16,128]{1,0:T(8,128)} %bitcast.21, s32[1,32]{1,0:T(1,128)} %bitcast.27, s32[16,128]{1,0:T(8,128)} %bitcast.22, f32[3,16,512]{2,1,0:T(8,128)} %gas_hbm.1, f32[16,512]{1,0:T(8,128)} %pres_hbm.1, s32[2,32]{1,0:T(2,128)} %bitcast.25, ...), custom_call_target="tpu_custom_call" | custom-call | tf_op jit(solution)/shard_map/pack/pallas_call | solution.py:326
  1.8 2.2 %all-gather = f32[784,128]{1,0:T(8,128)S(1)} all-gather(f32[392,128]{1,0:T(8,128)S(1)} %get-tuple-element.17), channel_id=2, replica_groups=mesh['ax'=16,'rad'=2] {'rad'}, dimensions={0}, use_global_device_ids=true | all-gather | bytes 602112 | tf_op jit(solution)/shard_map/all_gather | solution.py:360
  4.0 0.0 copy-start
  4.0 0.4 %move.1 = (f32[224,128]{1,0:T(8,128)S(1)}, f32[16,128]{1,0:T(8,128)S(1)}) custom-call(f32[2,392,128]{2,1,0:T(8,128)S(1)} %bitcast.19, s32[16,128]{1,0:T(8,128)S(1)} %get-tuple-element.18.aux), custom_call_target="tpu_custom_call" | custom-call | flops 4000000000 | bytes 1000000 | tf_op jit(solution)/shard_map/move/pallas_call | solution.py:362
  4.4 0.4 %collective-permute-start.1 = (f32[16,128]{1,0:T(8,128)S(1)}, f32[16,128]{1,0:T(8,128)S(1)}, u32[]{:S(2)}, u32[]{:S(2)}) collective-permute-start(f32[16,128]{1,0:T(8,128)S(1)} %get-tuple-element.21), channel_id=1, source_target_pairs={{0,1},{1,0},{2,4},{3,5},{4,2},{5,3},{6,8},{7,9},{8,6},{9,7},{10,12... | collective-permute-start | bytes 24584 | tf_op jit(solution)/shard_map/ppermute | solution.py:385
  4.9 4.0 %collective-permute-start = (f32[16,128]{1,0:T(8,128)S(1)}, f32[16,128]{1,0:T(8,128)S(1)}, u32[]{:S(2)}, u32[]{:S(2)}) collective-permute-start(f32[16,128]{1,0:T(8,128)S(1)} %get-tuple-element.21), channel_id=1, source_target_pairs={{0,2},{1,3},{2,0},{3,1},{4,6},{5,7},{6,4},{7,5},{8,10},{9,11},{10,... | collective-permute-start | bytes 24584 | tf_op jit(solution)/shard_map/ppermute | solution.py:385
  8.8 0.0 copy-done
  8.8 2.1 %rest.1 = (f32[6,2048]{1,0:T(8,128)}, f32[7,2,32]{2,1,0:T(2,128)}, f32[3,16,512]{2,1,0:T(8,128)}, f32[16,512]{1,0:T(8,128)}, f32[16,512]{1,0:T(8,128)S(1)}) custom-call(f32[2,392,128]{2,1,0:T(8,128)S(1)} %bitcast.20, s32[16,128]{1,0:T(8,128)S(1)} %get-tuple-element.18.aux, f32[8,128,128]{2,1,0:T(8,128)S(1)} %copy-done, f32[224,128]{1,0:T(8,128)S(1)} %get-tuple-element.19.state), custom_call_target="tpu_custom_call" | custom-call | flops 2000000000 | bytes 2000000 | tf_op jit(solution)/shard_map/rest/pallas_call | solution.py:390
  10.9 0.0 collective-permute-done.1.got_b
  10.9 0.0 collective-permute-done.got_a
  10.9 0.7 %finish.1 = (f32[7,2,64]{2,1,0:T(2,128)}, f32[16,512]{1,0:T(8,128)}) custom-call(f32[16,128]{1,0:T(8,128)S(1)} %collective-permute-done.got_a, f32[16,128]{1,0:T(8,128)S(1)} %collective-permute-done.1.got_b, f32[16,512]{1,0:T(8,128)S(1)} %get-tuple-element.22.image), custom_call_target="tpu_custom_call" | custom-call | tf_op jit(solution)/shard_map/finish/pallas_call | solution.py:416
Async XLA Ops:
  4.0 4.9 %copy-start = (f32[8,128,128]{2,1,0:T(8,128)S(1)}, f32[8,128,128]{2,1,0:T(8,128)}, u32[]{:S(2)}) copy-start(f32[8,128,128]{2,1,0:T(8,128)} %table.1) | copy-start | bytes 1572868
  4.4 6.5 %collective-permute-start.1 = (f32[16,128]{1,0:T(8,128)S(1)}, f32[16,128]{1,0:T(8,128)S(1)}, u32[]{:S(2)}, u32[]{:S(2)}) collective-permute-start(f32[16,128]{1,0:T(8,128)S(1)} %get-tuple-element.21), channel_id=1, source_target_pairs={{0,1},{1,0},{2,4},{3,5},{4,2},{5,3},{6,8},{7,9},{8,6},{9,7},{10,12... | collective-permute-start | bytes 24584 | tf_op jit(solution)/shard_map/ppermute | solution.py:385
  4.9 6.1 %collective-permute-start = (f32[16,128]{1,0:T(8,128)S(1)}, f32[16,128]{1,0:T(8,128)S(1)}, u32[]{:S(2)}, u32[]{:S(2)}) collective-permute-start(f32[16,128]{1,0:T(8,128)S(1)} %get-tuple-element.21), channel_id=1, source_target_pairs={{0,2},{1,3},{2,0},{3,1},{4,6},{5,7},{6,4},{7,5},{8,10},{9,11},{10,... | collective-permute-start | bytes 24584 | tf_op jit(solution)/shard_map/ppermute | solution.py:385

commit v8 on v7

--- a/solution.py
+++ b/solution.py
@@ -68,8 +68,8 @@
     motion, size, block, offset, gas, pres, radial, counts, cols, kinds, axial, sem,
 ):
     pairs = (
-        (motion_hbm, motion), (gas_hbm, gas), (pres_hbm, pres), (size_hbm, size), (offset_hbm, offset),
-        (block_hbm, block), (counts_hbm, counts), (radial_hbm, radial), (axial_hbm, axial), (cols_hbm, cols),
+        (motion_hbm, motion), *((gas_hbm.at[c], gas.at[c]) for c in range(3)), (pres_hbm, pres), (size_hbm, size),
+        (offset_hbm, offset), (block_hbm, block), (counts_hbm, counts), (radial_hbm, radial), (axial_hbm, axial), (cols_hbm, cols),
         (kinds_hbm, kinds),
     )
     copies = [pltpu.make_async_copy(src, dst, sem.at[i]) for i, (src, dst) in enumerate(pairs)]
@@ -80,14 +80,14 @@
     copies[0].wait()
     for i in range(sz.tiles):
         out[pl.ds(sz.motion + i, 6, stride=sz.tiles), :] = motion[:, i * BLOCK : (i + 1) * BLOCK]
-    copies[1].wait()
     for c in range(3):
+        copies[1 + c].wait()
         for q in range(sz.quarters):
             out[pl.ds(sz.gas + c * sz.blocks + q * layers, layers), :] = gas[c, :, q * BLOCK : (q + 1) * BLOCK]
-    copies[2].wait()
+    copies[4].wait()
     for q in range(sz.quarters):
         out[pl.ds(sz.pres + q * layers, layers), :] = pres[:, q * BLOCK : (q + 1) * BLOCK]
-    for copy in copies[3:]:
+    for copy in copies[5:]:
         copy.wait()
     out[pl.ds(sz.size, sz.tiles), :] = size[...]
     out[pl.ds(sz.offset, sz.tiles), :] = offset[...].astype(F32)
@@ -148,7 +148,7 @@
         axis=1,
     )
     high, low = split2(gas_slab)
-    found = dot(chooser, high) + dot(chooser, low)
+    found = dot(jnp.concatenate([chooser, chooser], axis=1), jnp.concatenate([high, low], axis=0))
     for c in range(3):
         near[c] = found[:, c * BLOCK : (c + 1) * BLOCK]
 
@@ -220,23 +220,30 @@
             deps[pl.ds((piece * 8 + 4 + c) * T, T), :] = jnp.where(even, 0.0, part)
     cell = iota((BLOCK, BLOCK), 0).astype(F32).astype(BF16)
     one, none = jnp.ones((BLOCK, BLOCK), BF16), jnp.zeros((BLOCK, BLOCK), BF16)
+    blank = jnp.zeros((16, BLOCK), BF16)
     for d in range(n_rad):
-        for i in range(tiles):
-            t = d * tiles + i
-            off = jnp.broadcast_to(G[d, pl.ds(sz.offset + i, 1), :], (16, BLOCK)).astype(BF16)
-            onehot = jnp.where(cell == jnp.concatenate([off] * (BLOCK // 16), axis=0), one, none)
-            lhs = deps[pl.ds(t, 16, stride=T), :].astype(BF16)
-            res = dot_nt(lhs, onehot)
-            res = res[:8] + res[8:]
-            spread[pl.ds(2 * t, 4, stride=2 * T), :] = res[:4]
-            spread[pl.ds(2 * t + 1, 4, stride=2 * T), :] = res[4:]
+        for i in range(0, tiles, 2):
+            onehot, lhs = [], []
+            for t in (i, i + 1):
+                off = jnp.broadcast_to(G[d, pl.ds(sz.offset + t, 1), :], (16, BLOCK)).astype(BF16)
+                onehot.append(jnp.where(cell == jnp.concatenate([off] * (BLOCK // 16), axis=0), one, none))
+                lhs.append(deps[pl.ds(d * tiles + t, 16, stride=T), :].astype(BF16))
+            lhs = jnp.concatenate(
+                [jnp.concatenate([lhs[0], blank], axis=1), jnp.concatenate([blank, lhs[1]], axis=1)], axis=0
+            )
+            res = dot_nt(lhs, jnp.concatenate(onehot, axis=1))
+            for k in range(2):
+                t = d * tiles + i + k
+                both = res[16 * k : 16 * k + 8] + res[16 * k + 8 : 16 * k + 16]
+                spread[pl.ds(2 * t, 4, stride=2 * T), :] = both[:4]
+                spread[pl.ds(2 * t + 1, 4, stride=2 * T), :] = both[4:]
     own = iota((blocks, groups), 0) + r * blocks
     adder = jnp.concatenate(
-        [(own == b[:, :groups].astype(I32)).astype(F32) for b in block_rows], axis=1
+        [(own == b[:, :groups].astype(I32)).astype(F32) for b in block_rows] * 2, axis=1
     ).astype(BF16)
     for c in range(4):
         high, low = split2(spread[pl.ds(c * 2 * T, 2 * T), :])
-        total = dot(adder, high) + dot(adder, low)
+        total = dot(adder, jnp.concatenate([high, low], axis=0))
         for q in range(sz.quarters):
             part = total[q * layers : (q + 1) * layers]
             at = slice(q * BLOCK, (q + 1) * BLOCK)
@@ -247,26 +254,35 @@
 
     pres = jnp.concatenate([G[d, pl.ds(sz.pres, blocks), :] for d in range(n_rad)], axis=0)
     index = [jnp.broadcast_to(aux[pl.ds(k, 1), :], (BLOCK, BLOCK)).astype(jnp.int16) for k in range(4)]
-    grouped = [None] * (NT // 2)
+    left, right = [], []
     for first in range(0, slab_blocks, BLOCK):
         p_high, p_low = split2(jnp.transpose(pres[first : first + BLOCK]))
         here = iota((BLOCK, BLOCK), 0) + first + jnp.where(iota((BLOCK, BLOCK), 1) < blocks, 0, slab_blocks)
+        counts = []
         for j in range(NT // 2):
             aim = (here + 2 * j * slab_blocks).astype(jnp.int16)
             count = none
             for k in range(4):
                 count = count + jnp.where(aim == index[k], one, none)
-            part = dot(p_high, count) + dot(p_low, count)
-            grouped[j] = part if grouped[j] is None else grouped[j] + part
+            counts.append(count)
+        counts = jnp.concatenate(counts, axis=1)
+        left += [p_high, p_low]
+        right += [counts, counts]
+    grouped = dot(jnp.concatenate(left, axis=1), jnp.concatenate(right, axis=0))
     for send in sends:
         send.start()
-    sums = [None, None]
-    for j in range(NT // 2):
-        g_high, g_low = split2(grouped[j])
-        for s in range(2):
-            t_high, t_low = split2(table[2 * j + s])
-            part = dot(t_high, g_high) + dot(t_low, g_high) + dot(t_high, g_low)
-            sums[s] = part if sums[s] is None else sums[s] + part
+    g_high, g_low = split2(
+        jnp.concatenate([grouped[:, j * BLOCK : (j + 1) * BLOCK] for j in range(NT // 2)], axis=0)
+    )
+    t_high, t_low = split2(
+        jnp.concatenate(
+            [jnp.concatenate([table[2 * j + s] for j in range(NT // 2)], axis=1) for s in range(2)], axis=0
+        )
+    )
+    sums = dot(
+        jnp.concatenate([t_high, t_low, t_high], axis=1), jnp.concatenate([g_high, g_high, g_low], axis=0)
+    )
+    sums = [sums[:BLOCK], sums[BLOCK:]]
     both = jnp.where(iota((BLOCK, BLOCK), 1) < blocks, sums[0], sums[1])
     both = both + pltpu.roll(jnp.where(iota((BLOCK, BLOCK), 1) < blocks, 0.0, sums[1]), blocks, 1)
     coup[...] = jnp.transpose(both)
@@ -343,7 +359,7 @@
             pltpu.VMEM((4, sz.blocks), I32),
             pltpu.VMEM((4, sz.blocks), I32),
             pltpu.VMEM((2, cap_ax), I32),
-            pltpu.SemaphoreType.DMA((11,)),
+            pltpu.SemaphoreType.DMA((13,)),
         ],
         compiler_params=params,
         name="pack",

time: 11.8 us -> 11.5 us (0.975)
  Pallas kernels: 4.35 us -> 4.06 us
    pallas_call x1, Pallas kernels: 2.08 us -> 1.87 us  [on_device(): pl.pallas_call(functools.partial(rest_kernel, sz, n_rad), out_shape=[jax....]
  transfers between devices with their start and end apart: 2 -> 2, of which waited for: 0 -> 0; matrix products, arithmetic and copies ran while one was open for 0% -> 0% of each run, Pallas kernels for 18% -> 17%
where the time goes in v8:
time: 11.5 us; the launch traced here: 11.3 us
  starting transfers between devices  4.41 us (38%)
  Pallas kernels  4.06 us (35%)
  blocking collectives  2.17 us (19%)
  between operations  0.68 us (6%)
    ppermute x2, starting transfers between devices, exchange(): return lax.ppermute(message, ('ax', 'rad'), list(enumerate(to)))  4.41 us
    all_gather x1, blocking collectives, on_device(): gathered = lax.all_gather(packed, 'rad', axis=0)  2.17 us
    pallas_call x1, Pallas kernels, on_device(): pl.pallas_call(functools.partial(rest_kernel, sz, n_rad), out_shape=[jax....  1.87 us
    pallas_call x1, Pallas kernels, on_device(): pl.pallas_call(functools.partial(pack_kernel, sz, n_rad), out_shape=[jax....  1.1 us
    pallas_call x1, Pallas kernels, on_device(): pl.pallas_call(functools.partial(finish_kernel, sz, n_ax), out_shape=[jax...  0.69 us
    pallas_call x1, Pallas kernels, on_device(): pl.pallas_call(functools.partial(move_kernel, sz, n_rad), out_shape=[jax....  0.4 us
  transfers between devices with their start and end apart: 2, of which 0 were waited for; matrix products, arithmetic and copies ran while one was open for 0% of the time, Pallas kernels for 17%

profile of v8, /device:TPU:0, one launch (start us, length us, event | category | flops | bytes accessed | tf_op | source)
XLA Modules:
  0.0 11.3 jit_solution(17738084745886125747)
XLA Ops:
  0.6 1.1 %pack.1 = (f32[392,128]{1,0:T(8,128)S(1)}, s32[16,128]{1,0:T(8,128)S(1)}) custom-call(f32[6,2048]{1,0:T(8,128)} %motion_hbm.1, f32[16,128]{1,0:T(8,128)} %bitcast.21, s32[1,32]{1,0:T(1,128)} %bitcast.27, s32[16,128]{1,0:T(8,128)} %bitcast.22, f32[3,16,512]{2,1,0:T(8,128)} %gas_hbm.1, f32[16,512]{1,0:T(8,128)} %pres_hbm.1, s32[2,32]{1,0:T(2,128)} %bitcast.25, ...), custom_call_target="tpu_custom_call" | custom-call | tf_op jit(solution)/shard_map/pack/pallas_call | solution.py:342
  1.7 2.2 %all-gather = f32[784,128]{1,0:T(8,128)S(1)} all-gather(f32[392,128]{1,0:T(8,128)S(1)} %get-tuple-element.17), channel_id=2, replica_groups=mesh['ax'=16,'rad'=2] {'rad'}, dimensions={0}, use_global_device_ids=true | all-gather | bytes 602112 | tf_op jit(solution)/shard_map/all_gather | solution.py:376
  3.9 0.0 copy-start
  3.9 0.4 %move.1 = (f32[224,128]{1,0:T(8,128)S(1)}, f32[16,128]{1,0:T(8,128)S(1)}) custom-call(f32[2,392,128]{2,1,0:T(8,128)S(1)} %bitcast.19, s32[16,128]{1,0:T(8,128)S(1)} %get-tuple-element.18.aux), custom_call_target="tpu_custom_call" | custom-call | flops 4000000000 | bytes 1000000 | tf_op jit(solution)/shard_map/move/pallas_call | solution.py:378
  4.3 0.4 %collective-permute-start.1 = (f32[16,128]{1,0:T(8,128)S(1)}, f32[16,128]{1,0:T(8,128)S(1)}, u32[]{:S(2)}, u32[]{:S(2)}) collective-permute-start(f32[16,128]{1,0:T(8,128)S(1)} %get-tuple-element.21), channel_id=1, source_target_pairs={{0,1},{1,0},{2,4},{3,5},{4,2},{5,3},{6,8},{7,9},{8,6},{9,7},{10,12... | collective-permute-start | bytes 24584 | tf_op jit(solution)/shard_map/ppermute | solution.py:401
  4.8 4.0 %collective-permute-start = (f32[16,128]{1,0:T(8,128)S(1)}, f32[16,128]{1,0:T(8,128)S(1)}, u32[]{:S(2)}, u32[]{:S(2)}) collective-permute-start(f32[16,128]{1,0:T(8,128)S(1)} %get-tuple-element.21), channel_id=1, source_target_pairs={{0,2},{1,3},{2,0},{3,1},{4,6},{5,7},{6,4},{7,5},{8,10},{9,11},{10,... | collective-permute-start | bytes 24584 | tf_op jit(solution)/shard_map/ppermute | solution.py:401
  8.7 0.0 copy-done
  8.7 1.9 %rest.1 = (f32[6,2048]{1,0:T(8,128)}, f32[7,2,32]{2,1,0:T(2,128)}, f32[3,16,512]{2,1,0:T(8,128)}, f32[16,512]{1,0:T(8,128)}, f32[16,512]{1,0:T(8,128)S(1)}) custom-call(f32[2,392,128]{2,1,0:T(8,128)S(1)} %bitcast.20, s32[16,128]{1,0:T(8,128)S(1)} %get-tuple-element.18.aux, f32[8,128,128]{2,1,0:T(8,128)S(1)} %copy-done, f32[224,128]{1,0:T(8,128)S(1)} %get-tuple-element.19.state), custom_call_target="tpu_custom_call" | custom-call | flops 2000000000 | bytes 2000000 | tf_op jit(solution)/shard_map/rest/pallas_call | solution.py:406
  10.6 0.0 collective-permute-done.1.got_b
  10.6 0.0 collective-permute-done.got_a
  10.6 0.7 %finish.1 = (f32[7,2,64]{2,1,0:T(2,128)}, f32[16,512]{1,0:T(8,128)}) custom-call(f32[16,128]{1,0:T(8,128)S(1)} %collective-permute-done.got_a, f32[16,128]{1,0:T(8,128)S(1)} %collective-permute-done.1.got_b, f32[16,512]{1,0:T(8,128)S(1)} %get-tuple-element.22.image), custom_call_target="tpu_custom_call" | custom-call | tf_op jit(solution)/shard_map/finish/pallas_call | solution.py:432
Async XLA Ops:
  3.9 4.8 %copy-start = (f32[8,128,128]{2,1,0:T(8,128)S(1)}, f32[8,128,128]{2,1,0:T(8,128)}, u32[]{:S(2)}) copy-start(f32[8,128,128]{2,1,0:T(8,128)} %table.1) | copy-start | bytes 1572868
  4.3 6.3 %collective-permute-start.1 = (f32[16,128]{1,0:T(8,128)S(1)}, f32[16,128]{1,0:T(8,128)S(1)}, u32[]{:S(2)}, u32[]{:S(2)}) collective-permute-start(f32[16,128]{1,0:T(8,128)S(1)} %get-tuple-element.21), channel_id=1, source_target_pairs={{0,1},{1,0},{2,4},{3,5},{4,2},{5,3},{6,8},{7,9},{8,6},{9,7},{10,12... | collective-permute-start | bytes 24584 | tf_op jit(solution)/shard_map/ppermute | solution.py:401
  4.8 5.9 %collective-permute-start = (f32[16,128]{1,0:T(8,128)S(1)}, f32[16,128]{1,0:T(8,128)S(1)}, u32[]{:S(2)}, u32[]{:S(2)}) collective-permute-start(f32[16,128]{1,0:T(8,128)S(1)} %get-tuple-element.21), channel_id=1, source_target_pairs={{0,2},{1,3},{2,0},{3,1},{4,6},{5,7},{6,4},{7,5},{8,10},{9,11},{10,... | collective-permute-start | bytes 24584 | tf_op jit(solution)/shard_map/ppermute | solution.py:401

commit v9 on v8

--- a/solution.py
+++ b/solution.py
@@ -67,27 +67,17 @@
     out, aux,
     motion, size, block, offset, gas, pres, radial, counts, cols, kinds, axial, sem,
 ):
-    pairs = (
-        (motion_hbm, motion), *((gas_hbm.at[c], gas.at[c]) for c in range(3)), (pres_hbm, pres), (size_hbm, size),
-        (offset_hbm, offset), (block_hbm, block), (counts_hbm, counts), (radial_hbm, radial), (axial_hbm, axial), (cols_hbm, cols),
-        (kinds_hbm, kinds),
-    )
-    copies = [pltpu.make_async_copy(src, dst, sem.at[i]) for i, (src, dst) in enumerate(pairs)]
+    small = (
+        (counts_hbm, counts), (block_hbm, block), (radial_hbm, radial), (axial_hbm, axial), (cols_hbm, cols),
+        (kinds_hbm, kinds), (offset_hbm, offset), (size_hbm, size),
+    )
+    large = ((motion_hbm, motion), (pres_hbm, pres), *((gas_hbm.at[c], gas.at[c]) for c in range(3)))
+    copies = [pltpu.make_async_copy(src, dst, sem.at[i]) for i, (src, dst) in enumerate(small + large)]
     for copy in copies:
         copy.start()
     out[pl.ds(sz.meta, 8), :] = jnp.full((8, BLOCK), -1.0, F32)
     layers = sz.layers
-    copies[0].wait()
-    for i in range(sz.tiles):
-        out[pl.ds(sz.motion + i, 6, stride=sz.tiles), :] = motion[:, i * BLOCK : (i + 1) * BLOCK]
-    for c in range(3):
-        copies[1 + c].wait()
-        for q in range(sz.quarters):
-            out[pl.ds(sz.gas + c * sz.blocks + q * layers, layers), :] = gas[c, :, q * BLOCK : (q + 1) * BLOCK]
-    copies[4].wait()
-    for q in range(sz.quarters):
-        out[pl.ds(sz.pres + q * layers, layers), :] = pres[:, q * BLOCK : (q + 1) * BLOCK]
-    for copy in copies[5:]:
+    for copy in copies[: len(small)]:
         copy.wait()
     out[pl.ds(sz.size, sz.tiles), :] = size[...]
     out[pl.ds(sz.offset, sz.tiles), :] = offset[...].astype(F32)
@@ -97,12 +87,22 @@
     for slot in range(2):
         kept = jnp.where(lane < counts[0, 2 + slot], radial[slot : slot + 1, :], -1)
         out[pl.ds(sz.meta + 1 + slot, 1), pl.ds(0, width)] = kept.astype(F32)
-
     index = kinds[...] * (n_rad * sz.blocks) + block_row(sz, cols[...])
     aux[pl.ds(0, index.shape[0]), :] = jnp.concatenate([index, index], axis=1)
     lane = iota((1, axial.shape[1]), 1)
     kept = [jnp.where(lane < counts[0, slot], axial[slot : slot + 1, :], -1) for slot in range(2)]
     aux[pl.ds(8, 1), :] = jnp.concatenate(kept, axis=1)
+    motion_copy, pres_copy, *gas_copies = copies[len(small) :]
+    motion_copy.wait()
+    for i in range(sz.tiles):
+        out[pl.ds(sz.motion + i, 6, stride=sz.tiles), :] = motion[:, i * BLOCK : (i + 1) * BLOCK]
+    pres_copy.wait()
+    for q in range(sz.quarters):
+        out[pl.ds(sz.pres + q * layers, layers), :] = pres[:, q * BLOCK : (q + 1) * BLOCK]
+    for c in range(3):
+        gas_copies[c].wait()
+        for q in range(sz.quarters):
+            out[pl.ds(sz.gas + c * sz.blocks + q * layers, layers), :] = gas[c, :, q * BLOCK : (q + 1) * BLOCK]
 
 
 def take_lanes(x, idx):
@@ -186,25 +186,16 @@
     sends = [
         pltpu.make_async_copy(src, dst, sem.at[i])
         for i, (src, dst) in enumerate(
-            ((motion_out, motion_hbm), (arr_rad, arr_hbm), (gas_out, gas_hbm), (liquid, liquid_hbm))
+            (
+                (motion_out, motion_hbm), (arr_rad, arr_hbm), *((gas_out.at[c], gas_hbm.at[c]) for c in range(3)),
+                (liquid, liquid_hbm),
+            )
         )
     ]
     layers, tiles, blocks, groups = sz.layers, sz.tiles, sz.blocks, sz.groups
     slab_blocks = n_rad * blocks
     T = n_rad * tiles
     block_rows = [G[d, pl.ds(sz.meta, 1), :] for d in range(n_rad)]
-
-    mine = pl.multiple_of(r * tiles, tiles)
-    for i in range(tiles):
-        motion_out[:, i * BLOCK : (i + 1) * BLOCK] = state[pl.ds(mine + i, 6, stride=T), :]
-
-    width = arr_rad.shape[2]
-    for slot, exists, other in ((0, r > 0, jnp.maximum(r - 1, 0)), (1, r < n_rad - 1, jnp.minimum(r + 1, n_rad - 1))):
-        idx = G[other, pl.ds(sz.meta + 1 + slot, 1), :].astype(I32)
-        idx = jnp.where(exists, idx, -1)
-        got = pick(sz, state_of(sz, T, state, other), idx)
-        for c in range(7):
-            arr_rad[c, slot : slot + 1, :] = got[c][:, :width]
 
     rows = functools.partial(slab_rows, sz, n_rad, G)
     size = rows(sz.size)
@@ -251,6 +242,8 @@
                 gas_out[c, :, at] = G[r, pl.ds(sz.gas + c * blocks + q * layers, layers), :] + part
             else:
                 liquid[:, at] = part
+    for send in sends[2:]:
+        send.start()
 
     pres = jnp.concatenate([G[d, pl.ds(sz.pres, blocks), :] for d in range(n_rad)], axis=0)
     index = [jnp.broadcast_to(aux[pl.ds(k, 1), :], (BLOCK, BLOCK)).astype(jnp.int16) for k in range(4)]
@@ -269,8 +262,19 @@
         left += [p_high, p_low]
         right += [counts, counts]
     grouped = dot(jnp.concatenate(left, axis=1), jnp.concatenate(right, axis=0))
-    for send in sends:
-        send.start()
+    mine = pl.multiple_of(r * tiles, tiles)
+    for i in range(tiles):
+        motion_out[:, i * BLOCK : (i + 1) * BLOCK] = state[pl.ds(mine + i, 6, stride=T), :]
+    sends[0].start()
+    width = arr_rad.shape[2]
+    for slot, exists, other in ((0, r > 0, jnp.maximum(r - 1, 0)), (1, r < n_rad - 1, jnp.minimum(r + 1, n_rad - 1))):
+        idx = G[other, pl.ds(sz.meta + 1 + slot, 1), :].astype(I32)
+        idx = jnp.where(exists, idx, -1)
+        got = pick(sz, state_of(sz, T, state, other), idx)
+        for c in range(7):
+            arr_rad[c, slot : slot + 1, :] = got[c][:, :width]
+    sends[1].start()
+
     g_high, g_low = split2(
         jnp.concatenate([grouped[:, j * BLOCK : (j + 1) * BLOCK] for j in range(NT // 2)], axis=0)
     )
@@ -422,7 +426,7 @@
             pltpu.VMEM((7, 2, cap_rad), F32),
             pltpu.VMEM(gas_velocity.shape, F32),
             pltpu.VMEM(pressure.shape, F32),
-            pltpu.SemaphoreType.DMA((4,)),
+            pltpu.SemaphoreType.DMA((6,)),
         ],
         compiler_params=params,
         cost_estimate=pl.CostEstimate(flops=2_000_000_000, bytes_accessed=2_000_000, transcendentals=0),

time: 11.5 us -> 11.5 us (level)
  transfers between devices with their start and end apart: 2 -> 2, of which waited for: 0 -> 0; matrix products, arithmetic and copies ran while one was open for 0% -> 0% of each run, Pallas kernels for 17% -> 16%
where the time goes in v9:
time: 11.5 us; the launch traced here: 11.3 us
  starting transfers between devices  4.41 us (38%)
  Pallas kernels  4.05 us (35%)
  blocking collectives  2.17 us (19%)
  between operations  0.68 us (6%)
    ppermute x2, starting transfers between devices, exchange(): return lax.ppermute(message, ('ax', 'rad'), list(enumerate(to)))  4.41 us
    all_gather x1, blocking collectives, on_device(): gathered = lax.all_gather(packed, 'rad', axis=0)  2.17 us
    pallas_call x1, Pallas kernels, on_device(): pl.pallas_call(functools.partial(rest_kernel, sz, n_rad), out_shape=[jax....  1.86 us
    pallas_call x1, Pallas kernels, on_device(): pl.pallas_call(functools.partial(pack_kernel, sz, n_rad), out_shape=[jax....  1.1 us
    pallas_call x1, Pallas kernels, on_device(): pl.pallas_call(functools.partial(finish_kernel, sz, n_ax), out_shape=[jax...  0.69 us
    pallas_call x1, Pallas kernels, on_device(): pl.pallas_call(functools.partial(move_kernel, sz, n_rad), out_shape=[jax....  0.4 us
  transfers between devices with their start and end apart: 2, of which 0 were waited for; matrix products, arithmetic and copies ran while one was open for 0% of the time, Pallas kernels for 16%

profile of v9, /device:TPU:0, one launch (start us, length us, event | category | flops | bytes accessed | tf_op | source)
XLA Modules:
  0.0 11.3 jit_solution(12486576480847328454)
XLA Ops:
  0.6 1.1 %pack.1 = (f32[392,128]{1,0:T(8,128)S(1)}, s32[16,128]{1,0:T(8,128)S(1)}) custom-call(f32[6,2048]{1,0:T(8,128)} %motion_hbm.1, f32[16,128]{1,0:T(8,128)} %bitcast.21, s32[1,32]{1,0:T(1,128)} %bitcast.27, s32[16,128]{1,0:T(8,128)} %bitcast.22, f32[3,16,512]{2,1,0:T(8,128)} %gas_hbm.1, f32[16,512]{1,0:T(8,128)} %pres_hbm.1, s32[2,32]{1,0:T(2,128)} %bitcast.25, ...), custom_call_target="tpu_custom_call" | custom-call | tf_op jit(solution)/shard_map/pack/pallas_call | solution.py:346
  1.7 2.2 %all-gather = f32[784,128]{1,0:T(8,128)S(1)} all-gather(f32[392,128]{1,0:T(8,128)S(1)} %get-tuple-element.17), channel_id=2, replica_groups=mesh['ax'=16,'rad'=2] {'rad'}, dimensions={0}, use_global_device_ids=true | all-gather | bytes 602112 | tf_op jit(solution)/shard_map/all_gather | solution.py:380
  3.9 0.0 copy-start
  3.9 0.4 %move.1 = (f32[224,128]{1,0:T(8,128)S(1)}, f32[16,128]{1,0:T(8,128)S(1)}) custom-call(f32[2,392,128]{2,1,0:T(8,128)S(1)} %bitcast.19, s32[16,128]{1,0:T(8,128)S(1)} %get-tuple-element.18.aux), custom_call_target="tpu_custom_call" | custom-call | flops 4000000000 | bytes 1000000 | tf_op jit(solution)/shard_map/move/pallas_call | solution.py:382
  4.3 0.4 %collective-permute-start.1 = (f32[16,128]{1,0:T(8,128)S(1)}, f32[16,128]{1,0:T(8,128)S(1)}, u32[]{:S(2)}, u32[]{:S(2)}) collective-permute-start(f32[16,128]{1,0:T(8,128)S(1)} %get-tuple-element.21), channel_id=1, source_target_pairs={{0,1},{1,0},{2,4},{3,5},{4,2},{5,3},{6,8},{7,9},{8,6},{9,7},{10,12... | collective-permute-start | bytes 24584 | tf_op jit(solution)/shard_map/ppermute | solution.py:405
  4.8 4.0 %collective-permute-start = (f32[16,128]{1,0:T(8,128)S(1)}, f32[16,128]{1,0:T(8,128)S(1)}, u32[]{:S(2)}, u32[]{:S(2)}) collective-permute-start(f32[16,128]{1,0:T(8,128)S(1)} %get-tuple-element.21), channel_id=1, source_target_pairs={{0,2},{1,3},{2,0},{3,1},{4,6},{5,7},{6,4},{7,5},{8,10},{9,11},{10,... | collective-permute-start | bytes 24584 | tf_op jit(solution)/shard_map/ppermute | solution.py:405
  8.7 0.0 copy-done
  8.7 1.9 %rest.1 = (f32[6,2048]{1,0:T(8,128)}, f32[7,2,32]{2,1,0:T(2,128)}, f32[3,16,512]{2,1,0:T(8,128)}, f32[16,512]{1,0:T(8,128)}, f32[16,512]{1,0:T(8,128)S(1)}) custom-call(f32[2,392,128]{2,1,0:T(8,128)S(1)} %bitcast.20, s32[16,128]{1,0:T(8,128)S(1)} %get-tuple-element.18.aux, f32[8,128,128]{2,1,0:T(8,128)S(1)} %copy-done, f32[224,128]{1,0:T(8,128)S(1)} %get-tuple-element.19.state), custom_call_target="tpu_custom_call" | custom-call | flops 2000000000 | bytes 2000000 | tf_op jit(solution)/shard_map/rest/pallas_call | solution.py:410
  10.6 0.0 collective-permute-done.1.got_b
  10.6 0.0 collective-permute-done.got_a
  10.6 0.7 %finish.1 = (f32[7,2,64]{2,1,0:T(2,128)}, f32[16,512]{1,0:T(8,128)}) custom-call(f32[16,128]{1,0:T(8,128)S(1)} %collective-permute-done.got_a, f32[16,128]{1,0:T(8,128)S(1)} %collective-permute-done.1.got_b, f32[16,512]{1,0:T(8,128)S(1)} %get-tuple-element.22.image), custom_call_target="tpu_custom_call" | custom-call | tf_op jit(solution)/shard_map/finish/pallas_call | solution.py:436
Async XLA Ops:
  3.9 4.8 %copy-start = (f32[8,128,128]{2,1,0:T(8,128)S(1)}, f32[8,128,128]{2,1,0:T(8,128)}, u32[]{:S(2)}) copy-start(f32[8,128,128]{2,1,0:T(8,128)} %table.1) | copy-start | bytes 1572868
  4.3 6.3 %collective-permute-start.1 = (f32[16,128]{1,0:T(8,128)S(1)}, f32[16,128]{1,0:T(8,128)S(1)}, u32[]{:S(2)}, u32[]{:S(2)}) collective-permute-start(f32[16,128]{1,0:T(8,128)S(1)} %get-tuple-element.21), channel_id=1, source_target_pairs={{0,1},{1,0},{2,4},{3,5},{4,2},{5,3},{6,8},{7,9},{8,6},{9,7},{10,12... | collective-permute-start | bytes 24584 | tf_op jit(solution)/shard_map/ppermute | solution.py:405
  4.8 5.9 %collective-permute-start = (f32[16,128]{1,0:T(8,128)S(1)}, f32[16,128]{1,0:T(8,128)S(1)}, u32[]{:S(2)}, u32[]{:S(2)}) collective-permute-start(f32[16,128]{1,0:T(8,128)S(1)} %get-tuple-element.21), channel_id=1, source_target_pairs={{0,2},{1,3},{2,0},{3,1},{4,6},{5,7},{6,4},{7,5},{8,10},{9,11},{10,... | collective-permute-start | bytes 24584 | tf_op jit(solution)/shard_map/ppermute | solution.py:405

commit v10 on v9

--- a/solution.py
+++ b/solution.py
@@ -36,7 +36,8 @@
         self.size = self.motion + 6 * self.tiles
         self.offset = self.size + self.tiles
         self.meta = self.offset + self.tiles
-        self.rows = self.meta + 8
+        self.column = self.meta + 8
+        self.rows = self.column + self.groups
 
 
 def split2(x):
@@ -81,17 +82,22 @@
         copy.wait()
     out[pl.ds(sz.size, sz.tiles), :] = size[...]
     out[pl.ds(sz.offset, sz.tiles), :] = offset[...].astype(F32)
-    out[pl.ds(sz.meta, 1), pl.ds(0, sz.groups)] = block_row(sz, block[...]).astype(F32)
+    numbers = block_row(sz, block[...]).astype(F32)
+    out[pl.ds(sz.meta, 1), pl.ds(0, sz.groups)] = numbers
+    numbers = jnp.concatenate([numbers, jnp.zeros((1, BLOCK - sz.groups), F32)], axis=1)
+    out[pl.ds(sz.column, sz.groups), :] = jnp.transpose(jnp.broadcast_to(numbers, (BLOCK, BLOCK)))[: sz.groups]
     width = radial.shape[1]
     lane = iota((1, width), 1)
     for slot in range(2):
         kept = jnp.where(lane < counts[0, 2 + slot], radial[slot : slot + 1, :], -1)
         out[pl.ds(sz.meta + 1 + slot, 1), pl.ds(0, width)] = kept.astype(F32)
     index = kinds[...] * (n_rad * sz.blocks) + block_row(sz, cols[...])
-    aux[pl.ds(0, index.shape[0]), :] = jnp.concatenate([index, index], axis=1)
+    index = jnp.concatenate([index, index], axis=1).astype(F32)
+    index = jnp.concatenate([index, jnp.zeros((BLOCK - index.shape[0], BLOCK), F32)], axis=0)
+    aux[pl.ds(8, sz.blocks), :] = jnp.transpose(index)[: sz.blocks].astype(I32)
     lane = iota((1, axial.shape[1]), 1)
     kept = [jnp.where(lane < counts[0, slot], axial[slot : slot + 1, :], -1) for slot in range(2)]
-    aux[pl.ds(8, 1), :] = jnp.concatenate(kept, axis=1)
+    aux[pl.ds(0, 1), :] = jnp.concatenate(kept, axis=1)
     motion_copy, pres_copy, *gas_copies = copies[len(small) :]
     motion_copy.wait()
     for i in range(sz.tiles):
@@ -132,10 +138,7 @@
     slab_blocks = n_rad * blocks
     T = n_rad * tiles
 
-    block_rows = [G[d, pl.ds(sz.meta, 1), :] for d in range(n_rad)]
-    column = jnp.concatenate(
-        [jnp.transpose(jnp.broadcast_to(b, (BLOCK, BLOCK)))[:groups] for b in block_rows], axis=0
-    ).astype(I32)
+    column = jnp.concatenate([G[d, pl.ds(sz.column, groups), :] for d in range(n_rad)], axis=0).astype(I32)
     lanes = iota((n_rad * groups, BLOCK), 1)
     chooser = jnp.concatenate(
         [(column == lanes + first).astype(F32).astype(BF16) for first in range(0, slab_blocks, BLOCK)], axis=1
@@ -167,7 +170,7 @@
         state[pl.ds((3 + c) * T, T), :] = new
     state[pl.ds(6 * T, T), :] = size
 
-    payload = pick(sz, state_of(sz, T, state, r), aux[pl.ds(8, 1), :])
+    payload = pick(sz, state_of(sz, T, state, r), aux[pl.ds(0, 1), :])
     for c in range(7):
         message[c : c + 1, :] = payload[c]
     message[7:8, :] = jnp.zeros((1, BLOCK), F32)
@@ -246,22 +249,23 @@
         send.start()
 
     pres = jnp.concatenate([G[d, pl.ds(sz.pres, blocks), :] for d in range(n_rad)], axis=0)
-    index = [jnp.broadcast_to(aux[pl.ds(k, 1), :], (BLOCK, BLOCK)).astype(jnp.int16) for k in range(4)]
-    left, right = [], []
-    for first in range(0, slab_blocks, BLOCK):
-        p_high, p_low = split2(jnp.transpose(pres[first : first + BLOCK]))
-        here = iota((BLOCK, BLOCK), 0) + first + jnp.where(iota((BLOCK, BLOCK), 1) < blocks, 0, slab_blocks)
-        counts = []
-        for j in range(NT // 2):
-            aim = (here + 2 * j * slab_blocks).astype(jnp.int16)
-            count = none
-            for k in range(4):
+    index = [
+        jnp.broadcast_to(aux[pl.ds(8, blocks), k : k + 1], (blocks, BLOCK)).astype(jnp.int16) for k in range(4)
+    ]
+    one, none = jnp.ones((blocks, BLOCK), BF16), jnp.zeros((blocks, BLOCK), BF16)
+    lanes = iota((blocks, BLOCK), 1)
+    counts = []
+    for t in range(NT):
+        row = []
+        for first in range(0, slab_blocks, BLOCK):
+            aim = (lanes + (t * slab_blocks + first)).astype(jnp.int16)
+            count = jnp.where(aim == index[0], one, none)
+            for k in range(1, 4):
                 count = count + jnp.where(aim == index[k], one, none)
-            counts.append(count)
-        counts = jnp.concatenate(counts, axis=1)
-        left += [p_high, p_low]
-        right += [counts, counts]
-    grouped = dot(jnp.concatenate(left, axis=1), jnp.concatenate(right, axis=0))
+            row.append(count)
+        counts.append(jnp.concatenate(row, axis=1))
+    grouped = dot(jnp.concatenate(counts, axis=0), jnp.concatenate(split2(pres), axis=1))
+    grouped = grouped[:, :BLOCK] + grouped[:, BLOCK:]
     mine = pl.multiple_of(r * tiles, tiles)
     for i in range(tiles):
         motion_out[:, i * BLOCK : (i + 1) * BLOCK] = state[pl.ds(mine + i, 6, stride=T), :]
@@ -275,21 +279,10 @@
             arr_rad[c, slot : slot + 1, :] = got[c][:, :width]
     sends[1].start()
 
-    g_high, g_low = split2(
-        jnp.concatenate([grouped[:, j * BLOCK : (j + 1) * BLOCK] for j in range(NT // 2)], axis=0)
-    )
-    t_high, t_low = split2(
-        jnp.concatenate(
-            [jnp.concatenate([table[2 * j + s] for j in range(NT // 2)], axis=1) for s in range(2)], axis=0
-        )
-    )
-    sums = dot(
-        jnp.concatenate([t_high, t_low, t_high], axis=1), jnp.concatenate([g_high, g_high, g_low], axis=0)
-    )
-    sums = [sums[:BLOCK], sums[BLOCK:]]
-    both = jnp.where(iota((BLOCK, BLOCK), 1) < blocks, sums[0], sums[1])
-    both = both + pltpu.roll(jnp.where(iota((BLOCK, BLOCK), 1) < blocks, 0.0, sums[1]), blocks, 1)
-    coup[...] = jnp.transpose(both)
+    grouped = jnp.concatenate([grouped[t * blocks : (t + 1) * blocks] for t in range(NT)], axis=1)
+    matrices = jnp.concatenate([table[t] for t in range(NT)], axis=1)
+    sums = dot_nt(jnp.concatenate(split2(grouped), axis=0), jnp.concatenate(split2(matrices), axis=0))
+    coup[...] = sums[:blocks, :BLOCK] + sums[:blocks, BLOCK:] + sums[blocks:, :BLOCK]
     layer = iota((layers, BLOCK), 0)
     for q in range(sz.quarters):
         p = G[r, pl.ds(sz.pres + q * layers, layers), :]
@@ -347,7 +340,7 @@
         functools.partial(pack_kernel, sz, n_rad),
         out_shape=[
             jax.ShapeDtypeStruct((sz.rows, BLOCK), F32),
-            jax.ShapeDtypeStruct((16, BLOCK), I32),
+            jax.ShapeDtypeStruct((8 + sz.blocks, BLOCK), I32),
         ],
         in_specs=[hbm] * 11,
         out_specs=[vmem] * 2,
@@ -421,7 +414,7 @@
         scratch_shapes=[
             pltpu.VMEM((16 * T, BLOCK), F32),
             pltpu.VMEM((4 * 2 * T, BLOCK), F32),
-            pltpu.VMEM((BLOCK, BLOCK), F32),
+            pltpu.VMEM((sz.blocks, BLOCK), F32),
             pltpu.VMEM((6, parcels), F32),
             pltpu.VMEM((7, 2, cap_rad), F32),
             pltpu.VMEM(gas_velocity.shape, F32),

time: 11.5 us -> 11.3 us (0.983)
  Pallas kernels: 4.05 us -> 3.82 us
    pallas_call x1, Pallas kernels: 1.86 us -> 1.67 us  [on_device(): pl.pallas_call(functools.partial(rest_kernel, sz, n_rad), out_shape=[jax....]
  transfers between devices with their start and end apart: 2 -> 2, of which waited for: 0 -> 0; matrix products, arithmetic and copies ran while one was open for 0% -> 0% of each run, Pallas kernels for 16% -> 15%
where the time goes in v10:
time: 11.3 us; the launch traced here: 11.1 us
  starting transfers between devices  4.42 us (39%)
  Pallas kernels  3.82 us (34%)
  blocking collectives  2.2 us (19%)
  between operations  0.67 us (6%)
    ppermute x2, starting transfers between devices, exchange(): return lax.ppermute(message, ('ax', 'rad'), list(enumerate(to)))  4.42 us
    all_gather x1, blocking collectives, on_device(): gathered = lax.all_gather(packed, 'rad', axis=0)  2.2 us
    pallas_call x1, Pallas kernels, on_device(): pl.pallas_call(functools.partial(rest_kernel, sz, n_rad), out_shape=[jax....  1.67 us
    pallas_call x1, Pallas kernels, on_device(): pl.pallas_call(functools.partial(pack_kernel, sz, n_rad), out_shape=[jax....  1.12 us
    pallas_call x1, Pallas kernels, on_device(): pl.pallas_call(functools.partial(finish_kernel, sz, n_ax), out_shape=[jax...  0.69 us
    pallas_call x1, Pallas kernels, on_device(): pl.pallas_call(functools.partial(move_kernel, sz, n_rad), out_shape=[jax....  0.35 us
  transfers between devices with their start and end apart: 2, of which 0 were waited for; matrix products, arithmetic and copies ran while one was open for 0% of the time, Pallas kernels for 15%

profile of v10, /device:TPU:0, one launch (start us, length us, event | category | flops | bytes accessed | tf_op | source)
XLA Modules:
  0.0 11.1 jit_solution(7170579232820991050)
XLA Ops:
  0.6 1.1 %pack.1 = (f32[424,128]{1,0:T(8,128)S(1)}, s32[72,128]{1,0:T(8,128)S(1)}) custom-call(f32[6,2048]{1,0:T(8,128)} %motion_hbm.1, f32[16,128]{1,0:T(8,128)} %bitcast.21, s32[1,32]{1,0:T(1,128)} %bitcast.27, s32[16,128]{1,0:T(8,128)} %bitcast.22, f32[3,16,512]{2,1,0:T(8,128)} %gas_hbm.1, f32[16,512]{1,0:T(8,128)} %pres_hbm.1, s32[2,32]{1,0:T(2,128)} %bitcast.25, ...), custom_call_target="tpu_custom_call" | custom-call | tf_op jit(solution)/shard_map/pack/pallas_call | solution.py:339
  1.8 2.2 %all-gather = f32[848,128]{1,0:T(8,128)S(1)} all-gather(f32[424,128]{1,0:T(8,128)S(1)} %get-tuple-element.17), channel_id=2, replica_groups=mesh['ax'=16,'rad'=2] {'rad'}, dimensions={0}, use_global_device_ids=true | all-gather | bytes 651264 | tf_op jit(solution)/shard_map/all_gather | solution.py:373
  4.0 0.0 copy-start
  4.0 0.4 %move.1 = (f32[224,128]{1,0:T(8,128)S(1)}, f32[16,128]{1,0:T(8,128)S(1)}) custom-call(f32[2,424,128]{2,1,0:T(8,128)S(1)} %bitcast.19, s32[72,128]{1,0:T(8,128)S(1)} %get-tuple-element.18.aux), custom_call_target="tpu_custom_call" | custom-call | flops 4000000000 | bytes 1000000 | tf_op jit(solution)/shard_map/move/pallas_call | solution.py:375
  4.3 0.4 %collective-permute-start.1 = (f32[16,128]{1,0:T(8,128)S(1)}, f32[16,128]{1,0:T(8,128)S(1)}, u32[]{:S(2)}, u32[]{:S(2)}) collective-permute-start(f32[16,128]{1,0:T(8,128)S(1)} %get-tuple-element.21), channel_id=1, source_target_pairs={{0,1},{1,0},{2,4},{3,5},{4,2},{5,3},{6,8},{7,9},{8,6},{9,7},{10,12... | collective-permute-start | bytes 24584 | tf_op jit(solution)/shard_map/ppermute | solution.py:398
  4.8 4.0 %collective-permute-start = (f32[16,128]{1,0:T(8,128)S(1)}, f32[16,128]{1,0:T(8,128)S(1)}, u32[]{:S(2)}, u32[]{:S(2)}) collective-permute-start(f32[16,128]{1,0:T(8,128)S(1)} %get-tuple-element.21), channel_id=1, source_target_pairs={{0,2},{1,3},{2,0},{3,1},{4,6},{5,7},{6,4},{7,5},{8,10},{9,11},{10,... | collective-permute-start | bytes 24584 | tf_op jit(solution)/shard_map/ppermute | solution.py:398
  8.7 0.0 copy-done
  8.7 1.7 %rest.1 = (f32[6,2048]{1,0:T(8,128)}, f32[7,2,32]{2,1,0:T(2,128)}, f32[3,16,512]{2,1,0:T(8,128)}, f32[16,512]{1,0:T(8,128)}, f32[16,512]{1,0:T(8,128)S(1)}) custom-call(f32[2,424,128]{2,1,0:T(8,128)S(1)} %bitcast.20, s32[72,128]{1,0:T(8,128)S(1)} %get-tuple-element.18.aux, f32[8,128,128]{2,1,0:T(8,128)S(1)} %copy-done, f32[224,128]{1,0:T(8,128)S(1)} %get-tuple-element.19.state), custom_call_target="tpu_custom_call" | custom-call | flops 2000000000 | bytes 2000000 | tf_op jit(solution)/shard_map/rest/pallas_call | solution.py:403
  10.4 0.0 collective-permute-done.1.got_b
  10.4 0.0 collective-permute-done.got_a
  10.4 0.7 %finish.1 = (f32[7,2,64]{2,1,0:T(2,128)}, f32[16,512]{1,0:T(8,128)}) custom-call(f32[16,128]{1,0:T(8,128)S(1)} %collective-permute-done.got_a, f32[16,128]{1,0:T(8,128)S(1)} %collective-permute-done.1.got_b, f32[16,512]{1,0:T(8,128)S(1)} %get-tuple-element.22.image), custom_call_target="tpu_custom_call" | custom-call | tf_op jit(solution)/shard_map/finish/pallas_call | solution.py:429
Async XLA Ops:
  4.0 4.8 %copy-start = (f32[8,128,128]{2,1,0:T(8,128)S(1)}, f32[8,128,128]{2,1,0:T(8,128)}, u32[]{:S(2)}) copy-start(f32[8,128,128]{2,1,0:T(8,128)} %table.1) | copy-start | bytes 1572868
  4.3 6.1 %collective-permute-start.1 = (f32[16,128]{1,0:T(8,128)S(1)}, f32[16,128]{1,0:T(8,128)S(1)}, u32[]{:S(2)}, u32[]{:S(2)}) collective-permute-start(f32[16,128]{1,0:T(8,128)S(1)} %get-tuple-element.21), channel_id=1, source_target_pairs={{0,1},{1,0},{2,4},{3,5},{4,2},{5,3},{6,8},{7,9},{8,6},{9,7},{10,12... | collective-permute-start | bytes 24584 | tf_op jit(solution)/shard_map/ppermute | solution.py:398
  4.8 5.7 %collective-permute-start = (f32[16,128]{1,0:T(8,128)S(1)}, f32[16,128]{1,0:T(8,128)S(1)}, u32[]{:S(2)}, u32[]{:S(2)}) collective-permute-start(f32[16,128]{1,0:T(8,128)S(1)} %get-tuple-element.21), channel_id=1, source_target_pairs={{0,2},{1,3},{2,0},{3,1},{4,6},{5,7},{6,4},{7,5},{8,10},{9,11},{10,... | collective-permute-start | bytes 24584 | tf_op jit(solution)/shard_map/ppermute | solution.py:398

commit v11 on v10

--- a/solution.py
+++ b/solution.py
@@ -63,14 +63,13 @@
 
 
 def pack_kernel(
-    sz, n_rad, motion_hbm, size_hbm, block_hbm, offset_hbm, gas_hbm, pres_hbm, radial_hbm, counts_hbm, cols_hbm,
-    kinds_hbm, axial_hbm,
+    sz, n_rad, motion_hbm, size_hbm, block_hbm, offset_hbm, gas_hbm, pres_hbm, radial_hbm, counts_hbm, axial_hbm,
     out, aux,
-    motion, size, block, offset, gas, pres, radial, counts, cols, kinds, axial, sem,
+    motion, size, block, offset, gas, pres, radial, counts, axial, sem,
 ):
     small = (
-        (counts_hbm, counts), (block_hbm, block), (radial_hbm, radial), (axial_hbm, axial), (cols_hbm, cols),
-        (kinds_hbm, kinds), (offset_hbm, offset), (size_hbm, size),
+        (counts_hbm, counts), (block_hbm, block), (radial_hbm, radial), (axial_hbm, axial), (offset_hbm, offset),
+        (size_hbm, size),
     )
     large = ((motion_hbm, motion), (pres_hbm, pres), *((gas_hbm.at[c], gas.at[c]) for c in range(3)))
     copies = [pltpu.make_async_copy(src, dst, sem.at[i]) for i, (src, dst) in enumerate(small + large)]
@@ -91,10 +90,6 @@
     for slot in range(2):
         kept = jnp.where(lane < counts[0, 2 + slot], radial[slot : slot + 1, :], -1)
         out[pl.ds(sz.meta + 1 + slot, 1), pl.ds(0, width)] = kept.astype(F32)
-    index = kinds[...] * (n_rad * sz.blocks) + block_row(sz, cols[...])
-    index = jnp.concatenate([index, index], axis=1).astype(F32)
-    index = jnp.concatenate([index, jnp.zeros((BLOCK - index.shape[0], BLOCK), F32)], axis=0)
-    aux[pl.ds(8, sz.blocks), :] = jnp.transpose(index)[: sz.blocks].astype(I32)
     lane = iota((1, axial.shape[1]), 1)
     kept = [jnp.where(lane < counts[0, slot], axial[slot : slot + 1, :], -1) for slot in range(2)]
     aux[pl.ds(0, 1), :] = jnp.concatenate(kept, axis=1)
@@ -181,11 +176,17 @@
 
 
 def rest_kernel(
-    sz, n_rad, G, aux, table, state,
+    sz, n_rad, G, cols_hbm, kinds_hbm, table, state,
     motion_hbm, arr_hbm, gas_hbm, liquid_hbm, image,
-    deps, spread, coup, motion_out, arr_rad, gas_out, liquid, sem,
+    deps, spread, coup, motion_out, arr_rad, gas_out, liquid, cols, kinds, sem,
 ):
     r = lax.axis_index("rad")
+    loads = [
+        pltpu.make_async_copy(cols_hbm, cols, sem.at[6]),
+        pltpu.make_async_copy(kinds_hbm, kinds, sem.at[7]),
+    ]
+    for load in loads:
+        load.start()
     sends = [
         pltpu.make_async_copy(src, dst, sem.at[i])
         for i, (src, dst) in enumerate(
@@ -248,10 +249,15 @@
     for send in sends[2:]:
         send.start()
 
+    for load in loads:
+        load.wait()
+
     pres = jnp.concatenate([G[d, pl.ds(sz.pres, blocks), :] for d in range(n_rad)], axis=0)
-    index = [
-        jnp.broadcast_to(aux[pl.ds(8, blocks), k : k + 1], (blocks, BLOCK)).astype(jnp.int16) for k in range(4)
-    ]
+    index = kinds[...] * slab_blocks + block_row(sz, cols[...])
+    index = jnp.concatenate([index, index], axis=1).astype(F32)
+    index = jnp.concatenate([index, jnp.zeros((BLOCK - index.shape[0], BLOCK), F32)], axis=0)
+    index = jnp.transpose(index)[:blocks].astype(I32)
+    index = [jnp.broadcast_to(index[:, k : k + 1], (blocks, BLOCK)).astype(jnp.int16) for k in range(4)]
     one, none = jnp.ones((blocks, BLOCK), BF16), jnp.zeros((blocks, BLOCK), BF16)
     lanes = iota((blocks, BLOCK), 1)
     counts = []
@@ -295,20 +301,27 @@
         send.wait()
 
 
-def finish_kernel(sz, n_ax, got_a, got_b, image, arr_ax, pressure_image):
+def finish_kernel(sz, n_ax, got_a, got_b, image, arr_hbm, pressure_hbm, arr_ax, pressure_image, sem):
+    sends = [pltpu.make_async_copy(arr_ax, arr_hbm, sem.at[sz.quarters])]
     a = lax.axis_index("ax")
     even = a % 2 == 0
     low = jnp.where(a > 0, jnp.where(even, got_b[...], got_a[...]), 0.0)
     up = jnp.where(a < n_ax - 1, jnp.where(even, got_a[...], got_b[...]), 0.0)
+    last = sz.layers - 1
+    layer = iota((sz.layers, BLOCK), 0)
+    for q in range(sz.quarters):
+        at = slice(q * BLOCK, (q + 1) * BLOCK)
+        edge = jnp.where(layer == 0, low[8 + q : 9 + q, :], jnp.where(layer == last, up[12 + q : 13 + q, :], 0.0))
+        pressure_image[:, at] = image[:, at] - edge
+        sends.append(pltpu.make_async_copy(pressure_image.at[:, at], pressure_hbm.at[:, at], sem.at[q]))
+    for send in sends[1:]:
+        send.start()
     half = arr_ax.shape[2]
     arr_ax[:, 0, :] = low[0:7, 0:half]
     arr_ax[:, 1, :] = up[0:7, half : 2 * half]
-    pressure_image[...] = image[...]
-    last = sz.layers - 1
-    for q in range(sz.quarters):
-        at = slice(q * BLOCK, (q + 1) * BLOCK)
-        pressure_image[0:1, at] = image[0:1, at] - low[8 + q : 9 + q, :]
-        pressure_image[last : last + 1, at] = image[last : last + 1, at] - up[12 + q : 13 + q, :]
+    sends[0].start()
+    for send in sends:
+        send.wait()
 
 
 def on_device(
@@ -340,9 +353,9 @@
         functools.partial(pack_kernel, sz, n_rad),
         out_shape=[
             jax.ShapeDtypeStruct((sz.rows, BLOCK), F32),
-            jax.ShapeDtypeStruct((8 + sz.blocks, BLOCK), I32),
-        ],
-        in_specs=[hbm] * 11,
+            jax.ShapeDtypeStruct((8, BLOCK), I32),
+        ],
+        in_specs=[hbm] * 9,
         out_specs=[vmem] * 2,
         scratch_shapes=[
             pltpu.VMEM(parcel_motion.shape, F32),
@@ -353,10 +366,8 @@
             pltpu.VMEM(pressure.shape, F32),
             pltpu.VMEM((2, cap_rad), I32),
             pltpu.SMEM((1, 4), I32),
-            pltpu.VMEM((4, sz.blocks), I32),
-            pltpu.VMEM((4, sz.blocks), I32),
             pltpu.VMEM((2, cap_ax), I32),
-            pltpu.SemaphoreType.DMA((13,)),
+            pltpu.SemaphoreType.DMA((11,)),
         ],
         compiler_params=params,
         name="pack",
@@ -365,8 +376,7 @@
             pltpu.with_memory_space_constraint(x, pltpu.HBM)
             for x in (
                 parcel_motion, size2, parcel_block.reshape(1, sz.groups), offset2, gas_velocity, pressure,
-                send_radial.reshape(2, cap_rad), counts, block_cols[0].T, block_kinds[0].T,
-                send_axial.reshape(2, cap_ax),
+                send_radial.reshape(2, cap_rad), counts, send_axial.reshape(2, cap_ax),
             )
         )
     )
@@ -409,7 +419,7 @@
             jax.ShapeDtypeStruct(pressure.shape, F32),
             jax.ShapeDtypeStruct(pressure.shape, F32),
         ],
-        in_specs=[vmem] * 4,
+        in_specs=[vmem, hbm, hbm, vmem, vmem],
         out_specs=[hbm] * 4 + [vmem],
         scratch_shapes=[
             pltpu.VMEM((16 * T, BLOCK), F32),
@@ -419,12 +429,20 @@
             pltpu.VMEM((7, 2, cap_rad), F32),
             pltpu.VMEM(gas_velocity.shape, F32),
             pltpu.VMEM(pressure.shape, F32),
-            pltpu.SemaphoreType.DMA((6,)),
+            pltpu.VMEM((4, sz.blocks), I32),
+            pltpu.VMEM((4, sz.blocks), I32),
+            pltpu.SemaphoreType.DMA((8,)),
         ],
         compiler_params=params,
         cost_estimate=pl.CostEstimate(flops=2_000_000_000, bytes_accessed=2_000_000, transcendentals=0),
         name="rest",
-    )(gathered, aux, block_table, state)
+    )(
+        gathered,
+        pltpu.with_memory_space_constraint(block_cols[0].T, pltpu.HBM),
+        pltpu.with_memory_space_constraint(block_kinds[0].T, pltpu.HBM),
+        block_table,
+        state,
+    )
 
     arr_ax, pressure_image = pl.pallas_call(
         functools.partial(finish_kernel, sz, n_ax),
@@ -433,7 +451,12 @@
             jax.ShapeDtypeStruct(pressure.shape, F32),
         ],
         in_specs=[vmem] * 3,
-        out_specs=[vmem] * 2,
+        out_specs=[hbm] * 2,
+        scratch_shapes=[
+            pltpu.VMEM((7, 2, cap_ax), F32),
+            pltpu.VMEM(pressure.shape, F32),
+            pltpu.SemaphoreType.DMA((sz.quarters + 1,)),
+        ],
         compiler_params=params,
         name="finish",
     )(got_a, got_b, image)

time: 11.3 us -> 11.8 us (1.044)
  Pallas kernels: 3.82 us -> 4.26 us
    pallas_call x1, Pallas kernels: 1.67 us -> 2.11 us  [on_device(): pl.pallas_call(functools.partial(rest_kernel, sz, n_rad), out_shape=[jax....]
  transfers between devices with their start and end apart: 2 -> 2, of which waited for: 0 -> 0; matrix products, arithmetic and copies ran while one was open for 0% -> 0% of each run, Pallas kernels for 15% -> 18%
where the time goes in v11:
time: 11.8 us; the launch traced here: 11.6 us
  starting transfers between devices  4.41 us (37%)
  Pallas kernels  4.26 us (36%)
  blocking collectives  2.2 us (19%)
  between operations  0.68 us (6%)
    ppermute x2, starting transfers between devices, exchange(): return lax.ppermute(message, ('ax', 'rad'), list(enumerate(to)))  4.41 us
    all_gather x1, blocking collectives, on_device(): gathered = lax.all_gather(packed, 'rad', axis=0)  2.2 us
    pallas_call x1, Pallas kernels, on_device(): pl.pallas_call(functools.partial(rest_kernel, sz, n_rad), out_shape=[jax....  2.11 us
    pallas_call x1, Pallas kernels, on_device(): pl.pallas_call(functools.partial(pack_kernel, sz, n_rad), out_shape=[jax....  1.05 us
    pallas_call x1, Pallas kernels, on_device(): pl.pallas_call(functools.partial(finish_kernel, sz, n_ax), out_shape=[jax...  0.74 us
    pallas_call x1, Pallas kernels, on_device(): pl.pallas_call(functools.partial(move_kernel, sz, n_rad), out_shape=[jax....  0.35 us
  transfers between devices with their start and end apart: 2, of which 0 were waited for; matrix products, arithmetic and copies ran while one was open for 0% of the time, Pallas kernels for 18%

profile of v11, /device:TPU:0, one launch (start us, length us, event | category | flops | bytes accessed | tf_op | source)
XLA Modules:
  0.0 11.6 jit_solution(4536369917377135190)
XLA Ops:
  0.6 1.1 %pack.1 = (f32[424,128]{1,0:T(8,128)S(1)}, s32[8,128]{1,0:T(8,128)S(1)}) custom-call(f32[6,2048]{1,0:T(8,128)} %motion_hbm.1, f32[16,128]{1,0:T(8,128)} %bitcast.21, s32[1,32]{1,0:T(1,128)} %bitcast.25, s32[16,128]{1,0:T(8,128)} %bitcast.22, f32[3,16,512]{2,1,0:T(8,128)} %gas_hbm.1, f32[16,512]{1,0:T(8,128)} %pres_hbm.1, s32[2,32]{1,0:T(2,128)} %bitcast.23, ...), custom_call_target="tpu_custom_call" | custom-call | tf_op jit(solution)/shard_map/pack/pallas_call | solution.py:352
  1.7 2.2 %all-gather = f32[848,128]{1,0:T(8,128)S(1)} all-gather(f32[424,128]{1,0:T(8,128)S(1)} %get-tuple-element.17), channel_id=2, replica_groups=mesh['ax'=16,'rad'=2] {'rad'}, dimensions={0}, use_global_device_ids=true | all-gather | bytes 651264 | tf_op jit(solution)/shard_map/all_gather | solution.py:383
  3.9 0.0 copy-start
  3.9 0.4 %move.1 = (f32[224,128]{1,0:T(8,128)S(1)}, f32[16,128]{1,0:T(8,128)S(1)}) custom-call(f32[2,424,128]{2,1,0:T(8,128)S(1)} %bitcast.19, s32[8,128]{1,0:T(8,128)S(1)} %get-tuple-element.18.aux), custom_call_target="tpu_custom_call" | custom-call | flops 4000000000 | bytes 1000000 | tf_op jit(solution)/shard_map/move/pallas_call | solution.py:385
  4.3 0.4 %collective-permute-start.1 = (f32[16,128]{1,0:T(8,128)S(1)}, f32[16,128]{1,0:T(8,128)S(1)}, u32[]{:S(2)}, u32[]{:S(2)}) collective-permute-start(f32[16,128]{1,0:T(8,128)S(1)} %get-tuple-element.21), channel_id=1, source_target_pairs={{0,1},{1,0},{2,4},{3,5},{4,2},{5,3},{6,8},{7,9},{8,6},{9,7},{10,12... | collective-permute-start | bytes 24584 | tf_op jit(solution)/shard_map/ppermute | solution.py:408
  4.7 4.0 %collective-permute-start = (f32[16,128]{1,0:T(8,128)S(1)}, f32[16,128]{1,0:T(8,128)S(1)}, u32[]{:S(2)}, u32[]{:S(2)}) collective-permute-start(f32[16,128]{1,0:T(8,128)S(1)} %get-tuple-element.21), channel_id=1, source_target_pairs={{0,2},{1,3},{2,0},{3,1},{4,6},{5,7},{6,4},{7,5},{8,10},{9,11},{10,... | collective-permute-start | bytes 24584 | tf_op jit(solution)/shard_map/ppermute | solution.py:408
  8.7 0.0 copy-done
  8.7 2.1 %rest.1 = (f32[6,2048]{1,0:T(8,128)}, f32[7,2,32]{2,1,0:T(2,128)}, f32[3,16,512]{2,1,0:T(8,128)}, f32[16,512]{1,0:T(8,128)}, f32[16,512]{1,0:T(8,128)S(1)}) custom-call(f32[2,424,128]{2,1,0:T(8,128)S(1)} %bitcast.20, s32[4,64]{1,0:T(4,128)} %bitcast.28, s32[4,64]{1,0:T(4,128)} %bitcast.29, f32[8,128,128]{2,1,0:T(8,128)S(1)} %copy-done, ...), custom_call_target="tpu_custom_call" | custom-call | flops 2000000000 | bytes 2000000 | tf_op jit(solution)/shard_map/rest/pallas_call | solution.py:413
  10.8 0.0 collective-permute-done.1.got_b
  10.8 0.0 collective-permute-done.got_a
  10.8 0.7 %finish.1 = (f32[7,2,64]{2,1,0:T(2,128)}, f32[16,512]{1,0:T(8,128)}) custom-call(f32[16,128]{1,0:T(8,128)S(1)} %collective-permute-done.got_a, f32[16,128]{1,0:T(8,128)S(1)} %collective-permute-done.1.got_b, f32[16,512]{1,0:T(8,128)S(1)} %get-tuple-element.22.image), custom_call_target="tpu_custom_call" | custom-call | tf_op jit(solution)/shard_map/finish/pallas_call | solution.py:447
Async XLA Ops:
  3.9 4.8 %copy-start = (f32[8,128,128]{2,1,0:T(8,128)S(1)}, f32[8,128,128]{2,1,0:T(8,128)}, u32[]{:S(2)}) copy-start(f32[8,128,128]{2,1,0:T(8,128)} %table.1) | copy-start | bytes 1572868
  4.3 6.5 %collective-permute-start.1 = (f32[16,128]{1,0:T(8,128)S(1)}, f32[16,128]{1,0:T(8,128)S(1)}, u32[]{:S(2)}, u32[]{:S(2)}) collective-permute-start(f32[16,128]{1,0:T(8,128)S(1)} %get-tuple-element.21), channel_id=1, source_target_pairs={{0,1},{1,0},{2,4},{3,5},{4,2},{5,3},{6,8},{7,9},{8,6},{9,7},{10,12... | collective-permute-start | bytes 24584 | tf_op jit(solution)/shard_map/ppermute | solution.py:408
  4.7 6.1 %collective-permute-start = (f32[16,128]{1,0:T(8,128)S(1)}, f32[16,128]{1,0:T(8,128)S(1)}, u32[]{:S(2)}, u32[]{:S(2)}) collective-permute-start(f32[16,128]{1,0:T(8,128)S(1)} %get-tuple-element.21), channel_id=1, source_target_pairs={{0,2},{1,3},{2,0},{3,1},{4,6},{5,7},{6,4},{7,5},{8,10},{9,11},{10,... | collective-permute-start | bytes 24584 | tf_op jit(solution)/shard_map/ppermute | solution.py:408

commit v12 on v10

--- a/solution.py
+++ b/solution.py
@@ -132,7 +132,7 @@
     return [state[pl.ds(c * T + first, sz.tiles), :] for c in range(7)]
 
 
-def move_kernel(sz, n_rad, G, aux, state, message, near):
+def move_kernel(sz, n_rad, G, aux, state, message_a, message_b, near):
     r = lax.axis_index("rad")
     layers, tiles, blocks, groups = sz.layers, sz.tiles, sz.blocks, sz.groups
     slab_blocks = n_rad * blocks
@@ -171,13 +171,23 @@
     state[pl.ds(6 * T, T), :] = size
 
     payload = pick(sz, state_of(sz, T, state, r), aux[pl.ds(0, 1), :])
-    for c in range(7):
-        message[c : c + 1, :] = payload[c]
-    message[7:8, :] = jnp.zeros((1, BLOCK), F32)
+    payload = jnp.concatenate([*payload, jnp.zeros((1, BLOCK), F32)], axis=0)
+    turned = pltpu.roll(payload, BLOCK // 2, 1)
+    first_half = iota((1, BLOCK), 1) < BLOCK // 2
+    even = lax.axis_index("ax") % 2 == 0
     for q in range(sz.quarters):
         first = sz.pres + q * layers
-        message[8 + q : 9 + q, :] = G[r, pl.ds(first + layers - 1, 1), :]
-        message[12 + q : 13 + q, :] = G[r, pl.ds(first, 1), :]
+        up = G[r, pl.ds(first + layers - 1, 1), :]
+        down = G[r, pl.ds(first, 1), :]
+        message_a[q : q + 1, :] = jnp.where(even, up, down)
+        message_b[q : q + 1, :] = jnp.where(even, down, up)
+    for i in range(4):
+        here = [x[2 * i : 2 * i + 1] for x in (payload, turned)]
+        then = [x[2 * i + 1 : 2 * i + 2] for x in (payload, turned)]
+        up = jnp.where(first_half, here[0], then[1])
+        down = jnp.where(first_half, here[1], then[0])
+        message_a[4 + i : 5 + i, :] = jnp.where(even, up, down)
+        message_b[4 + i : 5 + i, :] = jnp.where(even, down, up)
 
 
 def rest_kernel(
@@ -301,14 +311,16 @@
     low = jnp.where(a > 0, jnp.where(even, got_b[...], got_a[...]), 0.0)
     up = jnp.where(a < n_ax - 1, jnp.where(even, got_a[...], got_b[...]), 0.0)
     half = arr_ax.shape[2]
-    arr_ax[:, 0, :] = low[0:7, 0:half]
-    arr_ax[:, 1, :] = up[0:7, half : 2 * half]
+    for slot, got in enumerate((low, up)):
+        pair = (got, pltpu.roll(got, BLOCK // 2, 1))
+        for c in range(7):
+            arr_ax[c, slot : slot + 1, :] = pair[c % 2][4 + c // 2 : 5 + c // 2, :half]
     pressure_image[...] = image[...]
     last = sz.layers - 1
     for q in range(sz.quarters):
         at = slice(q * BLOCK, (q + 1) * BLOCK)
-        pressure_image[0:1, at] = image[0:1, at] - low[8 + q : 9 + q, :]
-        pressure_image[last : last + 1, at] = image[last : last + 1, at] - up[12 + q : 13 + q, :]
+        pressure_image[0:1, at] = image[0:1, at] - low[q : q + 1, :]
+        pressure_image[last : last + 1, at] = image[last : last + 1, at] - up[q : q + 1, :]
 
 
 def on_device(
@@ -372,21 +384,22 @@
     )
     gathered = lax.all_gather(packed, "rad", axis=0)
 
-    state, message = pl.pallas_call(
+    state, message_a, message_b = pl.pallas_call(
         functools.partial(move_kernel, sz, n_rad),
         out_shape=[
             jax.ShapeDtypeStruct((7 * T, BLOCK), F32),
-            jax.ShapeDtypeStruct((16, BLOCK), F32),
+            jax.ShapeDtypeStruct((8, BLOCK), F32),
+            jax.ShapeDtypeStruct((8, BLOCK), F32),
         ],
         in_specs=[vmem] * 2,
-        out_specs=[vmem] * 2,
+        out_specs=[vmem] * 3,
         scratch_shapes=[pltpu.VMEM((3, n_rad * sz.groups, BLOCK), F32)],
         compiler_params=params,
         cost_estimate=pl.CostEstimate(flops=4_000_000_000, bytes_accessed=1_000_000, transcendentals=0),
         name="move",
     )(gathered, aux)
 
-    def exchange(first):
+    def exchange(message, first):
         to = list(range(n_ax * n_rad))
         for low in range(first, n_ax - 1, 2):
             for r in range(n_rad):
@@ -397,8 +410,8 @@
             to[i], to[j] = j, i
         return lax.ppermute(message, ("ax", "rad"), list(enumerate(to)))
 
-    got_b = exchange(1)
-    got_a = exchange(0)
+    got_b = exchange(message_b, 1)
+    got_a = exchange(message_a, 0)
 
     motion_out, arr_rad, gas_out, liquid, image = pl.pallas_call(
         functools.partial(rest_kernel, sz, n_rad),

time: 11.3 us -> 12.1 us (1.071)
  the two profiles are of different devices: /device:TPU:0 before, /device:TPU:8 now
where the time goes in v12:
time: 12.1 us; the launch traced here: 11.9 us
  Pallas kernels  3.88 us (32%)
  starting transfers between devices  2.87 us (24%)
  waiting for transfers between devices  2.34 us (19%)
  blocking collectives  2.12 us (18%)
  between operations  0.66 us (5%)
    ppermute x2, starting transfers between devices, exchange(): return lax.ppermute(message, ('ax', 'rad'), list(enumerate(to)))  2.87 us
    ppermute x2, waiting for transfers between devices, exchange(): return lax.ppermute(message, ('ax', 'rad'), list(enumerate(to)))  2.34 us
    all_gather x1, blocking collectives, on_device(): gathered = lax.all_gather(packed, 'rad', axis=0)  2.12 us
    pallas_call x1, Pallas kernels, on_device(): pl.pallas_call(functools.partial(rest_kernel, sz, n_rad), out_shape=[jax....  1.67 us
    pallas_call x1, Pallas kernels, on_device(): pl.pallas_call(functools.partial(pack_kernel, sz, n_rad), out_shape=[jax....  1.12 us
    pallas_call x1, Pallas kernels, on_device(): pl.pallas_call(functools.partial(finish_kernel, sz, n_ax), out_shape=[jax...  0.68 us
    pallas_call x1, Pallas kernels, on_device(): pl.pallas_call(functools.partial(move_kernel, sz, n_rad), out_shape=[jax....  0.43 us
  transfers between devices with their start and end apart: 2, of which 1 were waited for; matrix products, arithmetic and copies ran while one was open for 0% of the time, Pallas kernels for 14%

profile of v12, /device:TPU:8, one launch (start us, length us, event | category | flops | bytes accessed | tf_op | source)
XLA Modules:
  0.0 11.9 jit_solution(11055812272157512770)
XLA Ops:
  0.6 1.1 %pack.1 = (f32[424,128]{1,0:T(8,128)S(1)}, s32[72,128]{1,0:T(8,128)S(1)}) custom-call(f32[6,2048]{1,0:T(8,128)} %motion_hbm.1, f32[16,128]{1,0:T(8,128)} %bitcast.21, s32[1,32]{1,0:T(1,128)} %bitcast.27, s32[16,128]{1,0:T(8,128)} %bitcast.22, f32[3,16,512]{2,1,0:T(8,128)} %gas_hbm.1, f32[16,512]{1,0:T(8,128)} %pres_hbm.1, s32[2,32]{1,0:T(2,128)} %bitcast.25, ...), custom_call_target="tpu_custom_call" | custom-call | tf_op jit(solution)/shard_map/pack/pallas_call | solution.py:351
  1.8 2.1 %all-gather = f32[848,128]{1,0:T(8,128)S(1)} all-gather(f32[424,128]{1,0:T(8,128)S(1)} %get-tuple-element.18), channel_id=2, replica_groups=mesh['ax'=16,'rad'=2] {'rad'}, dimensions={0}, use_global_device_ids=true | all-gather | bytes 651264 | tf_op jit(solution)/shard_map/all_gather | solution.py:385
  3.9 0.0 copy-start
  3.9 0.4 %move.1 = (f32[224,128]{1,0:T(8,128)S(1)}, f32[8,128]{1,0:T(8,128)S(1)}, f32[8,128]{1,0:T(8,128)S(1)}) custom-call(f32[2,424,128]{2,1,0:T(8,128)S(1)} %bitcast.19, s32[72,128]{1,0:T(8,128)S(1)} %get-tuple-element.19.aux), custom_call_target="tpu_custom_call" | custom-call | flops 4000000000 | bytes 1000000 | tf_op jit(solution)/shard_map/move/pallas_call | solution.py:387
  4.3 1.5 %collective-permute-start = (f32[8,128]{1,0:T(8,128)S(1)}, f32[8,128]{1,0:T(8,128)S(1)}, u32[]{:S(2)}, u32[]{:S(2)}) collective-permute-start(f32[8,128]{1,0:T(8,128)S(1)} %get-tuple-element.22), channel_id=1, source_target_pairs={{0,2},{1,3},{2,0},{3,1},{4,6},{5,7},{6,4},{7,5},{8,10},{9,11},{10,... | collective-permute-start | bytes 12296 | tf_op jit(solution)/shard_map/ppermute | solution.py:411
  5.8 1.4 %collective-permute-start.1 = (f32[8,128]{1,0:T(8,128)S(1)}, f32[8,128]{1,0:T(8,128)S(1)}, u32[]{:S(2)}, u32[]{:S(2)}) collective-permute-start(f32[8,128]{1,0:T(8,128)S(1)} %get-tuple-element.23), channel_id=1, source_target_pairs={{0,1},{1,0},{2,4},{3,5},{4,2},{5,3},{6,8},{7,9},{8,6},{9,7},{10,12... | collective-permute-start | bytes 12296 | tf_op jit(solution)/shard_map/ppermute | solution.py:411
  7.2 0.0 copy-done
  7.2 1.7 %rest.1 = (f32[6,2048]{1,0:T(8,128)}, f32[7,2,32]{2,1,0:T(2,128)}, f32[3,16,512]{2,1,0:T(8,128)}, f32[16,512]{1,0:T(8,128)}, f32[16,512]{1,0:T(8,128)S(1)}) custom-call(f32[2,424,128]{2,1,0:T(8,128)S(1)} %bitcast.20, s32[72,128]{1,0:T(8,128)S(1)} %get-tuple-element.19.aux, f32[8,128,128]{2,1,0:T(8,128)S(1)} %copy-done, f32[224,128]{1,0:T(8,128)S(1)} %get-tuple-element.20.state), custom_call_target="tpu_custom_call" | custom-call | flops 2000000000 | bytes 2000000 | tf_op jit(solution)/shard_map/rest/pallas_call | solution.py:416
  8.9 0.0 collective-permute-done.got_a
  8.9 2.3 %collective-permute-done.1.got_b = f32[8,128]{1,0:T(8,128)S(1)} collective-permute-done((f32[8,128]{1,0:T(8,128)S(1)}, f32[8,128]{1,0:T(8,128)S(1)}, u32[]{:S(2)}, u32[]{:S(2)}) %collective-permute-start.1) | collective-permute-done | bytes 4128 | tf_op jit(solution)/shard_map/ppermute | solution.py:411
  11.2 0.7 %finish.1 = (f32[7,2,64]{2,1,0:T(2,128)}, f32[16,512]{1,0:T(8,128)}) custom-call(f32[8,128]{1,0:T(8,128)S(1)} %collective-permute-done.got_a, f32[8,128]{1,0:T(8,128)S(1)} %collective-permute-done.1.got_b, f32[16,512]{1,0:T(8,128)S(1)} %get-tuple-element.24.image), custom_call_target="tpu_custom_call" | custom-call | tf_op jit(solution)/shard_map/finish/pallas_call | solution.py:442
Async XLA Ops:
  3.9 3.3 %copy-start = (f32[8,128,128]{2,1,0:T(8,128)S(1)}, f32[8,128,128]{2,1,0:T(8,128)}, u32[]{:S(2)}) copy-start(f32[8,128,128]{2,1,0:T(8,128)} %table.1) | copy-start | bytes 1572868
  4.3 4.6 %collective-permute-start = (f32[8,128]{1,0:T(8,128)S(1)}, f32[8,128]{1,0:T(8,128)S(1)}, u32[]{:S(2)}, u32[]{:S(2)}) collective-permute-start(f32[8,128]{1,0:T(8,128)S(1)} %get-tuple-element.22), channel_id=1, source_target_pairs={{0,2},{1,3},{2,0},{3,1},{4,6},{5,7},{6,4},{7,5},{8,10},{9,11},{10,... | collective-permute-start | bytes 12296 | tf_op jit(solution)/shard_map/ppermute | solution.py:411
  5.8 5.4 %collective-permute-start.1 = (f32[8,128]{1,0:T(8,128)S(1)}, f32[8,128]{1,0:T(8,128)S(1)}, u32[]{:S(2)}, u32[]{:S(2)}) collective-permute-start(f32[8,128]{1,0:T(8,128)S(1)} %get-tuple-element.23), channel_id=1, source_target_pairs={{0,1},{1,0},{2,4},{3,5},{4,2},{5,3},{6,8},{7,9},{8,6},{9,7},{10,12... | collective-permute-start | bytes 12296 | tf_op jit(solution)/shard_map/ppermute | solution.py:411

commit v13 on v10

--- a/solution.py
+++ b/solution.py
@@ -65,50 +65,52 @@
 def pack_kernel(
     sz, n_rad, motion_hbm, size_hbm, block_hbm, offset_hbm, gas_hbm, pres_hbm, radial_hbm, counts_hbm, cols_hbm,
     kinds_hbm, axial_hbm,
-    out, aux,
-    motion, size, block, offset, gas, pres, radial, counts, cols, kinds, axial, sem,
+    out, aux, cols, kinds,
+    motion, size, block, offset, gas, pres, radial, counts, axial, sem,
 ):
     small = (
-        (counts_hbm, counts), (block_hbm, block), (radial_hbm, radial), (axial_hbm, axial), (cols_hbm, cols),
-        (kinds_hbm, kinds), (offset_hbm, offset), (size_hbm, size),
+        (block_hbm, block), (counts_hbm, counts), (radial_hbm, radial), (axial_hbm, axial), (offset_hbm, offset),
+        (size_hbm, size),
     )
-    large = ((motion_hbm, motion), (pres_hbm, pres), *((gas_hbm.at[c], gas.at[c]) for c in range(3)))
-    copies = [pltpu.make_async_copy(src, dst, sem.at[i]) for i, (src, dst) in enumerate(small + large)]
+    large = ((motion_hbm, motion), *((gas_hbm.at[c], gas.at[c]) for c in range(3)), (pres_hbm, pres))
+    late = ((cols_hbm, cols), (kinds_hbm, kinds))
+    copies = [pltpu.make_async_copy(src, dst, sem.at[i]) for i, (src, dst) in enumerate(large + small + late)]
     for copy in copies:
         copy.start()
+    motion_copy, *gas_copies, pres_copy = copies[: len(large)]
+    late_copies = copies[len(large + small) :]
     out[pl.ds(sz.meta, 8), :] = jnp.full((8, BLOCK), -1.0, F32)
     layers = sz.layers
-    for copy in copies[: len(small)]:
+    for copy in copies[len(large) : len(large + small)]:
         copy.wait()
     out[pl.ds(sz.size, sz.tiles), :] = size[...]
     out[pl.ds(sz.offset, sz.tiles), :] = offset[...].astype(F32)
     numbers = block_row(sz, block[...]).astype(F32)
     out[pl.ds(sz.meta, 1), pl.ds(0, sz.groups)] = numbers
     numbers = jnp.concatenate([numbers, jnp.zeros((1, BLOCK - sz.groups), F32)], axis=1)
-    out[pl.ds(sz.column, sz.groups), :] = jnp.transpose(jnp.broadcast_to(numbers, (BLOCK, BLOCK)))[: sz.groups]
+    lane = iota((8, BLOCK), 1)
+    order = jnp.where(lane < sz.tiles, 2 * lane, 2 * (lane - sz.tiles) + 1) & (sz.groups - 1)
+    numbers = take_lanes(jnp.broadcast_to(numbers, (8, BLOCK)), order)
+    numbers = jnp.concatenate([numbers] * (BLOCK // 8), axis=0)
+    out[pl.ds(sz.column, sz.groups), :] = jnp.transpose(numbers)[: sz.groups]
     width = radial.shape[1]
     lane = iota((1, width), 1)
     for slot in range(2):
         kept = jnp.where(lane < counts[0, 2 + slot], radial[slot : slot + 1, :], -1)
         out[pl.ds(sz.meta + 1 + slot, 1), pl.ds(0, width)] = kept.astype(F32)
-    index = kinds[...] * (n_rad * sz.blocks) + block_row(sz, cols[...])
-    index = jnp.concatenate([index, index], axis=1).astype(F32)
-    index = jnp.concatenate([index, jnp.zeros((BLOCK - index.shape[0], BLOCK), F32)], axis=0)
-    aux[pl.ds(8, sz.blocks), :] = jnp.transpose(index)[: sz.blocks].astype(I32)
     lane = iota((1, axial.shape[1]), 1)
     kept = [jnp.where(lane < counts[0, slot], axial[slot : slot + 1, :], -1) for slot in range(2)]
     aux[pl.ds(0, 1), :] = jnp.concatenate(kept, axis=1)
-    motion_copy, pres_copy, *gas_copies = copies[len(small) :]
     motion_copy.wait()
     for i in range(sz.tiles):
         out[pl.ds(sz.motion + i, 6, stride=sz.tiles), :] = motion[:, i * BLOCK : (i + 1) * BLOCK]
-    pres_copy.wait()
+    for copy in (*gas_copies, pres_copy, *late_copies):
+        copy.wait()
+    for c in range(3):
+        for q in range(sz.quarters):
+            out[pl.ds(sz.gas + c * sz.blocks + q * layers, layers), :] = gas[c, :, q * BLOCK : (q + 1) * BLOCK]
     for q in range(sz.quarters):
         out[pl.ds(sz.pres + q * layers, layers), :] = pres[:, q * BLOCK : (q + 1) * BLOCK]
-    for c in range(3):
-        gas_copies[c].wait()
-        for q in range(sz.quarters):
-            out[pl.ds(sz.gas + c * sz.blocks + q * layers, layers), :] = gas[c, :, q * BLOCK : (q + 1) * BLOCK]
 
 
 def take_lanes(x, idx):
@@ -132,7 +134,7 @@
     return [state[pl.ds(c * T + first, sz.tiles), :] for c in range(7)]
 
 
-def move_kernel(sz, n_rad, G, aux, state, message, near):
+def move_kernel(sz, n_rad, G, aux, cols, kinds, state, message, columns):
     r = lax.axis_index("rad")
     layers, tiles, blocks, groups = sz.layers, sz.tiles, sz.blocks, sz.groups
     slab_blocks = n_rad * blocks
@@ -152,25 +154,37 @@
     )
     high, low = split2(gas_slab)
     found = dot(jnp.concatenate([chooser, chooser], axis=1), jnp.concatenate([high, low], axis=0))
-    for c in range(3):
-        near[c] = found[:, c * BLOCK : (c + 1) * BLOCK]
+
+    def groups_of(c, odd):
+        return jnp.concatenate(
+            [
+                found[d * groups + odd * tiles : d * groups + (odd + 1) * tiles, c * BLOCK : (c + 1) * BLOCK]
+                for d in range(n_rad)
+            ],
+            axis=0,
+        )
 
     rows = functools.partial(slab_rows, sz, n_rad, G)
     size = rows(sz.size)
     offset = rows(sz.offset).astype(I32)
     factor = jnp.exp(-DRAG / (size * size))
     even = iota((T, BLOCK), 1) < GROUP
+    values = [None] * 6 + [size]
     for c in range(3):
-        u_even = take_lanes(near[c, pl.ds(0, T, stride=2), :], offset)
-        u_odd = take_lanes(near[c, pl.ds(1, T, stride=2), :], offset)
-        u = jnp.where(even, u_even, u_odd)
+        u = jnp.where(even, take_lanes(groups_of(c, 0), offset), take_lanes(groups_of(c, 1), offset))
         v = rows(sz.motion + (3 + c) * tiles)
         new = u + (v - u) * factor
-        state[pl.ds(c * T, T), :] = rows(sz.motion + c * tiles) + STEP * new
-        state[pl.ds((3 + c) * T, T), :] = new
-    state[pl.ds(6 * T, T), :] = size
-
-    payload = pick(sz, state_of(sz, T, state, r), aux[pl.ds(0, 1), :])
+        values[c] = rows(sz.motion + c * tiles) + STEP * new
+        values[3 + c] = new
+    own = []
+    for c in range(7):
+        state[pl.ds(c * T, T), :] = values[c]
+        mine = values[c][:tiles]
+        for d in range(1, n_rad):
+            mine = jnp.where(r == d, values[c][d * tiles : (d + 1) * tiles], mine)
+        own.append(mine)
+
+    payload = pick(sz, own, aux[pl.ds(0, 1), :])
     for c in range(7):
         message[c : c + 1, :] = payload[c]
     message[7:8, :] = jnp.zeros((1, BLOCK), F32)
@@ -178,10 +192,14 @@
         first = sz.pres + q * layers
         message[8 + q : 9 + q, :] = G[r, pl.ds(first + layers - 1, 1), :]
         message[12 + q : 13 + q, :] = G[r, pl.ds(first, 1), :]
+    index = kinds[...] * slab_blocks + block_row(sz, cols[...])
+    index = jnp.concatenate([index, index], axis=1).astype(F32)
+    index = jnp.concatenate([index, jnp.zeros((BLOCK - index.shape[0], BLOCK), F32)], axis=0)
+    columns[...] = jnp.transpose(index)[:blocks].astype(I32)
 
 
 def rest_kernel(
-    sz, n_rad, G, aux, table, state,
+    sz, n_rad, G, columns, table, state,
     motion_hbm, arr_hbm, gas_hbm, liquid_hbm, image,
     deps, spread, coup, motion_out, arr_rad, gas_out, liquid, sem,
 ):
@@ -250,7 +268,7 @@
 
     pres = jnp.concatenate([G[d, pl.ds(sz.pres, blocks), :] for d in range(n_rad)], axis=0)
     index = [
-        jnp.broadcast_to(aux[pl.ds(8, blocks), k : k + 1], (blocks, BLOCK)).astype(jnp.int16) for k in range(4)
+        jnp.broadcast_to(columns[:, k : k + 1], (blocks, BLOCK)).astype(jnp.int16) for k in range(4)
     ]
     one, none = jnp.ones((blocks, BLOCK), BF16), jnp.zeros((blocks, BLOCK), BF16)
     lanes = iota((blocks, BLOCK), 1)
@@ -301,8 +319,9 @@
     low = jnp.where(a > 0, jnp.where(even, got_b[...], got_a[...]), 0.0)
     up = jnp.where(a < n_ax - 1, jnp.where(even, got_a[...], got_b[...]), 0.0)
     half = arr_ax.shape[2]
-    arr_ax[:, 0, :] = low[0:7, 0:half]
-    arr_ax[:, 1, :] = up[0:7, half : 2 * half]
+    for c in range(7):
+        arr_ax[c, 0:1, :] = low[c : c + 1, 0:half]
+        arr_ax[c, 1:2, :] = up[c : c + 1, half : 2 * half]
     pressure_image[...] = image[...]
     last = sz.layers - 1
     for q in range(sz.quarters):
@@ -336,14 +355,16 @@
     size2 = parcel_size.reshape(sz.tiles, BLOCK)
     offset2 = parcel_offset.reshape(sz.tiles, BLOCK)
 
-    packed, aux = pl.pallas_call(
+    packed, aux, cols, kinds = pl.pallas_call(
         functools.partial(pack_kernel, sz, n_rad),
         out_shape=[
             jax.ShapeDtypeStruct((sz.rows, BLOCK), F32),
-            jax.ShapeDtypeStruct((8 + sz.blocks, BLOCK), I32),
+            jax.ShapeDtypeStruct((8, BLOCK), I32),
+            jax.ShapeDtypeStruct((4, sz.blocks), I32),
+            jax.ShapeDtypeStruct((4, sz.blocks), I32),
         ],
         in_specs=[hbm] * 11,
-        out_specs=[vmem] * 2,
+        out_specs=[vmem] * 4,
         scratch_shapes=[
             pltpu.VMEM(parcel_motion.shape, F32),
             pltpu.VMEM(size2.shape, F32),
@@ -353,8 +374,6 @@
             pltpu.VMEM(pressure.shape, F32),
             pltpu.VMEM((2, cap_rad), I32),
             pltpu.SMEM((1, 4), I32),
-            pltpu.VMEM((4, sz.blocks), I32),
-            pltpu.VMEM((4, sz.blocks), I32),
             pltpu.VMEM((2, cap_ax), I32),
             pltpu.SemaphoreType.DMA((13,)),
         ],
@@ -372,19 +391,19 @@
     )
     gathered = lax.all_gather(packed, "rad", axis=0)
 
-    state, message = pl.pallas_call(
+    state, message, columns = pl.pallas_call(
         functools.partial(move_kernel, sz, n_rad),
         out_shape=[
             jax.ShapeDtypeStruct((7 * T, BLOCK), F32),
             jax.ShapeDtypeStruct((16, BLOCK), F32),
-        ],
-        in_specs=[vmem] * 2,
-        out_specs=[vmem] * 2,
-        scratch_shapes=[pltpu.VMEM((3, n_rad * sz.groups, BLOCK), F32)],
+            jax.ShapeDtypeStruct((sz.blocks, BLOCK), I32),
+        ],
+        in_specs=[vmem] * 4,
+        out_specs=[vmem] * 3,
         compiler_params=params,
         cost_estimate=pl.CostEstimate(flops=4_000_000_000, bytes_accessed=1_000_000, transcendentals=0),
         name="move",
-    )(gathered, aux)
+    )(gathered, aux, cols, kinds)
 
     def exchange(first):
         to = list(range(n_ax * n_rad))
@@ -424,7 +443,7 @@
         compiler_params=params,
         cost_estimate=pl.CostEstimate(flops=2_000_000_000, bytes_accessed=2_000_000, transcendentals=0),
         name="rest",
-    )(gathered, aux, block_table, state)
+    )(gathered, columns, block_table, state)
 
     arr_ax, pressure_image = pl.pallas_call(
         functools.partial(finish_kernel, sz, n_ax),

time: 11.3 us -> 11.3 us (level)
  no operation moved by 1% of the time
where the time goes in v13:
time: 11.3 us; the launch traced here: 11.2 us
  starting transfers between devices  4.41 us (39%)
  Pallas kernels  3.86 us (34%)
  blocking collectives  2.2 us (19%)
  between operations  0.67 us (6%)
    ppermute x2, starting transfers between devices, exchange(): return lax.ppermute(message, ('ax', 'rad'), list(enumerate(to)))  4.41 us
    all_gather x1, blocking collectives, on_device(): gathered = lax.all_gather(packed, 'rad', axis=0)  2.2 us
    pallas_call x1, Pallas kernels, on_device(): pl.pallas_call(functools.partial(rest_kernel, sz, n_rad), out_shape=[jax....  1.66 us
    pallas_call x1, Pallas kernels, on_device(): pl.pallas_call(functools.partial(pack_kernel, sz, n_rad), out_shape=[jax....  1.16 us
    pallas_call x1, Pallas kernels, on_device(): pl.pallas_call(functools.partial(finish_kernel, sz, n_ax), out_shape=[jax...  0.68 us
    pallas_call x1, Pallas kernels, on_device(): pl.pallas_call(functools.partial(move_kernel, sz, n_rad), out_shape=[jax....  0.37 us
  transfers between devices with their start and end apart: 2, of which 0 were waited for; matrix products, arithmetic and copies ran while one was open for 0% of the time, Pallas kernels for 15%

profile of v13, /device:TPU:0, one launch (start us, length us, event | category | flops | bytes accessed | tf_op | source)
XLA Modules:
  0.0 11.2 jit_solution(11354663504125998384)
XLA Ops:
  0.6 1.2 %pack.1 = (f32[424,128]{1,0:T(8,128)S(1)}, s32[8,128]{1,0:T(8,128)S(1)}, s32[4,64]{1,0:T(4,128)S(1)}, s32[4,64]{1,0:T(4,128)S(1)}) custom-call(f32[6,2048]{1,0:T(8,128)} %motion_hbm.1, f32[16,128]{1,0:T(8,128)} %bitcast.21, s32[1,32]{1,0:T(1,128)} %bitcast.27, s32[16,128]{1,0:T(8,128)} %bitcast.22, f32[3,16,512]{2,1,0:T(8,128)} %gas_hbm.1, ...), custom_call_target="tpu_custom_call" | custom-call | tf_op jit(solution)/shard_map/pack/pallas_call | solution.py:358
  1.8 2.2 %all-gather = f32[848,128]{1,0:T(8,128)S(1)} all-gather(f32[424,128]{1,0:T(8,128)S(1)} %get-tuple-element.20), channel_id=2, replica_groups=mesh['ax'=16,'rad'=2] {'rad'}, dimensions={0}, use_global_device_ids=true | all-gather | bytes 651264 | tf_op jit(solution)/shard_map/all_gather | solution.py:392
  4.0 0.0 copy-start
  4.0 0.4 %move.1 = (f32[224,128]{1,0:T(8,128)S(1)}, f32[16,128]{1,0:T(8,128)S(1)}, s32[64,128]{1,0:T(8,128)S(1)}) custom-call(f32[2,424,128]{2,1,0:T(8,128)S(1)} %bitcast.19, s32[8,128]{1,0:T(8,128)S(1)} %get-tuple-element.21.aux, s32[4,64]{1,0:T(4,128)S(1)} %get-tuple-element.22.cols, s32[4,64]{1,0:T(4,128)S(1)} %get-tuple-element.23.kinds), custom_call_target="tpu_custom_call" | custom-call | flops 4000000000 | bytes 1000000 | tf_op jit(solution)/shard_map/move/pallas_call | solution.py:394
  4.4 0.4 %collective-permute-start.1 = (f32[16,128]{1,0:T(8,128)S(1)}, f32[16,128]{1,0:T(8,128)S(1)}, u32[]{:S(2)}, u32[]{:S(2)}) collective-permute-start(f32[16,128]{1,0:T(8,128)S(1)} %get-tuple-element.27), channel_id=1, source_target_pairs={{0,1},{1,0},{2,4},{3,5},{4,2},{5,3},{6,8},{7,9},{8,6},{9,7},{10,12... | collective-permute-start | bytes 24584 | tf_op jit(solution)/shard_map/ppermute | solution.py:417
  4.8 4.0 %collective-permute-start = (f32[16,128]{1,0:T(8,128)S(1)}, f32[16,128]{1,0:T(8,128)S(1)}, u32[]{:S(2)}, u32[]{:S(2)}) collective-permute-start(f32[16,128]{1,0:T(8,128)S(1)} %get-tuple-element.27), channel_id=1, source_target_pairs={{0,2},{1,3},{2,0},{3,1},{4,6},{5,7},{6,4},{7,5},{8,10},{9,11},{10,... | collective-permute-start | bytes 24584 | tf_op jit(solution)/shard_map/ppermute | solution.py:417
  8.8 0.0 copy-done
  8.8 1.7 %rest.1 = (f32[6,2048]{1,0:T(8,128)}, f32[7,2,32]{2,1,0:T(2,128)}, f32[3,16,512]{2,1,0:T(8,128)}, f32[16,512]{1,0:T(8,128)}, f32[16,512]{1,0:T(8,128)S(1)}) custom-call(f32[2,424,128]{2,1,0:T(8,128)S(1)} %bitcast.20, s32[64,128]{1,0:T(8,128)S(1)} %get-tuple-element.24.columns, f32[8,128,128]{2,1,0:T(8,128)S(1)} %copy-done, ...), custom_call_target="tpu_custom_call" | custom-call | flops 2000000000 | bytes 2000000 | tf_op jit(solution)/shard_map/rest/pallas_call | solution.py:422
  10.5 0.0 collective-permute-done.1.got_b
  10.5 0.0 collective-permute-done.got_a
  10.5 0.7 %finish.1 = (f32[7,2,64]{2,1,0:T(2,128)}, f32[16,512]{1,0:T(8,128)}) custom-call(f32[16,128]{1,0:T(8,128)S(1)} %collective-permute-done.got_a, f32[16,128]{1,0:T(8,128)S(1)} %collective-permute-done.1.got_b, f32[16,512]{1,0:T(8,128)S(1)} %get-tuple-element.28.image), custom_call_target="tpu_custom_call" | custom-call | tf_op jit(solution)/shard_map/finish/pallas_call | solution.py:448
Async XLA Ops:
  4.0 4.8 %copy-start = (f32[8,128,128]{2,1,0:T(8,128)S(1)}, f32[8,128,128]{2,1,0:T(8,128)}, u32[]{:S(2)}) copy-start(f32[8,128,128]{2,1,0:T(8,128)} %table.1) | copy-start | bytes 1572868
  4.4 6.1 %collective-permute-start.1 = (f32[16,128]{1,0:T(8,128)S(1)}, f32[16,128]{1,0:T(8,128)S(1)}, u32[]{:S(2)}, u32[]{:S(2)}) collective-permute-start(f32[16,128]{1,0:T(8,128)S(1)} %get-tuple-element.27), channel_id=1, source_target_pairs={{0,1},{1,0},{2,4},{3,5},{4,2},{5,3},{6,8},{7,9},{8,6},{9,7},{10,12... | collective-permute-start | bytes 24584 | tf_op jit(solution)/shard_map/ppermute | solution.py:417
  4.8 5.7 %collective-permute-start = (f32[16,128]{1,0:T(8,128)S(1)}, f32[16,128]{1,0:T(8,128)S(1)}, u32[]{:S(2)}, u32[]{:S(2)}) collective-permute-start(f32[16,128]{1,0:T(8,128)S(1)} %get-tuple-element.27), channel_id=1, source_target_pairs={{0,2},{1,3},{2,0},{3,1},{4,6},{5,7},{6,4},{7,5},{8,10},{9,11},{10,... | collective-permute-start | bytes 24584 | tf_op jit(solution)/shard_map/ppermute | solution.py:417

commit v14 on v10

--- a/solution.py
+++ b/solution.py
@@ -68,6 +68,10 @@
     out, aux,
     motion, size, block, offset, gas, pres, radial, counts, cols, kinds, axial, sem,
 ):
+    def put(at, lanes, value):
+        for d in range(n_rad):
+            out[d, at, lanes] = value
+
     small = (
         (counts_hbm, counts), (block_hbm, block), (radial_hbm, radial), (axial_hbm, axial), (cols_hbm, cols),
         (kinds_hbm, kinds), (offset_hbm, offset), (size_hbm, size),
@@ -76,21 +80,21 @@
     copies = [pltpu.make_async_copy(src, dst, sem.at[i]) for i, (src, dst) in enumerate(small + large)]
     for copy in copies:
         copy.start()
-    out[pl.ds(sz.meta, 8), :] = jnp.full((8, BLOCK), -1.0, F32)
+    put(pl.ds(sz.meta, 8), slice(None), jnp.full((8, BLOCK), -1.0, F32))
     layers = sz.layers
     for copy in copies[: len(small)]:
         copy.wait()
-    out[pl.ds(sz.size, sz.tiles), :] = size[...]
-    out[pl.ds(sz.offset, sz.tiles), :] = offset[...].astype(F32)
+    put(pl.ds(sz.size, sz.tiles), slice(None), size[...])
+    put(pl.ds(sz.offset, sz.tiles), slice(None), offset[...].astype(F32))
     numbers = block_row(sz, block[...]).astype(F32)
-    out[pl.ds(sz.meta, 1), pl.ds(0, sz.groups)] = numbers
+    put(pl.ds(sz.meta, 1), pl.ds(0, sz.groups), numbers)
     numbers = jnp.concatenate([numbers, jnp.zeros((1, BLOCK - sz.groups), F32)], axis=1)
-    out[pl.ds(sz.column, sz.groups), :] = jnp.transpose(jnp.broadcast_to(numbers, (BLOCK, BLOCK)))[: sz.groups]
+    put(pl.ds(sz.column, sz.groups), slice(None), jnp.transpose(jnp.broadcast_to(numbers, (BLOCK, BLOCK)))[: sz.groups])
     width = radial.shape[1]
     lane = iota((1, width), 1)
     for slot in range(2):
         kept = jnp.where(lane < counts[0, 2 + slot], radial[slot : slot + 1, :], -1)
-        out[pl.ds(sz.meta + 1 + slot, 1), pl.ds(0, width)] = kept.astype(F32)
+        put(pl.ds(sz.meta + 1 + slot, 1), pl.ds(0, width), kept.astype(F32))
     index = kinds[...] * (n_rad * sz.blocks) + block_row(sz, cols[...])
     index = jnp.concatenate([index, index], axis=1).astype(F32)
     index = jnp.concatenate([index, jnp.zeros((BLOCK - index.shape[0], BLOCK), F32)], axis=0)
@@ -101,14 +105,14 @@
     motion_copy, pres_copy, *gas_copies = copies[len(small) :]
     motion_copy.wait()
     for i in range(sz.tiles):
-        out[pl.ds(sz.motion + i, 6, stride=sz.tiles), :] = motion[:, i * BLOCK : (i + 1) * BLOCK]
+        put(pl.ds(sz.motion + i, 6, stride=sz.tiles), slice(None), motion[:, i * BLOCK : (i + 1) * BLOCK])
     pres_copy.wait()
     for q in range(sz.quarters):
-        out[pl.ds(sz.pres + q * layers, layers), :] = pres[:, q * BLOCK : (q + 1) * BLOCK]
+        put(pl.ds(sz.pres + q * layers, layers), slice(None), pres[:, q * BLOCK : (q + 1) * BLOCK])
     for c in range(3):
         gas_copies[c].wait()
         for q in range(sz.quarters):
-            out[pl.ds(sz.gas + c * sz.blocks + q * layers, layers), :] = gas[c, :, q * BLOCK : (q + 1) * BLOCK]
+            put(pl.ds(sz.gas + c * sz.blocks + q * layers, layers), slice(None), gas[c, :, q * BLOCK : (q + 1) * BLOCK])
 
 
 def take_lanes(x, idx):
@@ -339,7 +343,7 @@
     packed, aux = pl.pallas_call(
         functools.partial(pack_kernel, sz, n_rad),
         out_shape=[
-            jax.ShapeDtypeStruct((sz.rows, BLOCK), F32),
+            jax.ShapeDtypeStruct((n_rad, sz.rows, BLOCK), F32),
             jax.ShapeDtypeStruct((8 + sz.blocks, BLOCK), I32),
         ],
         in_specs=[hbm] * 11,
@@ -370,7 +374,7 @@
             )
         )
     )
-    gathered = lax.all_gather(packed, "rad", axis=0)
+    gathered = lax.all_to_all(packed, "rad", 0, 0)
 
     state, message = pl.pallas_call(
         functools.partial(move_kernel, sz, n_rad),

time: 11.3 us -> 13.3 us (1.18)
  blocking collectives: 2.2 us -> 4.07 us
    all_to_all x0 -> x1, blocking collectives: none -> 4.07 us  [on_device(): gathered = lax.all_to_all(packed, 'rad', 0, 0)]
    all_gather x1 -> x0, blocking collectives: 2.2 us -> none  [on_device(): gathered = lax.all_gather(packed, 'rad', axis=0)]
  transfers between devices with their start and end apart: 2 -> 2, of which waited for: 0 -> 0; matrix products, arithmetic and copies ran while one was open for 0% -> 0% of each run, Pallas kernels for 15% -> 13%
where the time goes in v14:
time: 13.3 us; the launch traced here: 13.1 us
  starting transfers between devices  4.49 us (34%)
  blocking collectives  4.07 us (31%)
  Pallas kernels  3.84 us (29%)
  between operations  0.67 us (5%)
    ppermute x2, starting transfers between devices, exchange(): return lax.ppermute(message, ('ax', 'rad'), list(enumerate(to)))  4.49 us
    all_to_all x1, blocking collectives, on_device(): gathered = lax.all_to_all(packed, 'rad', 0, 0)  4.07 us
    pallas_call x1, Pallas kernels, on_device(): pl.pallas_call(functools.partial(rest_kernel, sz, n_rad), out_shape=[jax....  1.67 us
    pallas_call x1, Pallas kernels, on_device(): pl.pallas_call(functools.partial(pack_kernel, sz, n_rad), out_shape=[jax....  1.14 us
    pallas_call x1, Pallas kernels, on_device(): pl.pallas_call(functools.partial(finish_kernel, sz, n_ax), out_shape=[jax...  0.69 us
    pallas_call x1, Pallas kernels, on_device(): pl.pallas_call(functools.partial(move_kernel, sz, n_rad), out_shape=[jax....  0.35 us
  transfers between devices with their start and end apart: 2, of which 0 were waited for; matrix products, arithmetic and copies ran while one was open for 0% of the time, Pallas kernels for 13%

profile of v14, /device:TPU:0, one launch (start us, length us, event | category | flops | bytes accessed | tf_op | source)
XLA Modules:
  0.0 13.1 jit_solution(7841802091447704192)
XLA Ops:
  0.6 1.1 %pack.1 = (f32[2,424,128]{2,1,0:T(8,128)S(1)}, s32[72,128]{1,0:T(8,128)S(1)}) custom-call(f32[6,2048]{1,0:T(8,128)} %motion_hbm.1, f32[16,128]{1,0:T(8,128)} %bitcast.18, s32[1,32]{1,0:T(1,128)} %bitcast.24, s32[16,128]{1,0:T(8,128)} %bitcast.19, f32[3,16,512]{2,1,0:T(8,128)} %gas_hbm.1, f32[16,512]{1,0:T(8,128)} %pres_hbm.1, s32[2,32]{1,0:T(2,128)} %bitcast.22, ...), custom_call_target="tpu_custom_call" | custom-call | tf_op jit(solution)/shard_map/pack/pallas_call | solution.py:343
  1.8 4.1 %all_to_all.5.G = f32[2,424,128]{2,1,0:T(8,128)S(1)} all-to-all(f32[2,424,128]{2,1,0:T(8,128)S(1)} %get-tuple-element.17), channel_id=1, replica_groups=mesh['ax'=16,'rad'=2] {'rad'}, dimensions={0} | all-to-all | bytes 868352 | tf_op jit(solution)/shard_map/all_to_all | solution.py:377
  5.8 0.0 copy-start
  5.9 0.4 %move.1 = (f32[224,128]{1,0:T(8,128)S(1)}, f32[16,128]{1,0:T(8,128)S(1)}) custom-call(f32[2,424,128]{2,1,0:T(8,128)S(1)} %all_to_all.5.G, s32[72,128]{1,0:T(8,128)S(1)} %get-tuple-element.18.aux), custom_call_target="tpu_custom_call" | custom-call | flops 4000000000 | bytes 1000000 | tf_op jit(solution)/shard_map/move/pallas_call | solution.py:379
  6.2 0.2 %collective-permute-start.1 = (f32[16,128]{1,0:T(8,128)S(1)}, f32[16,128]{1,0:T(8,128)S(1)}, u32[]{:S(2)}, u32[]{:S(2)}) collective-permute-start(f32[16,128]{1,0:T(8,128)S(1)} %get-tuple-element.21), channel_id=1, source_target_pairs={{0,1},{1,0},{2,4},{3,5},{4,2},{5,3},{6,8},{7,9},{8,6},{9,7},{10,12... | collective-permute-start | bytes 24584 | tf_op jit(solution)/shard_map/ppermute | solution.py:402
  6.4 4.3 %collective-permute-start = (f32[16,128]{1,0:T(8,128)S(1)}, f32[16,128]{1,0:T(8,128)S(1)}, u32[]{:S(2)}, u32[]{:S(2)}) collective-permute-start(f32[16,128]{1,0:T(8,128)S(1)} %get-tuple-element.21), channel_id=1, source_target_pairs={{0,2},{1,3},{2,0},{3,1},{4,6},{5,7},{6,4},{7,5},{8,10},{9,11},{10,... | collective-permute-start | bytes 24584 | tf_op jit(solution)/shard_map/ppermute | solution.py:402
  10.7 0.0 copy-done
  10.7 1.7 %rest.1 = (f32[6,2048]{1,0:T(8,128)}, f32[7,2,32]{2,1,0:T(2,128)}, f32[3,16,512]{2,1,0:T(8,128)}, f32[16,512]{1,0:T(8,128)}, f32[16,512]{1,0:T(8,128)S(1)}) custom-call(f32[2,424,128]{2,1,0:T(8,128)S(1)} %all_to_all.5.G, s32[72,128]{1,0:T(8,128)S(1)} %get-tuple-element.18.aux, f32[8,128,128]{2,1,0:T(8,128)S(1)} %copy-done, ...), custom_call_target="tpu_custom_call" | custom-call | flops 2000000000 | bytes 2000000 | tf_op jit(solution)/shard_map/rest/pallas_call | solution.py:407
  12.4 0.0 collective-permute-done.1.got_b
  12.4 0.0 collective-permute-done.got_a
  12.4 0.7 %finish.1 = (f32[7,2,64]{2,1,0:T(2,128)}, f32[16,512]{1,0:T(8,128)}) custom-call(f32[16,128]{1,0:T(8,128)S(1)} %collective-permute-done.got_a, f32[16,128]{1,0:T(8,128)S(1)} %collective-permute-done.1.got_b, f32[16,512]{1,0:T(8,128)S(1)} %get-tuple-element.22.image), custom_call_target="tpu_custom_call" | custom-call | tf_op jit(solution)/shard_map/finish/pallas_call | solution.py:433
Async XLA Ops:
  5.8 4.9 %copy-start = (f32[8,128,128]{2,1,0:T(8,128)S(1)}, f32[8,128,128]{2,1,0:T(8,128)}, u32[]{:S(2)}) copy-start(f32[8,128,128]{2,1,0:T(8,128)} %table.1) | copy-start | bytes 1572868
  6.2 6.2 %collective-permute-start.1 = (f32[16,128]{1,0:T(8,128)S(1)}, f32[16,128]{1,0:T(8,128)S(1)}, u32[]{:S(2)}, u32[]{:S(2)}) collective-permute-start(f32[16,128]{1,0:T(8,128)S(1)} %get-tuple-element.21), channel_id=1, source_target_pairs={{0,1},{1,0},{2,4},{3,5},{4,2},{5,3},{6,8},{7,9},{8,6},{9,7},{10,12... | collective-permute-start | bytes 24584 | tf_op jit(solution)/shard_map/ppermute | solution.py:402
  6.4 6.0 %collective-permute-start = (f32[16,128]{1,0:T(8,128)S(1)}, f32[16,128]{1,0:T(8,128)S(1)}, u32[]{:S(2)}, u32[]{:S(2)}) collective-permute-start(f32[16,128]{1,0:T(8,128)S(1)} %get-tuple-element.21), channel_id=1, source_target_pairs={{0,2},{1,3},{2,0},{3,1},{4,6},{5,7},{6,4},{7,5},{8,10},{9,11},{10,... | collective-permute-start | bytes 24584 | tf_op jit(solution)/shard_map/ppermute | solution.py:402

commit v15 on v10

--- a/solution.py
+++ b/solution.py
@@ -65,8 +65,8 @@
 def pack_kernel(
     sz, n_rad, motion_hbm, size_hbm, block_hbm, offset_hbm, gas_hbm, pres_hbm, radial_hbm, counts_hbm, cols_hbm,
     kinds_hbm, axial_hbm,
-    out, aux,
-    motion, size, block, offset, gas, pres, radial, counts, cols, kinds, axial, sem,
+    out, aux, cols, kinds,
+    motion, size, block, offset, gas, pres, radial, counts, axial, sem,
 ):
     small = (
         (counts_hbm, counts), (block_hbm, block), (radial_hbm, radial), (axial_hbm, axial), (cols_hbm, cols),
@@ -91,10 +91,6 @@
     for slot in range(2):
         kept = jnp.where(lane < counts[0, 2 + slot], radial[slot : slot + 1, :], -1)
         out[pl.ds(sz.meta + 1 + slot, 1), pl.ds(0, width)] = kept.astype(F32)
-    index = kinds[...] * (n_rad * sz.blocks) + block_row(sz, cols[...])
-    index = jnp.concatenate([index, index], axis=1).astype(F32)
-    index = jnp.concatenate([index, jnp.zeros((BLOCK - index.shape[0], BLOCK), F32)], axis=0)
-    aux[pl.ds(8, sz.blocks), :] = jnp.transpose(index)[: sz.blocks].astype(I32)
     lane = iota((1, axial.shape[1]), 1)
     kept = [jnp.where(lane < counts[0, slot], axial[slot : slot + 1, :], -1) for slot in range(2)]
     aux[pl.ds(0, 1), :] = jnp.concatenate(kept, axis=1)
@@ -132,11 +128,16 @@
     return [state[pl.ds(c * T + first, sz.tiles), :] for c in range(7)]
 
 
-def move_kernel(sz, n_rad, G, aux, state, message, near):
+def move_kernel(sz, n_rad, G, aux, cols, kinds, state, message, columns, near):
     r = lax.axis_index("rad")
     layers, tiles, blocks, groups = sz.layers, sz.tiles, sz.blocks, sz.groups
     slab_blocks = n_rad * blocks
     T = n_rad * tiles
+
+    index = kinds[...] * slab_blocks + block_row(sz, cols[...])
+    index = jnp.concatenate([index, index], axis=1).astype(F32)
+    index = jnp.concatenate([index, jnp.zeros((BLOCK - index.shape[0], BLOCK), F32)], axis=0)
+    columns[...] = jnp.transpose(index)[:blocks].astype(I32)
 
     column = jnp.concatenate([G[d, pl.ds(sz.column, groups), :] for d in range(n_rad)], axis=0).astype(I32)
     lanes = iota((n_rad * groups, BLOCK), 1)
@@ -181,7 +182,7 @@
 
 
 def rest_kernel(
-    sz, n_rad, G, aux, table, state,
+    sz, n_rad, G, columns, table, state,
     motion_hbm, arr_hbm, gas_hbm, liquid_hbm, image,
     deps, spread, coup, motion_out, arr_rad, gas_out, liquid, sem,
 ):
@@ -250,7 +251,7 @@
 
     pres = jnp.concatenate([G[d, pl.ds(sz.pres, blocks), :] for d in range(n_rad)], axis=0)
     index = [
-        jnp.broadcast_to(aux[pl.ds(8, blocks), k : k + 1], (blocks, BLOCK)).astype(jnp.int16) for k in range(4)
+        jnp.broadcast_to(columns[:, k : k + 1], (blocks, BLOCK)).astype(jnp.int16) for k in range(4)
     ]
     one, none = jnp.ones((blocks, BLOCK), BF16), jnp.zeros((blocks, BLOCK), BF16)
     lanes = iota((blocks, BLOCK), 1)
@@ -336,14 +337,16 @@
     size2 = parcel_size.reshape(sz.tiles, BLOCK)
     offset2 = parcel_offset.reshape(sz.tiles, BLOCK)
 
-    packed, aux = pl.pallas_call(
+    packed, aux, cols, kinds = pl.pallas_call(
         functools.partial(pack_kernel, sz, n_rad),
         out_shape=[
             jax.ShapeDtypeStruct((sz.rows, BLOCK), F32),
-            jax.ShapeDtypeStruct((8 + sz.blocks, BLOCK), I32),
+            jax.ShapeDtypeStruct((8, BLOCK), I32),
+            jax.ShapeDtypeStruct((4, sz.blocks), I32),
+            jax.ShapeDtypeStruct((4, sz.blocks), I32),
         ],
         in_specs=[hbm] * 11,
-        out_specs=[vmem] * 2,
+        out_specs=[vmem] * 4,
         scratch_shapes=[
             pltpu.VMEM(parcel_motion.shape, F32),
             pltpu.VMEM(size2.shape, F32),
@@ -353,8 +356,6 @@
             pltpu.VMEM(pressure.shape, F32),
             pltpu.VMEM((2, cap_rad), I32),
             pltpu.SMEM((1, 4), I32),
-            pltpu.VMEM((4, sz.blocks), I32),
-            pltpu.VMEM((4, sz.blocks), I32),
             pltpu.VMEM((2, cap_ax), I32),
             pltpu.SemaphoreType.DMA((13,)),
         ],
@@ -372,19 +373,20 @@
     )
     gathered = lax.all_gather(packed, "rad", axis=0)
 
-    state, message = pl.pallas_call(
+    state, message, columns = pl.pallas_call(
         functools.partial(move_kernel, sz, n_rad),
         out_shape=[
             jax.ShapeDtypeStruct((7 * T, BLOCK), F32),
             jax.ShapeDtypeStruct((16, BLOCK), F32),
-        ],
-        in_specs=[vmem] * 2,
-        out_specs=[vmem] * 2,
+            jax.ShapeDtypeStruct((sz.blocks, BLOCK), I32),
+        ],
+        in_specs=[vmem] * 4,
+        out_specs=[vmem] * 3,
         scratch_shapes=[pltpu.VMEM((3, n_rad * sz.groups, BLOCK), F32)],
         compiler_params=params,
         cost_estimate=pl.CostEstimate(flops=4_000_000_000, bytes_accessed=1_000_000, transcendentals=0),
         name="move",
-    )(gathered, aux)
+    )(gathered, aux, cols, kinds)
 
     def exchange(first):
         to = list(range(n_ax * n_rad))
@@ -424,7 +426,7 @@
         compiler_params=params,
         cost_estimate=pl.CostEstimate(flops=2_000_000_000, bytes_accessed=2_000_000, transcendentals=0),
         name="rest",
-    )(gathered, aux, block_table, state)
+    )(gathered, columns, block_table, state)
 
     arr_ax, pressure_image = pl.pallas_call(
         functools.partial(finish_kernel, sz, n_ax),

time: 11.3 us -> 11.3 us (level)
  no operation moved by 1% of the time
where the time goes in v15:
time: 11.3 us; the launch traced here: 11.2 us
  starting transfers between devices  4.41 us (39%)
  Pallas kernels  3.84 us (34%)
  blocking collectives  2.2 us (19%)
  between operations  0.67 us (6%)
    ppermute x2, starting transfers between devices, exchange(): return lax.ppermute(message, ('ax', 'rad'), list(enumerate(to)))  4.41 us
    all_gather x1, blocking collectives, on_device(): gathered = lax.all_gather(packed, 'rad', axis=0)  2.2 us
    pallas_call x1, Pallas kernels, on_device(): pl.pallas_call(functools.partial(rest_kernel, sz, n_rad), out_shape=[jax....  1.66 us
    pallas_call x1, Pallas kernels, on_device(): pl.pallas_call(functools.partial(pack_kernel, sz, n_rad), out_shape=[jax....  1.1 us
    pallas_call x1, Pallas kernels, on_device(): pl.pallas_call(functools.partial(finish_kernel, sz, n_ax), out_shape=[jax...  0.68 us
    pallas_call x1, Pallas kernels, on_device(): pl.pallas_call(functools.partial(move_kernel, sz, n_rad), out_shape=[jax....  0.39 us
  transfers between devices with their start and end apart: 2, of which 0 were waited for; matrix products, arithmetic and copies ran while one was open for 0% of the time, Pallas kernels for 15%

profile of v15, /device:TPU:0, one launch (start us, length us, event | category | flops | bytes accessed | tf_op | source)
XLA Modules:
  0.0 11.2 jit_solution(10753622561834461452)
XLA Ops:
  0.6 1.1 %pack.1 = (f32[424,128]{1,0:T(8,128)S(1)}, s32[8,128]{1,0:T(8,128)S(1)}, s32[4,64]{1,0:T(4,128)S(1)}, s32[4,64]{1,0:T(4,128)S(1)}) custom-call(f32[6,2048]{1,0:T(8,128)} %motion_hbm.1, f32[16,128]{1,0:T(8,128)} %bitcast.21, s32[1,32]{1,0:T(1,128)} %bitcast.27, s32[16,128]{1,0:T(8,128)} %bitcast.22, f32[3,16,512]{2,1,0:T(8,128)} %gas_hbm.1, ...), custom_call_target="tpu_custom_call" | custom-call | tf_op jit(solution)/shard_map/pack/pallas_call | solution.py:340
  1.7 2.2 %all-gather = f32[848,128]{1,0:T(8,128)S(1)} all-gather(f32[424,128]{1,0:T(8,128)S(1)} %get-tuple-element.20), channel_id=2, replica_groups=mesh['ax'=16,'rad'=2] {'rad'}, dimensions={0}, use_global_device_ids=true | all-gather | bytes 651264 | tf_op jit(solution)/shard_map/all_gather | solution.py:374
  3.9 0.0 copy-start
  3.9 0.4 %move.1 = (f32[224,128]{1,0:T(8,128)S(1)}, f32[16,128]{1,0:T(8,128)S(1)}, s32[64,128]{1,0:T(8,128)S(1)}) custom-call(f32[2,424,128]{2,1,0:T(8,128)S(1)} %bitcast.19, s32[8,128]{1,0:T(8,128)S(1)} %get-tuple-element.21.aux, s32[4,64]{1,0:T(4,128)S(1)} %get-tuple-element.22.cols, s32[4,64]{1,0:T(4,128)S(1)} %get-tuple-element.23.kinds), custom_call_target="tpu_custom_call" | custom-call | flops 4000000000 | bytes 1000000 | tf_op jit(solution)/shard_map/move/pallas_call | solution.py:376
  4.3 0.4 %collective-permute-start.1 = (f32[16,128]{1,0:T(8,128)S(1)}, f32[16,128]{1,0:T(8,128)S(1)}, u32[]{:S(2)}, u32[]{:S(2)}) collective-permute-start(f32[16,128]{1,0:T(8,128)S(1)} %get-tuple-element.27), channel_id=1, source_target_pairs={{0,1},{1,0},{2,4},{3,5},{4,2},{5,3},{6,8},{7,9},{8,6},{9,7},{10,12... | collective-permute-start | bytes 24584 | tf_op jit(solution)/shard_map/ppermute | solution.py:400
  4.8 4.0 %collective-permute-start = (f32[16,128]{1,0:T(8,128)S(1)}, f32[16,128]{1,0:T(8,128)S(1)}, u32[]{:S(2)}, u32[]{:S(2)}) collective-permute-start(f32[16,128]{1,0:T(8,128)S(1)} %get-tuple-element.27), channel_id=1, source_target_pairs={{0,2},{1,3},{2,0},{3,1},{4,6},{5,7},{6,4},{7,5},{8,10},{9,11},{10,... | collective-permute-start | bytes 24584 | tf_op jit(solution)/shard_map/ppermute | solution.py:400
  8.8 0.0 copy-done
  8.8 1.7 %rest.1 = (f32[6,2048]{1,0:T(8,128)}, f32[7,2,32]{2,1,0:T(2,128)}, f32[3,16,512]{2,1,0:T(8,128)}, f32[16,512]{1,0:T(8,128)}, f32[16,512]{1,0:T(8,128)S(1)}) custom-call(f32[2,424,128]{2,1,0:T(8,128)S(1)} %bitcast.20, s32[64,128]{1,0:T(8,128)S(1)} %get-tuple-element.24.columns, f32[8,128,128]{2,1,0:T(8,128)S(1)} %copy-done, ...), custom_call_target="tpu_custom_call" | custom-call | flops 2000000000 | bytes 2000000 | tf_op jit(solution)/shard_map/rest/pallas_call | solution.py:405
  10.4 0.0 collective-permute-done.1.got_b
  10.4 0.0 collective-permute-done.got_a
  10.5 0.7 %finish.1 = (f32[7,2,64]{2,1,0:T(2,128)}, f32[16,512]{1,0:T(8,128)}) custom-call(f32[16,128]{1,0:T(8,128)S(1)} %collective-permute-done.got_a, f32[16,128]{1,0:T(8,128)S(1)} %collective-permute-done.1.got_b, f32[16,512]{1,0:T(8,128)S(1)} %get-tuple-element.28.image), custom_call_target="tpu_custom_call" | custom-call | tf_op jit(solution)/shard_map/finish/pallas_call | solution.py:431
Async XLA Ops:
  3.9 4.8 %copy-start = (f32[8,128,128]{2,1,0:T(8,128)S(1)}, f32[8,128,128]{2,1,0:T(8,128)}, u32[]{:S(2)}) copy-start(f32[8,128,128]{2,1,0:T(8,128)} %table.1) | copy-start | bytes 1572868
  4.3 6.1 %collective-permute-start.1 = (f32[16,128]{1,0:T(8,128)S(1)}, f32[16,128]{1,0:T(8,128)S(1)}, u32[]{:S(2)}, u32[]{:S(2)}) collective-permute-start(f32[16,128]{1,0:T(8,128)S(1)} %get-tuple-element.27), channel_id=1, source_target_pairs={{0,1},{1,0},{2,4},{3,5},{4,2},{5,3},{6,8},{7,9},{8,6},{9,7},{10,12... | collective-permute-start | bytes 24584 | tf_op jit(solution)/shard_map/ppermute | solution.py:400
  4.8 5.7 %collective-permute-start = (f32[16,128]{1,0:T(8,128)S(1)}, f32[16,128]{1,0:T(8,128)S(1)}, u32[]{:S(2)}, u32[]{:S(2)}) collective-permute-start(f32[16,128]{1,0:T(8,128)S(1)} %get-tuple-element.27), channel_id=1, source_target_pairs={{0,2},{1,3},{2,0},{3,1},{4,6},{5,7},{6,4},{7,5},{8,10},{9,11},{10,... | collective-permute-start | bytes 24584 | tf_op jit(solution)/shard_map/ppermute | solution.py:400

commit v16 on v10

--- a/solution.py
+++ b/solution.py
@@ -94,10 +94,10 @@
     index = kinds[...] * (n_rad * sz.blocks) + block_row(sz, cols[...])
     index = jnp.concatenate([index, index], axis=1).astype(F32)
     index = jnp.concatenate([index, jnp.zeros((BLOCK - index.shape[0], BLOCK), F32)], axis=0)
-    aux[pl.ds(8, sz.blocks), :] = jnp.transpose(index)[: sz.blocks].astype(I32)
+    aux[...] = jnp.transpose(index)[: sz.blocks].astype(I32)
     lane = iota((1, axial.shape[1]), 1)
     kept = [jnp.where(lane < counts[0, slot], axial[slot : slot + 1, :], -1) for slot in range(2)]
-    aux[pl.ds(0, 1), :] = jnp.concatenate(kept, axis=1)
+    out[pl.ds(sz.meta + 3, 1), :] = jnp.concatenate(kept, axis=1).astype(F32)
     motion_copy, pres_copy, *gas_copies = copies[len(small) :]
     motion_copy.wait()
     for i in range(sz.tiles):
@@ -132,8 +132,12 @@
     return [state[pl.ds(c * T + first, sz.tiles), :] for c in range(7)]
 
 
-def move_kernel(sz, n_rad, G, aux, state, message, near):
-    r = lax.axis_index("rad")
+def cross(r, n_rad):
+    return r + 1 - 2 * (r % 2) if n_rad % 2 == 0 else r
+
+
+def move_kernel(sz, n_rad, G, state, message, near):
+    sent = cross(lax.axis_index("rad"), n_rad)
     layers, tiles, blocks, groups = sz.layers, sz.tiles, sz.blocks, sz.groups
     slab_blocks = n_rad * blocks
     T = n_rad * tiles
@@ -170,14 +174,14 @@
         state[pl.ds((3 + c) * T, T), :] = new
     state[pl.ds(6 * T, T), :] = size
 
-    payload = pick(sz, state_of(sz, T, state, r), aux[pl.ds(0, 1), :])
+    payload = pick(sz, state_of(sz, T, state, sent), G[sent, pl.ds(sz.meta + 3, 1), :].astype(I32))
     for c in range(7):
         message[c : c + 1, :] = payload[c]
     message[7:8, :] = jnp.zeros((1, BLOCK), F32)
     for q in range(sz.quarters):
         first = sz.pres + q * layers
-        message[8 + q : 9 + q, :] = G[r, pl.ds(first + layers - 1, 1), :]
-        message[12 + q : 13 + q, :] = G[r, pl.ds(first, 1), :]
+        message[8 + q : 9 + q, :] = G[sent, pl.ds(first + layers - 1, 1), :]
+        message[12 + q : 13 + q, :] = G[sent, pl.ds(first, 1), :]
 
 
 def rest_kernel(
@@ -250,7 +254,7 @@
 
     pres = jnp.concatenate([G[d, pl.ds(sz.pres, blocks), :] for d in range(n_rad)], axis=0)
     index = [
-        jnp.broadcast_to(aux[pl.ds(8, blocks), k : k + 1], (blocks, BLOCK)).astype(jnp.int16) for k in range(4)
+        jnp.broadcast_to(aux[:, k : k + 1], (blocks, BLOCK)).astype(jnp.int16) for k in range(4)
     ]
     one, none = jnp.ones((blocks, BLOCK), BF16), jnp.zeros((blocks, BLOCK), BF16)
     lanes = iota((blocks, BLOCK), 1)
@@ -340,7 +344,7 @@
         functools.partial(pack_kernel, sz, n_rad),
         out_shape=[
             jax.ShapeDtypeStruct((sz.rows, BLOCK), F32),
-            jax.ShapeDtypeStruct((8 + sz.blocks, BLOCK), I32),
+            jax.ShapeDtypeStruct((sz.blocks, BLOCK), I32),
         ],
         in_specs=[hbm] * 11,
         out_specs=[vmem] * 2,
@@ -378,19 +382,19 @@
             jax.ShapeDtypeStruct((7 * T, BLOCK), F32),
             jax.ShapeDtypeStruct((16, BLOCK), F32),
         ],
-        in_specs=[vmem] * 2,
+        in_specs=[vmem],
         out_specs=[vmem] * 2,
         scratch_shapes=[pltpu.VMEM((3, n_rad * sz.groups, BLOCK), F32)],
         compiler_params=params,
         cost_estimate=pl.CostEstimate(flops=4_000_000_000, bytes_accessed=1_000_000, transcendentals=0),
         name="move",
-    )(gathered, aux)
+    )(gathered)
 
     def exchange(first):
         to = list(range(n_ax * n_rad))
         for low in range(first, n_ax - 1, 2):
             for r in range(n_rad):
-                i, j = low * n_rad + r, (low + 1) * n_rad + r
+                i, j = low * n_rad + r, (low + 1) * n_rad + cross(r, n_rad)
                 to[i], to[j] = j, i
         alone = [i for i in range(n_ax * n_rad) if to[i] == i]
         for i, j in zip(alone[0::2], alone[1::2]):

time: 11.3 us -> 11 us (0.973)
  starting transfers between devices: 4.42 us -> 4.14 us
    ppermute x2, starting transfers between devices: 4.42 us -> 4.14 us  [exchange(): return lax.ppermute(message, ('ax', 'rad'), list(enumerate(to)))]
where the time goes in v16:
time: 11 us; the launch traced here: 10.9 us
  starting transfers between devices  4.14 us (38%)
  Pallas kernels  3.84 us (35%)
  blocking collectives  2.2 us (20%)
  between operations  0.68 us (6%)
    ppermute x2, starting transfers between devices, exchange(): return lax.ppermute(message, ('ax', 'rad'), list(enumerate(to)))  4.14 us
    all_gather x1, blocking collectives, on_device(): gathered = lax.all_gather(packed, 'rad', axis=0)  2.2 us
    pallas_call x1, Pallas kernels, on_device(): pl.pallas_call(functools.partial(rest_kernel, sz, n_rad), out_shape=[jax....  1.67 us
    pallas_call x1, Pallas kernels, on_device(): pl.pallas_call(functools.partial(pack_kernel, sz, n_rad), out_shape=[jax....  1.12 us
    pallas_call x1, Pallas kernels, on_device(): pl.pallas_call(functools.partial(finish_kernel, sz, n_ax), out_shape=[jax...  0.69 us
    pallas_call x1, Pallas kernels, on_device(): pl.pallas_call(functools.partial(move_kernel, sz, n_rad), out_shape=[jax....  0.36 us
  transfers between devices with their start and end apart: 2, of which 0 were waited for; matrix products, arithmetic and copies ran while one was open for 0% of the time, Pallas kernels for 15%

profile of v16, /device:TPU:0, one launch (start us, length us, event | category | flops | bytes accessed | tf_op | source)
XLA Modules:
  0.0 10.9 jit_solution(2211810041383643978)
XLA Ops:
  0.6 1.1 %pack.1 = (f32[424,128]{1,0:T(8,128)S(1)}, s32[64,128]{1,0:T(8,128)S(1)}) custom-call(f32[6,2048]{1,0:T(8,128)} %motion_hbm.1, f32[16,128]{1,0:T(8,128)} %bitcast.21, s32[1,32]{1,0:T(1,128)} %bitcast.27, s32[16,128]{1,0:T(8,128)} %bitcast.22, f32[3,16,512]{2,1,0:T(8,128)} %gas_hbm.1, f32[16,512]{1,0:T(8,128)} %pres_hbm.1, s32[2,32]{1,0:T(2,128)} %bitcast.25, ...), custom_call_target="tpu_custom_call" | custom-call | tf_op jit(solution)/shard_map/pack/pallas_call | solution.py:343
  1.8 2.2 %all-gather = f32[848,128]{1,0:T(8,128)S(1)} all-gather(f32[424,128]{1,0:T(8,128)S(1)} %get-tuple-element.17), channel_id=2, replica_groups=mesh['ax'=16,'rad'=2] {'rad'}, dimensions={0}, use_global_device_ids=true | all-gather | bytes 651264 | tf_op jit(solution)/shard_map/all_gather | solution.py:377
  4.0 0.0 copy-start
  4.0 0.4 %move.1 = (f32[224,128]{1,0:T(8,128)S(1)}, f32[16,128]{1,0:T(8,128)S(1)}) custom-call(f32[2,424,128]{2,1,0:T(8,128)S(1)} %bitcast.19), custom_call_target="tpu_custom_call" | custom-call | flops 4000000000 | bytes 1000000 | tf_op jit(solution)/shard_map/move/pallas_call | solution.py:379
  4.3 0.4 %collective-permute-start.1 = (f32[16,128]{1,0:T(8,128)S(1)}, f32[16,128]{1,0:T(8,128)S(1)}, u32[]{:S(2)}, u32[]{:S(2)}) collective-permute-start(f32[16,128]{1,0:T(8,128)S(1)} %get-tuple-element.21), channel_id=1, source_target_pairs={{0,1},{1,0},{2,5},{3,4},{4,3},{5,2},{6,9},{7,8},{8,7},{9,6},{10,13... | collective-permute-start | bytes 24584 | tf_op jit(solution)/shard_map/ppermute | solution.py:402
  4.8 3.7 %collective-permute-start = (f32[16,128]{1,0:T(8,128)S(1)}, f32[16,128]{1,0:T(8,128)S(1)}, u32[]{:S(2)}, u32[]{:S(2)}) collective-permute-start(f32[16,128]{1,0:T(8,128)S(1)} %get-tuple-element.21), channel_id=1, source_target_pairs={{0,3},{1,2},{2,1},{3,0},{4,7},{5,6},{6,5},{7,4},{8,11},{9,10},{10,... | collective-permute-start | bytes 24584 | tf_op jit(solution)/shard_map/ppermute | solution.py:402
  8.5 0.0 copy-done
  8.5 1.7 %rest.1 = (f32[6,2048]{1,0:T(8,128)}, f32[7,2,32]{2,1,0:T(2,128)}, f32[3,16,512]{2,1,0:T(8,128)}, f32[16,512]{1,0:T(8,128)}, f32[16,512]{1,0:T(8,128)S(1)}) custom-call(f32[2,424,128]{2,1,0:T(8,128)S(1)} %bitcast.20, s32[64,128]{1,0:T(8,128)S(1)} %get-tuple-element.18.aux, f32[8,128,128]{2,1,0:T(8,128)S(1)} %copy-done, f32[224,128]{1,0:T(8,128)S(1)} %get-tuple-element.19.state), custom_call_target="tpu_custom_call" | custom-call | flops 2000000000 | bytes 2000000 | tf_op jit(solution)/shard_map/rest/pallas_call | solution.py:407
  10.1 0.0 collective-permute-done.1.got_b
  10.1 0.0 collective-permute-done.got_a
  10.2 0.7 %finish.1 = (f32[7,2,64]{2,1,0:T(2,128)}, f32[16,512]{1,0:T(8,128)}) custom-call(f32[16,128]{1,0:T(8,128)S(1)} %collective-permute-done.got_a, f32[16,128]{1,0:T(8,128)S(1)} %collective-permute-done.1.got_b, f32[16,512]{1,0:T(8,128)S(1)} %get-tuple-element.22.image), custom_call_target="tpu_custom_call" | custom-call | tf_op jit(solution)/shard_map/finish/pallas_call | solution.py:433
Async XLA Ops:
  4.0 4.5 %copy-start = (f32[8,128,128]{2,1,0:T(8,128)S(1)}, f32[8,128,128]{2,1,0:T(8,128)}, u32[]{:S(2)}) copy-start(f32[8,128,128]{2,1,0:T(8,128)} %table.1) | copy-start | bytes 1572868
  4.3 5.8 %collective-permute-start.1 = (f32[16,128]{1,0:T(8,128)S(1)}, f32[16,128]{1,0:T(8,128)S(1)}, u32[]{:S(2)}, u32[]{:S(2)}) collective-permute-start(f32[16,128]{1,0:T(8,128)S(1)} %get-tuple-element.21), channel_id=1, source_target_pairs={{0,1},{1,0},{2,5},{3,4},{4,3},{5,2},{6,9},{7,8},{8,7},{9,6},{10,13... | collective-permute-start | bytes 24584 | tf_op jit(solution)/shard_map/ppermute | solution.py:402
  4.8 5.4 %collective-permute-start = (f32[16,128]{1,0:T(8,128)S(1)}, f32[16,128]{1,0:T(8,128)S(1)}, u32[]{:S(2)}, u32[]{:S(2)}) collective-permute-start(f32[16,128]{1,0:T(8,128)S(1)} %get-tuple-element.21), channel_id=1, source_target_pairs={{0,3},{1,2},{2,1},{3,0},{4,7},{5,6},{6,5},{7,4},{8,11},{9,10},{10,... | collective-permute-start | bytes 24584 | tf_op jit(solution)/shard_map/ppermute | solution.py:402

commit v17 on v16

--- a/solution.py
+++ b/solution.py
@@ -136,8 +136,8 @@
     return r + 1 - 2 * (r % 2) if n_rad % 2 == 0 else r
 
 
-def move_kernel(sz, n_rad, G, state, message, near):
-    sent = cross(lax.axis_index("rad"), n_rad)
+def move_kernel(sz, n_rad, G, state, far, near, found_gas):
+    r = lax.axis_index("rad")
     layers, tiles, blocks, groups = sz.layers, sz.tiles, sz.blocks, sz.groups
     slab_blocks = n_rad * blocks
     T = n_rad * tiles
@@ -157,7 +157,7 @@
     high, low = split2(gas_slab)
     found = dot(jnp.concatenate([chooser, chooser], axis=1), jnp.concatenate([high, low], axis=0))
     for c in range(3):
-        near[c] = found[:, c * BLOCK : (c + 1) * BLOCK]
+        found_gas[c] = found[:, c * BLOCK : (c + 1) * BLOCK]
 
     rows = functools.partial(slab_rows, sz, n_rad, G)
     size = rows(sz.size)
@@ -165,8 +165,8 @@
     factor = jnp.exp(-DRAG / (size * size))
     even = iota((T, BLOCK), 1) < GROUP
     for c in range(3):
-        u_even = take_lanes(near[c, pl.ds(0, T, stride=2), :], offset)
-        u_odd = take_lanes(near[c, pl.ds(1, T, stride=2), :], offset)
+        u_even = take_lanes(found_gas[c, pl.ds(0, T, stride=2), :], offset)
+        u_odd = take_lanes(found_gas[c, pl.ds(1, T, stride=2), :], offset)
         u = jnp.where(even, u_even, u_odd)
         v = rows(sz.motion + (3 + c) * tiles)
         new = u + (v - u) * factor
@@ -174,14 +174,15 @@
         state[pl.ds((3 + c) * T, T), :] = new
     state[pl.ds(6 * T, T), :] = size
 
-    payload = pick(sz, state_of(sz, T, state, sent), G[sent, pl.ds(sz.meta + 3, 1), :].astype(I32))
-    for c in range(7):
-        message[c : c + 1, :] = payload[c]
-    message[7:8, :] = jnp.zeros((1, BLOCK), F32)
-    for q in range(sz.quarters):
-        first = sz.pres + q * layers
-        message[8 + q : 9 + q, :] = G[sent, pl.ds(first + layers - 1, 1), :]
-        message[12 + q : 13 + q, :] = G[sent, pl.ds(first, 1), :]
+    for message, sent in ((far, r), (near, cross(r, n_rad))):
+        payload = pick(sz, state_of(sz, T, state, sent), G[sent, pl.ds(sz.meta + 3, 1), :].astype(I32))
+        for c in range(7):
+            message[c : c + 1, :] = payload[c]
+        message[7:8, :] = jnp.zeros((1, BLOCK), F32)
+        for q in range(sz.quarters):
+            first = sz.pres + q * layers
+            message[8 + q : 9 + q, :] = G[sent, pl.ds(first + layers - 1, 1), :]
+            message[12 + q : 13 + q, :] = G[sent, pl.ds(first, 1), :]
 
 
 def rest_kernel(
@@ -299,7 +300,7 @@
         send.wait()
 
 
-def finish_kernel(sz, n_ax, got_a, got_b, image, arr_ax, pressure_image):
+def finish_kernel(sz, n_ax, got_b, got_a, image, arr_ax, pressure_image):
     a = lax.axis_index("ax")
     even = a % 2 == 0
     low = jnp.where(a > 0, jnp.where(even, got_b[...], got_a[...]), 0.0)
@@ -376,33 +377,34 @@
     )
     gathered = lax.all_gather(packed, "rad", axis=0)
 
-    state, message = pl.pallas_call(
+    state, far, near = pl.pallas_call(
         functools.partial(move_kernel, sz, n_rad),
         out_shape=[
             jax.ShapeDtypeStruct((7 * T, BLOCK), F32),
             jax.ShapeDtypeStruct((16, BLOCK), F32),
+            jax.ShapeDtypeStruct((16, BLOCK), F32),
         ],
         in_specs=[vmem],
-        out_specs=[vmem] * 2,
+        out_specs=[vmem] * 3,
         scratch_shapes=[pltpu.VMEM((3, n_rad * sz.groups, BLOCK), F32)],
         compiler_params=params,
         cost_estimate=pl.CostEstimate(flops=4_000_000_000, bytes_accessed=1_000_000, transcendentals=0),
         name="move",
     )(gathered)
 
-    def exchange(first):
+    def exchange(message, first, partner):
         to = list(range(n_ax * n_rad))
         for low in range(first, n_ax - 1, 2):
             for r in range(n_rad):
-                i, j = low * n_rad + r, (low + 1) * n_rad + cross(r, n_rad)
+                i, j = low * n_rad + r, (low + 1) * n_rad + partner(r)
                 to[i], to[j] = j, i
         alone = [i for i in range(n_ax * n_rad) if to[i] == i]
         for i, j in zip(alone[0::2], alone[1::2]):
             to[i], to[j] = j, i
         return lax.ppermute(message, ("ax", "rad"), list(enumerate(to)))
 
-    got_b = exchange(1)
-    got_a = exchange(0)
+    got_b = exchange(far, 1, lambda r: r)
+    got_a = exchange(near, 0, lambda r: cross(r, n_rad))
 
     motion_out, arr_rad, gas_out, liquid, image = pl.pallas_call(
         functools.partial(rest_kernel, sz, n_rad),
@@ -440,7 +442,7 @@
         out_specs=[vmem] * 2,
         compiler_params=params,
         name="finish",
-    )(got_a, got_b, image)
+    )(got_b, got_a, image)
 
     arrivals_axial = arr_ax.transpose(1, 0, 2)[None, None]
     arrivals_radial = arr_rad.transpose(1, 0, 2)[None, None]

time: 11 us -> 11 us (level)
  the two profiles are of different devices: /device:TPU:0 before, /device:TPU:1 now
where the time goes in v17:
time: 11 us; the launch traced here: 10.8 us
  starting transfers between devices  4.16 us (38%)
  Pallas kernels  3.85 us (35%)
  blocking collectives  2.12 us (19%)
  between operations  0.68 us (6%)
    ppermute x2, starting transfers between devices, exchange(): return lax.ppermute(message, ('ax', 'rad'), list(enumerate(to)))  4.16 us
    all_gather x1, blocking collectives, on_device(): gathered = lax.all_gather(packed, 'rad', axis=0)  2.12 us
    pallas_call x1, Pallas kernels, on_device(): pl.pallas_call(functools.partial(rest_kernel, sz, n_rad), out_shape=[jax....  1.66 us
    pallas_call x1, Pallas kernels, on_device(): pl.pallas_call(functools.partial(pack_kernel, sz, n_rad), out_shape=[jax....  1.12 us
    pallas_call x1, Pallas kernels, on_device(): pl.pallas_call(functools.partial(finish_kernel, sz, n_ax), out_shape=[jax...  0.69 us
    pallas_call x1, Pallas kernels, on_device(): pl.pallas_call(functools.partial(move_kernel, sz, n_rad), out_shape=[jax....  0.37 us
  transfers between devices with their start and end apart: 2, of which 0 were waited for; matrix products, arithmetic and copies ran while one was open for 0% of the time, Pallas kernels for 15%

profile of v17, /device:TPU:1, one launch (start us, length us, event | category | flops | bytes accessed | tf_op | source)
XLA Modules:
  0.0 10.8 jit_solution(15120575608411033619)
XLA Ops:
  0.6 1.1 %pack.1 = (f32[424,128]{1,0:T(8,128)S(1)}, s32[64,128]{1,0:T(8,128)S(1)}) custom-call(f32[6,2048]{1,0:T(8,128)} %motion_hbm.1, f32[16,128]{1,0:T(8,128)} %bitcast.21, s32[1,32]{1,0:T(1,128)} %bitcast.27, s32[16,128]{1,0:T(8,128)} %bitcast.22, f32[3,16,512]{2,1,0:T(8,128)} %gas_hbm.1, f32[16,512]{1,0:T(8,128)} %pres_hbm.1, s32[2,32]{1,0:T(2,128)} %bitcast.25, ...), custom_call_target="tpu_custom_call" | custom-call | tf_op jit(solution)/shard_map/pack/pallas_call | solution.py:344
  1.8 2.1 %all-gather = f32[848,128]{1,0:T(8,128)S(1)} all-gather(f32[424,128]{1,0:T(8,128)S(1)} %get-tuple-element.18), channel_id=2, replica_groups=mesh['ax'=16,'rad'=2] {'rad'}, dimensions={0}, use_global_device_ids=true | all-gather | bytes 651264 | tf_op jit(solution)/shard_map/all_gather | solution.py:378
  3.9 0.0 copy-start
  3.9 0.4 %move.1 = (f32[224,128]{1,0:T(8,128)S(1)}, f32[16,128]{1,0:T(8,128)S(1)}, f32[16,128]{1,0:T(8,128)S(1)}) custom-call(f32[2,424,128]{2,1,0:T(8,128)S(1)} %bitcast.19), custom_call_target="tpu_custom_call" | custom-call | flops 4000000000 | bytes 1000000 | tf_op jit(solution)/shard_map/move/pallas_call | solution.py:380
  4.3 0.2 %collective-permute-start = (f32[16,128]{1,0:T(8,128)S(1)}, f32[16,128]{1,0:T(8,128)S(1)}, u32[]{:S(2)}, u32[]{:S(2)}) collective-permute-start(f32[16,128]{1,0:T(8,128)S(1)} %get-tuple-element.22), channel_id=1, source_target_pairs={{0,1},{1,0},{2,4},{3,5},{4,2},{5,3},{6,8},{7,9},{8,6},{9,7},{10,12... | collective-permute-start | bytes 24584 | tf_op jit(solution)/shard_map/ppermute | solution.py:404
  4.5 4.0 %collective-permute-start.1 = (f32[16,128]{1,0:T(8,128)S(1)}, f32[16,128]{1,0:T(8,128)S(1)}, u32[]{:S(2)}, u32[]{:S(2)}) collective-permute-start(f32[16,128]{1,0:T(8,128)S(1)} %get-tuple-element.23), channel_id=1, source_target_pairs={{0,3},{1,2},{2,1},{3,0},{4,7},{5,6},{6,5},{7,4},{8,11},{9,10},{10,... | collective-permute-start | bytes 24584 | tf_op jit(solution)/shard_map/ppermute | solution.py:404
  8.4 0.0 copy-done
  8.4 1.7 %rest.1 = (f32[6,2048]{1,0:T(8,128)}, f32[7,2,32]{2,1,0:T(2,128)}, f32[3,16,512]{2,1,0:T(8,128)}, f32[16,512]{1,0:T(8,128)}, f32[16,512]{1,0:T(8,128)S(1)}) custom-call(f32[2,424,128]{2,1,0:T(8,128)S(1)} %bitcast.20, s32[64,128]{1,0:T(8,128)S(1)} %get-tuple-element.19.aux, f32[8,128,128]{2,1,0:T(8,128)S(1)} %copy-done, f32[224,128]{1,0:T(8,128)S(1)} %get-tuple-element.20.state), custom_call_target="tpu_custom_call" | custom-call | flops 2000000000 | bytes 2000000 | tf_op jit(solution)/shard_map/rest/pallas_call | solution.py:409
  10.1 0.0 collective-permute-done.got_b
  10.1 0.0 collective-permute-done.1.got_a
  10.1 0.7 %finish.1 = (f32[7,2,64]{2,1,0:T(2,128)}, f32[16,512]{1,0:T(8,128)}) custom-call(f32[16,128]{1,0:T(8,128)S(1)} %collective-permute-done.got_b, f32[16,128]{1,0:T(8,128)S(1)} %collective-permute-done.1.got_a, f32[16,512]{1,0:T(8,128)S(1)} %get-tuple-element.24.image), custom_call_target="tpu_custom_call" | custom-call | tf_op jit(solution)/shard_map/finish/pallas_call | solution.py:435
Async XLA Ops:
  3.9 4.5 %copy-start = (f32[8,128,128]{2,1,0:T(8,128)S(1)}, f32[8,128,128]{2,1,0:T(8,128)}, u32[]{:S(2)}) copy-start(f32[8,128,128]{2,1,0:T(8,128)} %table.1) | copy-start | bytes 1572868
  4.3 5.8 %collective-permute-start = (f32[16,128]{1,0:T(8,128)S(1)}, f32[16,128]{1,0:T(8,128)S(1)}, u32[]{:S(2)}, u32[]{:S(2)}) collective-permute-start(f32[16,128]{1,0:T(8,128)S(1)} %get-tuple-element.22), channel_id=1, source_target_pairs={{0,1},{1,0},{2,4},{3,5},{4,2},{5,3},{6,8},{7,9},{8,6},{9,7},{10,12... | collective-permute-start | bytes 24584 | tf_op jit(solution)/shard_map/ppermute | solution.py:404
  4.5 5.6 %collective-permute-start.1 = (f32[16,128]{1,0:T(8,128)S(1)}, f32[16,128]{1,0:T(8,128)S(1)}, u32[]{:S(2)}, u32[]{:S(2)}) collective-permute-start(f32[16,128]{1,0:T(8,128)S(1)} %get-tuple-element.23), channel_id=1, source_target_pairs={{0,3},{1,2},{2,1},{3,0},{4,7},{5,6},{6,5},{7,4},{8,11},{9,10},{10,... | collective-permute-start | bytes 24584 | tf_op jit(solution)/shard_map/ppermute | solution.py:404

commit v18 on v17

--- a/solution.py
+++ b/solution.py
@@ -174,7 +174,7 @@
         state[pl.ds((3 + c) * T, T), :] = new
     state[pl.ds(6 * T, T), :] = size
 
-    for message, sent in ((far, r), (near, cross(r, n_rad))):
+    for message, sent in ((far, cross(r, n_rad)), (near, r)):
         payload = pick(sz, state_of(sz, T, state, sent), G[sent, pl.ds(sz.meta + 3, 1), :].astype(I32))
         for c in range(7):
             message[c : c + 1, :] = payload[c]
@@ -403,8 +403,8 @@
             to[i], to[j] = j, i
         return lax.ppermute(message, ("ax", "rad"), list(enumerate(to)))
 
-    got_b = exchange(far, 1, lambda r: r)
-    got_a = exchange(near, 0, lambda r: cross(r, n_rad))
+    got_b = exchange(far, 1, lambda r: cross(r, n_rad))
+    got_a = exchange(near, 0, lambda r: r)
 
     motion_out, arr_rad, gas_out, liquid, image = pl.pallas_call(
         functools.partial(rest_kernel, sz, n_rad),

time: 11 us -> 11.1 us (level)
  the two profiles are of different devices: /device:TPU:1 before, /device:TPU:0 now
where the time goes in v18:
time: 11.1 us; the launch traced here: 10.9 us
  starting transfers between devices  4.17 us (38%)
  Pallas kernels  3.85 us (35%)
  blocking collectives  2.2 us (20%)
  between operations  0.67 us (6%)
    ppermute x2, starting transfers between devices, exchange(): return lax.ppermute(message, ('ax', 'rad'), list(enumerate(to)))  4.17 us
    all_gather x1, blocking collectives, on_device(): gathered = lax.all_gather(packed, 'rad', axis=0)  2.2 us
    pallas_call x1, Pallas kernels, on_device(): pl.pallas_call(functools.partial(rest_kernel, sz, n_rad), out_shape=[jax....  1.67 us
    pallas_call x1, Pallas kernels, on_device(): pl.pallas_call(functools.partial(pack_kernel, sz, n_rad), out_shape=[jax....  1.12 us
    pallas_call x1, Pallas kernels, on_device(): pl.pallas_call(functools.partial(finish_kernel, sz, n_ax), out_shape=[jax...  0.69 us
    pallas_call x1, Pallas kernels, on_device(): pl.pallas_call(functools.partial(move_kernel, sz, n_rad), out_shape=[jax....  0.37 us
  transfers between devices with their start and end apart: 2, of which 0 were waited for; matrix products, arithmetic and copies ran while one was open for 0% of the time, Pallas kernels for 15%

profile of v18, /device:TPU:0, one launch (start us, length us, event | category | flops | bytes accessed | tf_op | source)
XLA Modules:
  0.0 10.9 jit_solution(17065664932483247083)
XLA Ops:
  0.6 1.1 %pack.1 = (f32[424,128]{1,0:T(8,128)S(1)}, s32[64,128]{1,0:T(8,128)S(1)}) custom-call(f32[6,2048]{1,0:T(8,128)} %motion_hbm.1, f32[16,128]{1,0:T(8,128)} %bitcast.21, s32[1,32]{1,0:T(1,128)} %bitcast.27, s32[16,128]{1,0:T(8,128)} %bitcast.22, f32[3,16,512]{2,1,0:T(8,128)} %gas_hbm.1, f32[16,512]{1,0:T(8,128)} %pres_hbm.1, s32[2,32]{1,0:T(2,128)} %bitcast.25, ...), custom_call_target="tpu_custom_call" | custom-call | tf_op jit(solution)/shard_map/pack/pallas_call | solution.py:344
  1.8 2.2 %all-gather = f32[848,128]{1,0:T(8,128)S(1)} all-gather(f32[424,128]{1,0:T(8,128)S(1)} %get-tuple-element.18), channel_id=2, replica_groups=mesh['ax'=16,'rad'=2] {'rad'}, dimensions={0}, use_global_device_ids=true | all-gather | bytes 651264 | tf_op jit(solution)/shard_map/all_gather | solution.py:378
  4.0 0.0 copy-start
  4.0 0.4 %move.1 = (f32[224,128]{1,0:T(8,128)S(1)}, f32[16,128]{1,0:T(8,128)S(1)}, f32[16,128]{1,0:T(8,128)S(1)}) custom-call(f32[2,424,128]{2,1,0:T(8,128)S(1)} %bitcast.19), custom_call_target="tpu_custom_call" | custom-call | flops 4000000000 | bytes 1000000 | tf_op jit(solution)/shard_map/move/pallas_call | solution.py:380
  4.3 0.4 %collective-permute-start = (f32[16,128]{1,0:T(8,128)S(1)}, f32[16,128]{1,0:T(8,128)S(1)}, u32[]{:S(2)}, u32[]{:S(2)}) collective-permute-start(f32[16,128]{1,0:T(8,128)S(1)} %get-tuple-element.22), channel_id=1, source_target_pairs={{0,1},{1,0},{2,5},{3,4},{4,3},{5,2},{6,9},{7,8},{8,7},{9,6},{10,13... | collective-permute-start | bytes 24584 | tf_op jit(solution)/shard_map/ppermute | solution.py:404
  4.8 3.7 %collective-permute-start.1 = (f32[16,128]{1,0:T(8,128)S(1)}, f32[16,128]{1,0:T(8,128)S(1)}, u32[]{:S(2)}, u32[]{:S(2)}) collective-permute-start(f32[16,128]{1,0:T(8,128)S(1)} %get-tuple-element.23), channel_id=1, source_target_pairs={{0,2},{1,3},{2,0},{3,1},{4,6},{5,7},{6,4},{7,5},{8,10},{9,11},{10,... | collective-permute-start | bytes 24584 | tf_op jit(solution)/shard_map/ppermute | solution.py:404
  8.5 0.0 copy-done
  8.5 1.7 %rest.1 = (f32[6,2048]{1,0:T(8,128)}, f32[7,2,32]{2,1,0:T(2,128)}, f32[3,16,512]{2,1,0:T(8,128)}, f32[16,512]{1,0:T(8,128)}, f32[16,512]{1,0:T(8,128)S(1)}) custom-call(f32[2,424,128]{2,1,0:T(8,128)S(1)} %bitcast.20, s32[64,128]{1,0:T(8,128)S(1)} %get-tuple-element.19.aux, f32[8,128,128]{2,1,0:T(8,128)S(1)} %copy-done, f32[224,128]{1,0:T(8,128)S(1)} %get-tuple-element.20.state), custom_call_target="tpu_custom_call" | custom-call | flops 2000000000 | bytes 2000000 | tf_op jit(solution)/shard_map/rest/pallas_call | solution.py:409
  10.2 0.0 collective-permute-done.got_b
  10.2 0.0 collective-permute-done.1.got_a
  10.2 0.7 %finish.1 = (f32[7,2,64]{2,1,0:T(2,128)}, f32[16,512]{1,0:T(8,128)}) custom-call(f32[16,128]{1,0:T(8,128)S(1)} %collective-permute-done.got_b, f32[16,128]{1,0:T(8,128)S(1)} %collective-permute-done.1.got_a, f32[16,512]{1,0:T(8,128)S(1)} %get-tuple-element.24.image), custom_call_target="tpu_custom_call" | custom-call | tf_op jit(solution)/shard_map/finish/pallas_call | solution.py:435
Async XLA Ops:
  4.0 4.6 %copy-start = (f32[8,128,128]{2,1,0:T(8,128)S(1)}, f32[8,128,128]{2,1,0:T(8,128)}, u32[]{:S(2)}) copy-start(f32[8,128,128]{2,1,0:T(8,128)} %table.1) | copy-start | bytes 1572868
  4.3 5.9 %collective-permute-start = (f32[16,128]{1,0:T(8,128)S(1)}, f32[16,128]{1,0:T(8,128)S(1)}, u32[]{:S(2)}, u32[]{:S(2)}) collective-permute-start(f32[16,128]{1,0:T(8,128)S(1)} %get-tuple-element.22), channel_id=1, source_target_pairs={{0,1},{1,0},{2,5},{3,4},{4,3},{5,2},{6,9},{7,8},{8,7},{9,6},{10,13... | collective-permute-start | bytes 24584 | tf_op jit(solution)/shard_map/ppermute | solution.py:404
  4.8 5.4 %collective-permute-start.1 = (f32[16,128]{1,0:T(8,128)S(1)}, f32[16,128]{1,0:T(8,128)S(1)}, u32[]{:S(2)}, u32[]{:S(2)}) collective-permute-start(f32[16,128]{1,0:T(8,128)S(1)} %get-tuple-element.23), channel_id=1, source_target_pairs={{0,2},{1,3},{2,0},{3,1},{4,6},{5,7},{6,4},{7,5},{8,10},{9,11},{10,... | collective-permute-start | bytes 24584 | tf_op jit(solution)/shard_map/ppermute | solution.py:404

commit v19 on v16

--- a/solution.py
+++ b/solution.py
@@ -249,7 +249,17 @@
                 gas_out[c, :, at] = G[r, pl.ds(sz.gas + c * blocks + q * layers, layers), :] + part
             else:
                 liquid[:, at] = part
-    for send in sends[2:]:
+    mine = pl.multiple_of(r * tiles, tiles)
+    for i in range(tiles):
+        motion_out[:, i * BLOCK : (i + 1) * BLOCK] = state[pl.ds(mine + i, 6, stride=T), :]
+    width = arr_rad.shape[2]
+    for slot, exists, other in ((0, r > 0, jnp.maximum(r - 1, 0)), (1, r < n_rad - 1, jnp.minimum(r + 1, n_rad - 1))):
+        idx = G[other, pl.ds(sz.meta + 1 + slot, 1), :].astype(I32)
+        idx = jnp.where(exists, idx, -1)
+        got = pick(sz, state_of(sz, T, state, other), idx)
+        for c in range(7):
+            arr_rad[c, slot : slot + 1, :] = got[c][:, :width]
+    for send in sends:
         send.start()
 
     pres = jnp.concatenate([G[d, pl.ds(sz.pres, blocks), :] for d in range(n_rad)], axis=0)
@@ -270,18 +280,6 @@
         counts.append(jnp.concatenate(row, axis=1))
     grouped = dot(jnp.concatenate(counts, axis=0), jnp.concatenate(split2(pres), axis=1))
     grouped = grouped[:, :BLOCK] + grouped[:, BLOCK:]
-    mine = pl.multiple_of(r * tiles, tiles)
-    for i in range(tiles):
-        motion_out[:, i * BLOCK : (i + 1) * BLOCK] = state[pl.ds(mine + i, 6, stride=T), :]
-    sends[0].start()
-    width = arr_rad.shape[2]
-    for slot, exists, other in ((0, r > 0, jnp.maximum(r - 1, 0)), (1, r < n_rad - 1, jnp.minimum(r + 1, n_rad - 1))):
-        idx = G[other, pl.ds(sz.meta + 1 + slot, 1), :].astype(I32)
-        idx = jnp.where(exists, idx, -1)
-        got = pick(sz, state_of(sz, T, state, other), idx)
-        for c in range(7):
-            arr_rad[c, slot : slot + 1, :] = got[c][:, :width]
-    sends[1].start()
 
     grouped = jnp.concatenate([grouped[t * blocks : (t + 1) * blocks] for t in range(NT)], axis=1)
     matrices = jnp.concatenate([table[t] for t in range(NT)], axis=1)

time: 11 us -> 11.1 us (level)
  transfers between devices with their start and end apart: 2 -> 2, of which waited for: 0 -> 0; matrix products, arithmetic and copies ran while one was open for 0% -> 0% of each run, Pallas kernels for 15% -> 16%
where the time goes in v19:
time: 11.1 us; the launch traced here: 10.9 us
  starting transfers between devices  4.14 us (37%)
  Pallas kernels  3.87 us (35%)
  blocking collectives  2.2 us (20%)
  between operations  0.68 us (6%)
    ppermute x2, starting transfers between devices, exchange(): return lax.ppermute(message, ('ax', 'rad'), list(enumerate(to)))  4.14 us
    all_gather x1, blocking collectives, on_device(): gathered = lax.all_gather(packed, 'rad', axis=0)  2.2 us
    pallas_call x1, Pallas kernels, on_device(): pl.pallas_call(functools.partial(rest_kernel, sz, n_rad), out_shape=[jax....  1.71 us
    pallas_call x1, Pallas kernels, on_device(): pl.pallas_call(functools.partial(pack_kernel, sz, n_rad), out_shape=[jax....  1.12 us
    pallas_call x1, Pallas kernels, on_device(): pl.pallas_call(functools.partial(finish_kernel, sz, n_ax), out_shape=[jax...  0.69 us
    pallas_call x1, Pallas kernels, on_device(): pl.pallas_call(functools.partial(move_kernel, sz, n_rad), out_shape=[jax....  0.36 us
  transfers between devices with their start and end apart: 2, of which 0 were waited for; matrix products, arithmetic and copies ran while one was open for 0% of the time, Pallas kernels for 16%

profile of v19, /device:TPU:0, one launch (start us, length us, event | category | flops | bytes accessed | tf_op | source)
XLA Modules:
  0.0 10.9 jit_solution(11708456902215324385)
XLA Ops:
  0.6 1.1 %pack.1 = (f32[424,128]{1,0:T(8,128)S(1)}, s32[64,128]{1,0:T(8,128)S(1)}) custom-call(f32[6,2048]{1,0:T(8,128)} %motion_hbm.1, f32[16,128]{1,0:T(8,128)} %bitcast.21, s32[1,32]{1,0:T(1,128)} %bitcast.27, s32[16,128]{1,0:T(8,128)} %bitcast.22, f32[3,16,512]{2,1,0:T(8,128)} %gas_hbm.1, f32[16,512]{1,0:T(8,128)} %pres_hbm.1, s32[2,32]{1,0:T(2,128)} %bitcast.25, ...), custom_call_target="tpu_custom_call" | custom-call | tf_op jit(solution)/shard_map/pack/pallas_call | solution.py:341
  1.8 2.2 %all-gather = f32[848,128]{1,0:T(8,128)S(1)} all-gather(f32[424,128]{1,0:T(8,128)S(1)} %get-tuple-element.17), channel_id=2, replica_groups=mesh['ax'=16,'rad'=2] {'rad'}, dimensions={0}, use_global_device_ids=true | all-gather | bytes 651264 | tf_op jit(solution)/shard_map/all_gather | solution.py:375
  4.0 0.0 copy-start
  4.0 0.4 %move.1 = (f32[224,128]{1,0:T(8,128)S(1)}, f32[16,128]{1,0:T(8,128)S(1)}) custom-call(f32[2,424,128]{2,1,0:T(8,128)S(1)} %bitcast.19), custom_call_target="tpu_custom_call" | custom-call | flops 4000000000 | bytes 1000000 | tf_op jit(solution)/shard_map/move/pallas_call | solution.py:377
  4.3 0.4 %collective-permute-start.1 = (f32[16,128]{1,0:T(8,128)S(1)}, f32[16,128]{1,0:T(8,128)S(1)}, u32[]{:S(2)}, u32[]{:S(2)}) collective-permute-start(f32[16,128]{1,0:T(8,128)S(1)} %get-tuple-element.21), channel_id=1, source_target_pairs={{0,1},{1,0},{2,5},{3,4},{4,3},{5,2},{6,9},{7,8},{8,7},{9,6},{10,13... | collective-permute-start | bytes 24584 | tf_op jit(solution)/shard_map/ppermute | solution.py:400
  4.8 3.7 %collective-permute-start = (f32[16,128]{1,0:T(8,128)S(1)}, f32[16,128]{1,0:T(8,128)S(1)}, u32[]{:S(2)}, u32[]{:S(2)}) collective-permute-start(f32[16,128]{1,0:T(8,128)S(1)} %get-tuple-element.21), channel_id=1, source_target_pairs={{0,3},{1,2},{2,1},{3,0},{4,7},{5,6},{6,5},{7,4},{8,11},{9,10},{10,... | collective-permute-start | bytes 24584 | tf_op jit(solution)/shard_map/ppermute | solution.py:400
  8.5 0.0 copy-done
  8.5 1.7 %rest.1 = (f32[6,2048]{1,0:T(8,128)}, f32[7,2,32]{2,1,0:T(2,128)}, f32[3,16,512]{2,1,0:T(8,128)}, f32[16,512]{1,0:T(8,128)}, f32[16,512]{1,0:T(8,128)S(1)}) custom-call(f32[2,424,128]{2,1,0:T(8,128)S(1)} %bitcast.20, s32[64,128]{1,0:T(8,128)S(1)} %get-tuple-element.18.aux, f32[8,128,128]{2,1,0:T(8,128)S(1)} %copy-done, f32[224,128]{1,0:T(8,128)S(1)} %get-tuple-element.19.state), custom_call_target="tpu_custom_call" | custom-call | flops 2000000000 | bytes 2000000 | tf_op jit(solution)/shard_map/rest/pallas_call | solution.py:405
  10.2 0.0 collective-permute-done.1.got_b
  10.2 0.0 collective-permute-done.got_a
  10.2 0.7 %finish.1 = (f32[7,2,64]{2,1,0:T(2,128)}, f32[16,512]{1,0:T(8,128)}) custom-call(f32[16,128]{1,0:T(8,128)S(1)} %collective-permute-done.got_a, f32[16,128]{1,0:T(8,128)S(1)} %collective-permute-done.1.got_b, f32[16,512]{1,0:T(8,128)S(1)} %get-tuple-element.22.image), custom_call_target="tpu_custom_call" | custom-call | tf_op jit(solution)/shard_map/finish/pallas_call | solution.py:431
Async XLA Ops:
  4.0 4.5 %copy-start = (f32[8,128,128]{2,1,0:T(8,128)S(1)}, f32[8,128,128]{2,1,0:T(8,128)}, u32[]{:S(2)}) copy-start(f32[8,128,128]{2,1,0:T(8,128)} %table.1) | copy-start | bytes 1572868
  4.3 5.9 %collective-permute-start.1 = (f32[16,128]{1,0:T(8,128)S(1)}, f32[16,128]{1,0:T(8,128)S(1)}, u32[]{:S(2)}, u32[]{:S(2)}) collective-permute-start(f32[16,128]{1,0:T(8,128)S(1)} %get-tuple-element.21), channel_id=1, source_target_pairs={{0,1},{1,0},{2,5},{3,4},{4,3},{5,2},{6,9},{7,8},{8,7},{9,6},{10,13... | collective-permute-start | bytes 24584 | tf_op jit(solution)/shard_map/ppermute | solution.py:400
  4.8 5.4 %collective-permute-start = (f32[16,128]{1,0:T(8,128)S(1)}, f32[16,128]{1,0:T(8,128)S(1)}, u32[]{:S(2)}, u32[]{:S(2)}) collective-permute-start(f32[16,128]{1,0:T(8,128)S(1)} %get-tuple-element.21), channel_id=1, source_target_pairs={{0,3},{1,2},{2,1},{3,0},{4,7},{5,6},{6,5},{7,4},{8,11},{9,10},{10,... | collective-permute-start | bytes 24584 | tf_op jit(solution)/shard_map/ppermute | solution.py:400
